TPU v7x, 32 devices: a whole 2x2x4 slice. The times are simulated.
32 devices in a mesh: groups: 2 (over y), expert: 4 (over z), dp: 4 (over x, core).
Axes of the slice: x: 2, y: 2, z: 4, core: 2. Of those that a mesh axis runs over, the one named last changes fastest.
Arguments:
- tokens: bfloat16 [4096, 7168], P(('groups', 'expert', 'dp')), parts along dimension 0, may hold values from -6 to 6
- expert_ids: int32 [4096, 8], P(('groups', 'expert', 'dp')), parts along dimension 0, may hold values from 0 to 255, all different within a row; in each aligned block of 128 rows (0 to 127, 128 to 255, ...) at most 8 rows name the same one
Outputs:
- routed_hessian: float32 [8, 384, 7168], P(('groups', 'expert'), None, 'dp'), parts along dimension 0
- shared_hessian: float32 [14336, 128], P(('groups', 'expert', 'dp')), parts along dimension 0
There are 2 independent parts, one for each index of `groups`. A program takes and returns all parts, laid end to end along the dimension named above; each array names one. Nothing has to cross between parts.
Inputs may be any that keep to these rules, and one draw needn't show every extreme that they name: `expert_ids`: each row names 8 different experts; within the rows of one device no expert is named by more than 8 rows; every expert is named by some row.
All inputs are finite; a program needn't handle non-finite values.
Results may differ from a plain program's by a relative error of at most 0.0003.
Values may be sent and summed in bfloat16 or wider, within the bound.
No kernel may reach another device: no remote copies, remote signals or barrier semaphores. Data moves between devices by JAX's collectives and lax.ppermute only.
A program may use at most 128 MiB of HBM per device.

v0:
```python
import jax
import jax.numpy as jnp
from jax import lax
from jax.sharding import PartitionSpec as P

BAND = 384
SBAND = 128
CAP = 8


def spread(value, axis, root):
    mine = lax.axis_index(axis) == root
    return lax.psum(jnp.where(mine, value, jnp.zeros_like(value)), axis)


def on_device(tokens, expert_ids):
    tok_rows = tokens.shape[0]
    feature_count = tokens.shape[1]
    choices_each = expert_ids.shape[1]
    expert_devices = lax.axis_size("expert")
    data_devices = lax.axis_size("dp")
    capacity = CAP
    flat_ids = expert_ids.reshape(-1)
    one_hot = (flat_ids[:, None] == jnp.arange(expert_devices, dtype=jnp.int32)[None, :]).astype(
        jnp.int32
    )
    earlier = jnp.cumsum(one_hot, axis=0) - one_hot
    slot_index = jnp.sum(earlier * one_hot, axis=1)
    inside = flat_ids < expert_devices
    target = jnp.where(inside, flat_ids * capacity + slot_index, expert_devices * capacity)
    source = jnp.arange(flat_ids.shape[0], dtype=jnp.int32) // choices_each
    table = (
        jnp.full((expert_devices * capacity,), tok_rows, jnp.int32)
        .at[target]
        .set(source, mode="drop")
    )
    padded = jnp.concatenate([tokens, jnp.zeros((1, feature_count), tokens.dtype)], axis=0)
    outgoing = padded[table].reshape(expert_devices, capacity, feature_count)
    filled = (table < tok_rows).astype(jnp.bfloat16).reshape(expert_devices, capacity, 1)
    flags = jnp.broadcast_to(filled, (expert_devices, capacity, data_devices))
    arrived, marks = (
        lax.all_to_all(
            lax.all_to_all(outgoing, "expert", split_axis=0, concat_axis=0, tiled=True),
            "dp",
            split_axis=2,
            concat_axis=0,
            tiled=True,
        ),
        lax.all_to_all(
            lax.all_to_all(flags, "expert", split_axis=0, concat_axis=0, tiled=True),
            "dp",
            split_axis=2,
            concat_axis=0,
            tiled=True,
        ),
    )
    column_block = arrived.reshape(-1, arrived.shape[2])
    member_count = jnp.sum(marks.astype(jnp.float32))
    band_cols = spread(column_block[:, :BAND], "dp", 0)
    product = lax.dot_general(
        band_cols, column_block, (((0,), (0,)), ((), ())), preferred_element_type=jnp.float32
    )
    routed_out = (product * (2.0 / member_count))[None]
    all_tokens = tok_rows * expert_devices * data_devices
    leading = tokens[:, :SBAND]
    summed = lax.psum_scatter(
        lax.dot_general(
            tokens, leading, (((0,), (0,)), ((), ())), preferred_element_type=jnp.float32
        ),
        ("expert", "dp"),
        scatter_dimension=0,
        tiled=True,
    )
    shared_out = summed * (2.0 / all_tokens)
    return (routed_out, shared_out)


def solution(mesh):
    in_specs = (P(("groups", "expert", "dp"), None), P(("groups", "expert", "dp"), None))
    out_specs = (P(("groups", "expert"), None, "dp"), P(("groups", "expert", "dp"), None))
    return jax.shard_map(
        on_device, mesh=mesh, in_specs=in_specs, out_specs=out_specs, check_vma=False
    )
```

profile of v0, /device:TPU:0, one launch (start us, length us, event | category | flops | bytes accessed | tf_op | source)
XLA Modules:
  0.0 167.3 jit_solution(15370434553348684264)
XLA Ops:
  8.0 0.8 copy.23
  9.0 0.7 broadcast_multiply_fusion.1
  9.7 0.7 broadcast_compare_fusion
  10.4 1.1 reduce-window.6
  11.5 0.2 slice_reduce_fusion
  12.5 4.3 %scatter_custom_fusion = s32[32]{0:T(128)S(1)} fusion(s32[1024]{0:T(1024)S(1)} %bitcast.41, s32[1024]{0:T(1024)S(1)} %add_select_fusion, s32[]{:T(128)} %constant.14.clone.1), kind=kCustom, calls=%fused_computation.31 | custom fusion | bytes 132 | tf_op jit(solution)/shard_map/scatter | solution.py:35
  16.8 1.7 %concatenate.3 = bf16[129,7168]{1,0:T(8,128)(2,1)S(1)} pad(bf16[128,7168]{1,0:T(8,128)(2,1)} %param.2, bf16[]{:T(256)} %constant.17.clone.1), padding=0_1x0_0 | pad | bytes 3684354 | tf_op jit(solution)/shard_map/concatenate | solution.py:37
  18.5 0.8 gather_fusion
  19.3 19.2 %all_to_all.34 = bf16[4,8,7168]{2,1,0:T(8,128)(2,1)S(1)} all-to-all(bf16[4,8,7168]{2,1,0:T(8,128)(2,1)S(1)} %bitcast.38), channel_id=1, replica_groups=mesh['groups'=2,'expert'=4,'dp'=4] {'expert'}, dimensions={0} | all-to-all | bytes 917504 | tf_op jit(solution)/shard_map/all_to_all | solution.py:43
  38.5 7.2 %copy.25 = bf16[4,8,7168]{1,0,2:T(4,128)(2,1)} copy(bf16[4,8,7168]{2,1,0:T(8,128)(2,1)S(1)} %all_to_all.34) | data formatting | bytes 917504 | tf_op jit(solution)/shard_map/all_to_all | solution.py:43
  45.7 10.1 %reshape.101 = bf16[4,2,28672]{2,1,0:T(2,128)(2,1)} reshape(bf16[7168,4,8]{2,1,0:T(4,128)(2,1)} %bitcast.34) | data formatting | bytes 917504
  55.8 3.5 %all-to-all-start.1 = ((bf16[4,2,28672]{2,1,0:T(2,128)(2,1)}), bf16[4,2,28672]{2,1,0:T(2,128)(2,1)S(1)}, u32[]{:S(2)}, u32[]{:S(2)}) async-start(bf16[4,2,28672]{2,1,0:T(2,128)(2,1)} %reshape.101), calls=%async_computation.1 | async-start | bytes 917504 | tf_op jit(solution)/shard_map/all_to_all | solution.py:42
  59.3 8.1 %all-to-all-done.1 = bf16[4,2,28672]{2,1,0:T(2,128)(2,1)S(1)} async-done(((bf16[4,2,28672]{2,1,0:T(2,128)(2,1)}), bf16[4,2,28672]{2,1,0:T(2,128)(2,1)S(1)}, u32[]{:S(2)}, u32[]{:S(2)}) %all-to-all-start.1) | async-done | bytes 458784 | tf_op jit(solution)/shard_map/all_to_all | solution.py:42
  67.4 9.8 %reshape.102 = bf16[7168,4,8]{2,1,0:T(4,128)(2,1)} reshape(bf16[4,2,28672]{2,1,0:T(2,128)(2,1)S(1)} %all-to-all-done.1) | data formatting | bytes 917504
  77.2 8.8 %copy.27 = bf16[4,4,8,1792]{3,2,1,0:T(8,128)(2,1)S(1)} copy(bf16[4,4,8,1792]{2,1,3,0:T(4,128)(2,1)} %bitcast.35) | data formatting | bytes 917504 | tf_op jit(solution)/shard_map/all_to_all | solution.py:42
  86.1 0.7 slice_select_fusion
  86.8 2.5 %fusion.1 = f32[7168,128]{1,0:T(8,128)} fusion(bf16[128,7168]{1,0:T(8,128)(2,1)S(1)} %copy-done), kind=kOutput, calls=%fused_computation.6 | convolution fusion | flops 234881024 | bytes 5537792 | tf_op jit(solution)/shard_map/dot_general | solution.py:67
  89.4 8.1 %all_to_all.35 = bf16[4,8,4]{1,2,0:T(4,128)(2,1)S(1)} all-to-all(bf16[4,8,4]{1,2,0:T(4,128)(2,1)S(1)} %broadcast_in_dim.31), channel_id=1, replica_groups=mesh['groups'=2,'expert'=4,'dp'=4] {'expert'}, dimensions={0} | all-to-all | bytes 512 | tf_op jit(solution)/shard_map/all_to_all | solution.py:50
  97.5 6.1 %all_to_all.36 = bf16[4,8,4]{1,0,2:T(4,128)(2,1)S(1)} all-to-all(bf16[4,8,4]{1,0,2:T(4,128)(2,1)S(1)} %copy.28), channel_id=1, replica_groups=mesh['groups'=2,'expert'=4,'dp'=4] {'dp'}, dimensions={2} | all-to-all | bytes 512 | tf_op jit(solution)/shard_map/all_to_all | solution.py:49
  103.6 0.6 convert_reduce_fusion
  104.9 11.4 %all-reduce.3.cloned.1.call-done = bf16[128,384]{1,0:T(8,128)(2,1)} async-done(((bf16[128,384]{1,0:T(8,128)(2,1)}), bf16[128,384]{1,0:T(8,128)(2,1)}) %all-reduce.3.cloned.1.call-update) | async-done | bytes 98320 | tf_op jit(solution)/shard_map/psum | solution.py:13
  116.4 3.0 %fusion = f32[1,384,1792]{2,1,0:T(8,128)} fusion(bf16[128,384]{1,0:T(8,128)(2,1)} %all-reduce.3.cloned.1.call-done, bf16[128,1792]{1,0:T(8,128)(2,1)S(1)} %bitcast.37, f32[]{:T(128)S(6)} %div.13), kind=kOutput, calls=%fused_computation.3 | convolution fusion | flops 176848896 | bytes 3309572 | tf_op jit(solution)/shard_map/dot_general | solution.py:60
  119.3 38.8 %reduce-scatter.2.cloned.1.call-done = f32[448,128]{1,0:T(8,128)} async-done(((f32[7168,128]{1,0:T(8,128)}), f32[448,128]{1,0:T(8,128)}) %reduce-scatter.2.cloned.1.call-update) | async-done | bytes 229392 | tf_op jit(solution)/shard_map/reduce_scatter | solution.py:66
  158.2 1.6 broadcast_multiply_fusion
  (24 shorter events, 1.1 us)
Async XLA Ops:
  55.8 11.6 %all-to-all-start.1 = ((bf16[4,2,28672]{2,1,0:T(2,128)(2,1)}), bf16[4,2,28672]{2,1,0:T(2,128)(2,1)S(1)}, u32[]{:S(2)}, u32[]{:S(2)}) async-start(bf16[4,2,28672]{2,1,0:T(2,128)(2,1)} %reshape.101), calls=%async_computation.1 | async-start | bytes 917504 | tf_op jit(solution)/shard_map/all_to_all | solution.py:42
  59.3 57.1 %all-reduce.3.cloned.1.call-start = ((), (), s32[]{:S(2)}) async-start(), calls=%async_computation.5 | async-start | bytes 196608 | tf_op jit(solution)/shard_map/psum | solution.py:13
  77.2 9.6 %copy-start = (bf16[128,7168]{1,0:T(8,128)(2,1)S(1)}, bf16[128,7168]{1,0:T(8,128)(2,1)}, u32[]{:S(2)}) copy-start(bf16[128,7168]{1,0:T(8,128)(2,1)} %param.2) | copy-start | bytes 5505028
  86.7 71.4 %reduce-scatter.2.cloned.1.call-start = ((), (), s32[]{:S(2)}) async-start(), calls=%async_computation.6 | async-start | bytes 3899392 | tf_op jit(solution)/shard_map/reduce_scatter | solution.py:66
Sparse Core Ops, SparseCore 0:
  86.9 29.4 all-reduce.2
Sparse Core Ops, SparseCore 1:
  91.5 66.6 reduce-scatter.1
where the time goes:
time: 168 us; the launch traced here: 167 us
  waiting for transfers between devices  58.4 us (35%)
  local copies, waits for them, and re-layouts  44.5 us (26%)
  blocking collectives  33.4 us (20%)
  between operations  16.3 us (10%)
  other arithmetic  5.75 us (3%)
  matrix products  5.46 us (3%)
  starting transfers between devices  3.55 us (2%)
    reduce_scatter x1, waiting for transfers between devices, on_device(): lax.psum_scatter(lax.dot_general(tokens, leading, (((0,), (0,)), ((), ())...  38.8 us
    unnamed x5, local copies, waits for them, and re-layouts  20.7 us
    all_to_all x1, blocking collectives, on_device(): lax.all_to_all(outgoing, 'expert', split_axis=0, concat_axis=0, tiled=True)  19.2 us
    psum x1, waiting for transfers between devices, spread(): return lax.psum(jnp.where(mine, value, jnp.zeros_like(value)), axis)  11.4 us
    all_to_all x1, local copies, waits for them, and re-layouts, on_device(): lax.all_to_all(lax.all_to_all(outgoing, 'expert', split_axis=0, concat_ax...  8.83 us
    all_to_all x1, blocking collectives, on_device(): lax.all_to_all(flags, 'expert', split_axis=0, concat_axis=0, tiled=True)  8.1 us
    all_to_all x1, waiting for transfers between devices, on_device(): lax.all_to_all(lax.all_to_all(outgoing, 'expert', split_axis=0, concat_ax...  8.05 us
    all_to_all x1, local copies, waits for them, and re-layouts, on_device(): lax.all_to_all(outgoing, 'expert', split_axis=0, concat_axis=0, tiled=True)  7.18 us
  transfers between devices with their start and end apart: 3, of which 3 were waited for; matrix products, arithmetic and copies ran while one was open for 4% of the time, Pallas kernels for 0%

commit v1 on v0

v1 whole, which is shorter than its diff:
```python
import functools

import jax
import jax.numpy as jnp
from jax import lax
from jax.experimental import pallas as pl
from jax.experimental.pallas import tpu as pltpu
from jax.sharding import PartitionSpec as P

BAND = 384
SBAND = 128
CAP = 8
LANES = 128
VMEM_LIMIT = 32 * 1024 * 1024


def exchange(value, axis, distance):
    size = lax.axis_size(axis)
    return lax.ppermute(value, axis, [(i, i ^ distance) for i in range(size)])


def call(kernel, out_shape, *operands, flops, nbytes, grid_spec=None):
    where = {"grid_spec": grid_spec} if grid_spec is not None else {}
    return pl.pallas_call(
        kernel,
        out_shape=out_shape,
        compiler_params=pltpu.CompilerParams(vmem_limit_bytes=VMEM_LIMIT),
        cost_estimate=pl.CostEstimate(flops=flops, bytes_accessed=nbytes, transcendentals=0),
        **where,
    )(*operands)


def select_kernel(ids_ref, tokens_ref, *out_refs):
    me = lax.axis_index("expert")
    experts = len(out_refs)
    rows, features = tokens_ref.shape
    ids = ids_ref[...]
    members = [
        jnp.max((ids == (me ^ k)).astype(jnp.float32), axis=0, keepdims=True)
        for k in range(experts)
    ]
    member = jnp.concatenate(members, axis=0)
    earlier = (
        lax.broadcasted_iota(jnp.int32, (rows, rows), 0)
        < lax.broadcasted_iota(jnp.int32, (rows, rows), 1)
    ).astype(jnp.bfloat16)
    rank = jnp.dot(member.astype(jnp.bfloat16), earlier, preferred_element_type=jnp.float32)
    slot = lax.broadcasted_iota(jnp.int32, (CAP, rows), 0).astype(jnp.float32)
    picks = jnp.concatenate(
        [
            jnp.where(slot == rank[k : k + 1], member[k : k + 1], 0.0)
            for k in range(experts)
        ],
        axis=0,
    )
    flags = jnp.broadcast_to(jnp.sum(picks, axis=1, keepdims=True), (experts * CAP, LANES))
    chosen = jnp.dot(
        picks.astype(jnp.bfloat16), tokens_ref[...], preferred_element_type=jnp.float32
    )
    for k, out_ref in enumerate(out_refs):
        out_ref[:, :features] = chosen[k * CAP : (k + 1) * CAP].astype(jnp.bfloat16)
        out_ref[:, features:] = flags[k * CAP : (k + 1) * CAP].astype(jnp.bfloat16)


def split_kernel(*refs, peers):
    in_refs, out_refs = refs[:-peers], refs[-peers:]
    me = lax.axis_index("dp")
    features = in_refs[0].shape[1] - LANES
    width = features // peers

    def stacked(columns):
        return jnp.concatenate(
            [ref[:, columns].astype(jnp.float32) for ref in in_refs], axis=0
        ).astype(jnp.bfloat16)

    band = stacked(slice(0, BAND))
    flag = stacked(slice(features, features + LANES))
    for k, out_ref in enumerate(out_refs):
        start = pl.multiple_of((me ^ k) * width, LANES)
        out_ref[:, :width] = stacked(pl.ds(start, width))
        out_ref[:, width : width + BAND] = band
        out_ref[:, width + BAND :] = flag


def hessian_kernel(*refs):
    in_refs, out_ref = refs[:-1], refs[-1]
    width = out_ref.shape[2]
    step = out_ref.shape[1]
    begin = pl.multiple_of(pl.program_id(0) * step, LANES)
    rows = jnp.concatenate([ref[:, :width] for ref in in_refs], axis=0)
    band = jnp.concatenate([ref[:, pl.ds(width + begin, step)] for ref in in_refs], axis=0)
    count = sum(
        jnp.sum(ref[:, width + BAND :].astype(jnp.float32), axis=0, keepdims=True)[:, :1]
        for ref in in_refs
    )
    product = lax.dot_general(
        band, rows, (((0,), (0,)), ((), ())), preferred_element_type=jnp.float32
    )
    out_ref[0] = product * (2.0 / count)


def pair_kernel(mine_ref, other_ref, out_ref):
    features = mine_ref.shape[1]
    block = 4 * LANES
    lead = jnp.concatenate([mine_ref[:, :SBAND], other_ref[:, :SBAND]], axis=0)
    for begin in range(0, features, block):
        part = slice(begin, min(begin + block, features))
        rows = jnp.concatenate([mine_ref[:, part], other_ref[:, part]], axis=0)
        out_ref[part] = lax.dot_general(
            rows, lead, (((0,), (0,)), ((), ())), preferred_element_type=jnp.float32
        )


def on_device(tokens, expert_ids):
    tok_rows, features = tokens.shape
    experts = lax.axis_size("expert")
    peers = lax.axis_size("dp")
    e = lax.axis_index("expert")
    d = lax.axis_index("dp")
    width = features // peers
    share = features // (experts * peers)

    other = exchange(tokens, "dp", 1)

    outgoing = call(
        select_kernel,
        [jax.ShapeDtypeStruct((CAP, features + LANES), jnp.bfloat16)] * experts,
        expert_ids.T,
        tokens,
        flops=2 * experts * CAP * tok_rows * features,
        nbytes=2 * (tok_rows + experts * CAP) * features,
    )
    arrived = [outgoing[0]] + [exchange(outgoing[k], "expert", k) for k in range(1, experts)]

    pair = call(
        pair_kernel,
        jax.ShapeDtypeStruct((features, SBAND), jnp.float32),
        tokens,
        other,
        flops=4 * tok_rows * features * SBAND,
        nbytes=4 * tok_rows * features + 4 * features * SBAND,
    )

    def block(m, k):
        start = ((e ^ m) * peers + (d ^ k)) * share
        return lax.dynamic_slice_in_dim(pair, start, share, axis=0)

    def over_dp(m):
        far = [exchange(block(m, k), "dp", k) for k in range(2, peers, 2)]
        return sum(far, block(m, 0))

    order = list(range(3, experts, 2)) + list(range(2, experts, 2)) + [1, 0]
    part = {m: over_dp(m) for m in order}
    for m in range(2, experts, 2):
        part[m] = part[m] + exchange(part[m + 1], "expert", 1)
    summed = part[0] + exchange(part[1], "expert", 1)
    for m in range(2, experts, 2):
        summed = summed + exchange(part[m], "expert", m)
    shared_out = summed * (2.0 / (tok_rows * experts * peers))

    wide = width + BAND + LANES
    packed = call(
        functools.partial(split_kernel, peers=peers),
        [jax.ShapeDtypeStruct((experts * CAP, wide), jnp.bfloat16)] * peers,
        *arrived,
        flops=0,
        nbytes=4 * experts * CAP * features,
    )
    gathered = [packed[0]] + [exchange(packed[k], "dp", k) for k in range(1, peers)]
    steps = BAND // LANES
    routed_out = call(
        hessian_kernel,
        jax.ShapeDtypeStruct((1, BAND, width), jnp.float32),
        *gathered,
        flops=2 * BAND * width * experts * peers * CAP,
        nbytes=4 * BAND * width,
        grid_spec=pl.GridSpec(
            grid=(steps,),
            in_specs=[pl.BlockSpec((experts * CAP, wide), lambda i: (0, 0))] * peers,
            out_specs=pl.BlockSpec((1, BAND // steps, width), lambda i: (0, i, 0)),
        ),
    )
    return routed_out, shared_out


def solution(mesh):
    in_specs = (P(("groups", "expert", "dp"), None), P(("groups", "expert", "dp"), None))
    out_specs = (P(("groups", "expert"), None, "dp"), P(("groups", "expert", "dp"), None))
    return jax.shard_map(
        on_device, mesh=mesh, in_specs=in_specs, out_specs=out_specs, check_vma=False
    )
```

time: 168 us -> 62.8 us (0.37)
  the two profiles are of different devices: /device:TPU:0 before, /device:TPU:1 now
where the time goes in v1:
time: 62.8 us; the launch traced here: 62.5 us
  waiting for transfers between devices  29.5 us (47%)
  starting transfers between devices  17.5 us (28%)
  local copies, waits for them, and re-layouts  6.77 us (11%)
  Pallas kernels  4.21 us (7%)
  other arithmetic  3.82 us (6%)
  between operations  0.68 us (1%)
    ppermute x14, waiting for transfers between devices, exchange(): return lax.ppermute(value, axis, [(i, i ^ distance) for i in range(size)])  29.5 us
    ppermute x14, starting transfers between devices, exchange(): return lax.ppermute(value, axis, [(i, i ^ distance) for i in range(size)])  17.5 us
    unnamed x12, local copies, waits for them, and re-layouts  6.02 us
    pallas_call x4, Pallas kernels, call(): pl.pallas_call(kernel, out_shape=out_shape, compiler_params=pltpu.Compile...  4.21 us
    mul x1, other arithmetic, on_device(): shared_out = summed * (2.0 / (tok_rows * experts * peers))  1.7 us
  transfers between devices with their start and end apart: 14, of which 7 were waited for; matrix products, arithmetic and copies ran while one was open for 3% of the time, Pallas kernels for 5%

profile of v1, /device:TPU:1, one launch (start us, length us, event | category | flops | bytes accessed | tf_op | source)
XLA Modules:
  0.0 62.5 jit_solution(16385799268778724629)
XLA Ops:
  0.8 3.9 %collective-permute-done.6.other_ref = bf16[128,7168]{1,0:T(8,128)(2,1)S(1)} collective-permute-done((bf16[128,7168]{1,0:T(8,128)(2,1)}, bf16[128,7168]{1,0:T(8,128)(2,1)S(1)}, u32[]{:S(2)}, u32[]{:S(2)}) %collective-permute-start.6) | collective-permute-done | bytes 1835040 | tf_op jit(solution)/shard_map/ppermute | solution.py:19
  4.7 1.2 %copy-done.3 = bf16[128,7168]{1,0:T(8,128)(2,1)} copy-done((bf16[128,7168]{1,0:T(8,128)(2,1)}, bf16[128,7168]{1,0:T(8,128)(2,1)S(1)}, u32[]{:S(2)}) %copy-start.3) | copy-done | bytes 1835032
  5.9 1.5 %copy-done.1 = bf16[128,7168]{1,0:T(8,128)(2,1)S(1)} copy-done((bf16[128,7168]{1,0:T(8,128)(2,1)S(1)}, bf16[128,7168]{1,0:T(8,128)(2,1)}, u32[]{:S(2)}) %copy-start.1) | copy-done | bytes 1835032
  7.4 1.5 %copy-done.4 = bf16[128,7168]{1,0:T(8,128)(2,1)S(1)} copy-done((bf16[128,7168]{1,0:T(8,128)(2,1)S(1)}, bf16[128,7168]{1,0:T(8,128)(2,1)}, u32[]{:S(2)}) %copy-start.4) | copy-done | bytes 1835032
  8.9 1.2 %shard_map.44 = f32[7168,128]{1,0:T(8,128)S(1)} custom-call(bf16[128,7168]{1,0:T(8,128)(2,1)S(1)} %copy-done.1, bf16[128,7168]{1,0:T(8,128)(2,1)S(1)} %copy-done.4), custom_call_target="tpu_custom_call" | custom-call | flops 469762048 | bytes 7340032 | tf_op jit(solution)/shard_map/pallas_call | solution.py:24
  10.1 1.8 %copy-done = f32[7168,128]{1,0:T(8,128)} copy-done((f32[7168,128]{1,0:T(8,128)}, f32[7168,128]{1,0:T(8,128)S(1)}, u32[]{:S(2)}) %copy-start) | copy-done | bytes 3670040
  12.6 2.3 %collective-permute-start.11 = (f32[448,128]{1,0:T(8,128)S(1)}, f32[448,128]{1,0:T(8,128)S(1)}, u32[]{:S(2)}, u32[]{:S(2)}) collective-permute-start(f32[448,128]{1,0:T(8,128)S(1)} %get-tuple-element.19), channel_id=1, source_target_pairs={{0,2},{1,3},{2,0},{3,1},{4,6},{5,7},{6,4},{7,5},{8,10},{9,11},{10,... | collective-permute-start | bytes 688136 | tf_op jit(solution)/shard_map/ppermute | solution.py:19
  15.0 1.4 %collective-permute-start.10 = (f32[448,128]{1,0:T(8,128)}, f32[448,128]{1,0:T(8,128)S(1)}, u32[]{:S(2)}, u32[]{:S(2)}) collective-permute-start(f32[448,128]{1,0:T(8,128)} %get-tuple-element.20), channel_id=1, source_target_pairs={{0,2},{1,3},{2,0},{3,1},{4,6},{5,7},{6,4},{7,5},{8,10},{9,11},{10,... | collective-permute-start | bytes 688136 | tf_op jit(solution)/shard_map/ppermute | solution.py:19
  16.5 4.2 %collective-permute-done.11 = f32[448,128]{1,0:T(8,128)S(1)} collective-permute-done((f32[448,128]{1,0:T(8,128)S(1)}, f32[448,128]{1,0:T(8,128)S(1)}, u32[]{:S(2)}, u32[]{:S(2)}) %collective-permute-start.11) | collective-permute-done | bytes 229408 | tf_op jit(solution)/shard_map/ppermute | solution.py:19
  20.7 4.9 %collective-permute-done.8 = f32[448,128]{1,0:T(8,128)S(1)} collective-permute-done((f32[448,128]{1,0:T(8,128)S(1)}, f32[448,128]{1,0:T(8,128)S(1)}, u32[]{:S(2)}, u32[]{:S(2)}) %collective-permute-start.8) | collective-permute-done | bytes 229408 | tf_op jit(solution)/shard_map/ppermute | solution.py:19
  25.6 1.1 %dynamic-slice_add_fusion.1 = (f32[448,128]{1,0:T(8,128)S(1)}, f32[448,128]{1,0:T(8,128)S(1)}) fusion(f32[448,128]{1,0:T(8,128)S(1)} %collective-permute-done.8, f32[7168,128]{1,0:T(8,128)} %copy-done, s32[]{:T(128)S(6)} %select_n.26, f32[448,128]{1,0:T(8,128)S(1)} %collective-permute-done.11, s32[]{:T(128)S(6)} %select_n.30), kind=kLoop, calls=%fused_computation.3 | loop fusion | flops 114688 | bytes 1376264 | tf_op jit(solution)/shard_map/add | solution.py:150
  26.7 1.3 %collective-permute-start.12 = (f32[448,128]{1,0:T(8,128)S(1)}, f32[448,128]{1,0:T(8,128)S(1)}, u32[]{:S(2)}, u32[]{:S(2)}) collective-permute-start(f32[448,128]{1,0:T(8,128)S(1)} %get-tuple-element.23), channel_id=1, source_target_pairs={{0,4},{4,0},{8,12},{12,8},{1,5},{5,1},{9,13},{13,9},{2,6},{6,2},{1... | collective-permute-start | bytes 688136 | tf_op jit(solution)/shard_map/ppermute | solution.py:19
  28.8 2.3 %collective-permute-start.1 = (bf16[8,7296]{1,0:T(8,128)(2,1)S(1)}, bf16[8,7296]{1,0:T(8,128)(2,1)S(1)}, u32[]{:S(2)}, u32[]{:S(2)}) collective-permute-start(bf16[8,7296]{1,0:T(8,128)(2,1)S(1)} %get-tuple-element.12), channel_id=1, source_target_pairs={{0,8},{4,12},{8,0},{12,4},{1,9},{5,13},{9,1},{13,5},{2,10},{6,14},... | collective-permute-start | bytes 350216 | tf_op jit(solution)/shard_map/ppermute | solution.py:19
  31.1 1.1 %collective-permute-start.2 = (bf16[8,7296]{1,0:T(8,128)(2,1)S(1)}, bf16[8,7296]{1,0:T(8,128)(2,1)S(1)}, u32[]{:S(2)}, u32[]{:S(2)}) collective-permute-start(bf16[8,7296]{1,0:T(8,128)(2,1)S(1)} %get-tuple-element.13), channel_id=1, source_target_pairs={{0,12},{4,8},{8,4},{12,0},{1,13},{5,9},{9,5},{13,1},{2,14},{6,10},... | collective-permute-start | bytes 350216 | tf_op jit(solution)/shard_map/ppermute | solution.py:19
  32.1 4.7 %collective-permute-done.refs_1_ = bf16[8,7296]{1,0:T(8,128)(2,1)S(1)} collective-permute-done((bf16[8,7296]{1,0:T(8,128)(2,1)S(1)}, bf16[8,7296]{1,0:T(8,128)(2,1)S(1)}, u32[]{:S(2)}, u32[]{:S(2)}) %collective-permute-start) | collective-permute-done | bytes 116768 | tf_op jit(solution)/shard_map/ppermute | solution.py:19
  36.9 4.1 %collective-permute-done.2.refs_3_ = bf16[8,7296]{1,0:T(8,128)(2,1)S(1)} collective-permute-done((bf16[8,7296]{1,0:T(8,128)(2,1)S(1)}, bf16[8,7296]{1,0:T(8,128)(2,1)S(1)}, u32[]{:S(2)}, u32[]{:S(2)}) %collective-permute-start.2) | collective-permute-done | bytes 116768 | tf_op jit(solution)/shard_map/ppermute | solution.py:19
  41.1 3.3 %collective-permute-start.3 = (bf16[32,2304]{1,0:T(8,128)(2,1)S(1)}, bf16[32,2304]{1,0:T(8,128)(2,1)S(1)}, u32[]{:S(2)}, u32[]{:S(2)}) collective-permute-start(bf16[32,2304]{1,0:T(8,128)(2,1)S(1)} %get-tuple-element.15), channel_id=1, source_target_pairs={{0,1},{1,0},{2,3},{3,2},{4,5},{5,4},{6,7},{7,6},{8,9},{9,8},{10,11... | collective-permute-start | bytes 442376 | tf_op jit(solution)/shard_map/ppermute | solution.py:19
  44.4 1.2 %collective-permute-start.7 = (f32[448,128]{1,0:T(8,128)S(1)}, f32[448,128]{1,0:T(8,128)S(1)}, u32[]{:S(2)}, u32[]{:S(2)}) collective-permute-start(f32[448,128]{1,0:T(8,128)S(1)} %get-tuple-element.18), channel_id=1, source_target_pairs={{0,2},{1,3},{2,0},{3,1},{4,6},{5,7},{6,4},{7,5},{8,10},{9,11},{10,... | collective-permute-start | bytes 688136 | tf_op jit(solution)/shard_map/ppermute | solution.py:19
  46.6 1.6 %collective-permute-start.13 = (f32[448,128]{1,0:T(8,128)S(1)}, f32[448,128]{1,0:T(8,128)S(1)}, u32[]{:S(2)}, u32[]{:S(2)}) collective-permute-start(f32[448,128]{1,0:T(8,128)S(1)} %add_add_fusion), channel_id=1, source_target_pairs={{0,8},{4,12},{8,0},{12,4},{1,9},{5,13},{9,1},{13,5},{2,10},{6,14},... | collective-permute-start | bytes 688136 | tf_op jit(solution)/shard_map/ppermute | solution.py:19
  48.5 2.2 %collective-permute-start.5 = (bf16[32,2304]{1,0:T(8,128)(2,1)S(1)}, bf16[32,2304]{1,0:T(8,128)(2,1)S(1)}, u32[]{:S(2)}, u32[]{:S(2)}) collective-permute-start(bf16[32,2304]{1,0:T(8,128)(2,1)S(1)} %get-tuple-element.17), channel_id=1, source_target_pairs={{0,3},{1,2},{2,1},{3,0},{4,7},{5,6},{6,5},{7,4},{8,11},{9,10},{10,... | collective-permute-start | bytes 442376 | tf_op jit(solution)/shard_map/ppermute | solution.py:19
  50.7 4.0 %collective-permute-done.4.refs_2_ = bf16[32,2304]{1,0:T(8,128)(2,1)S(1)} collective-permute-done((bf16[32,2304]{1,0:T(8,128)(2,1)S(1)}, bf16[32,2304]{1,0:T(8,128)(2,1)S(1)}, u32[]{:S(2)}, u32[]{:S(2)}) %collective-permute-start.4) | collective-permute-done | bytes 147488 | tf_op jit(solution)/shard_map/ppermute | solution.py:19
  54.7 3.6 %collective-permute-done.5.refs_3_ = bf16[32,2304]{1,0:T(8,128)(2,1)S(1)} collective-permute-done((bf16[32,2304]{1,0:T(8,128)(2,1)S(1)}, bf16[32,2304]{1,0:T(8,128)(2,1)S(1)}, u32[]{:S(2)}, u32[]{:S(2)}) %collective-permute-start.5) | collective-permute-done | bytes 147488 | tf_op jit(solution)/shard_map/ppermute | solution.py:19
  58.3 2.5 %shard_map.43 = f32[1,384,1792]{2,1,0:T(8,128)} custom-call(bf16[32,2304]{1,0:T(8,128)(2,1)S(1)} %get-tuple-element.14.refs_0_, bf16[32,2304]{1,0:T(8,128)(2,1)S(1)} %collective-permute-done.3.refs_1_, bf16[32,2304]{1,0:T(8,128)(2,1)S(1)} %collective-permute-done.4.refs_2_, bf16[32,2304]{1,0:T(8,128)(2,1)S(1)} %collective-permute-done.5.refs_3_), custom_call_target="tpu_custom_call" | custom-call | flops 176160768 | bytes 2752512 | tf_op jit(solution)/shard_map/pallas_call | solution.py:24
  60.8 1.7 %add_multiply_fusion = f32[448,128]{1,0:T(8,128)} fusion(f32[448,128]{1,0:T(8,128)S(1)} %collective-permute-done.13, f32[448,128]{1,0:T(8,128)S(1)} %collective-permute-done.9, f32[448,128]{1,0:T(8,128)S(1)} %collective-permute-done.7, f32[7168,128]{1,0:T(8,128)} %copy-done, s32[]{:T(128)S(6)} %select_n.24), kind=kLoop, calls=%fused_computation | loop fusion | flops 229376 | bytes 1146884 | tf_op jit(solution)/shard_map/mul | solution.py:159
  (24 shorter events, 3.1 us)
Async XLA Ops:
  0.6 4.1 %collective-permute-start.6 = (bf16[128,7168]{1,0:T(8,128)(2,1)}, bf16[128,7168]{1,0:T(8,128)(2,1)S(1)}, u32[]{:S(2)}, u32[]{:S(2)}) collective-permute-start(bf16[128,7168]{1,0:T(8,128)(2,1)} %mine_ref.1), channel_id=1, source_target_pairs={{0,1},{1,0},{2,3},{3,2},{4,5},{5,4},{6,7},{7,6},{8,9},{9,8},{10,11... | collective-permute-start | bytes 5505032 | tf_op jit(solution)/shard_map/ppermute | solution.py:19
  4.7 1.2 %copy-start.3 = (bf16[128,7168]{1,0:T(8,128)(2,1)}, bf16[128,7168]{1,0:T(8,128)(2,1)S(1)}, u32[]{:S(2)}) copy-start(bf16[128,7168]{1,0:T(8,128)(2,1)S(1)} %collective-permute-done.6.other_ref) | copy-start | bytes 5505028
  5.9 1.5 %copy-start.1 = (bf16[128,7168]{1,0:T(8,128)(2,1)S(1)}, bf16[128,7168]{1,0:T(8,128)(2,1)}, u32[]{:S(2)}) copy-start(bf16[128,7168]{1,0:T(8,128)(2,1)} %mine_ref.1) | copy-start | bytes 5505028
  7.4 1.5 %copy-start.4 = (bf16[128,7168]{1,0:T(8,128)(2,1)S(1)}, bf16[128,7168]{1,0:T(8,128)(2,1)}, u32[]{:S(2)}) copy-start(bf16[128,7168]{1,0:T(8,128)(2,1)} %copy-done.3) | copy-start | bytes 5505028
  8.9 19.1 %copy-start.2 = (bf16[128,7168]{1,0:T(8,128)(2,1)S(1)}, bf16[128,7168]{1,0:T(8,128)(2,1)}, u32[]{:S(2)}) copy-start(bf16[128,7168]{1,0:T(8,128)(2,1)} %mine_ref.1) | copy-start | bytes 5505028
  8.9 19.1 %copy-start.5 = (s32[128,8]{0,1:T(8,128)S(1)}, s32[128,8]{0,1:T(8,128)}, u32[]{:S(2)}) copy-start(s32[128,8]{0,1:T(8,128)} %param.3) | copy-start | bytes 12292
  10.1 1.8 %copy-start = (f32[7168,128]{1,0:T(8,128)}, f32[7168,128]{1,0:T(8,128)S(1)}, u32[]{:S(2)}) copy-start(f32[7168,128]{1,0:T(8,128)S(1)} %shard_map.44) | copy-start | bytes 11010052
  12.6 8.0 %collective-permute-start.11 = (f32[448,128]{1,0:T(8,128)S(1)}, f32[448,128]{1,0:T(8,128)S(1)}, u32[]{:S(2)}, u32[]{:S(2)}) collective-permute-start(f32[448,128]{1,0:T(8,128)S(1)} %get-tuple-element.19), channel_id=1, source_target_pairs={{0,2},{1,3},{2,0},{3,1},{4,6},{5,7},{6,4},{7,5},{8,10},{9,11},{10,... | collective-permute-start | bytes 688136 | tf_op jit(solution)/shard_map/ppermute | solution.py:19
  15.0 10.6 %collective-permute-start.8 = (f32[448,128]{1,0:T(8,128)S(1)}, f32[448,128]{1,0:T(8,128)S(1)}, u32[]{:S(2)}, u32[]{:S(2)}) collective-permute-start(f32[448,128]{1,0:T(8,128)S(1)} %get-tuple-element.21), channel_id=1, source_target_pairs={{0,2},{1,3},{2,0},{3,1},{4,6},{5,7},{6,4},{7,5},{8,10},{9,11},{10,... | collective-permute-start | bytes 688136 | tf_op jit(solution)/shard_map/ppermute | solution.py:19
  15.0 30.5 %collective-permute-start.10 = (f32[448,128]{1,0:T(8,128)}, f32[448,128]{1,0:T(8,128)S(1)}, u32[]{:S(2)}, u32[]{:S(2)}) collective-permute-start(f32[448,128]{1,0:T(8,128)} %get-tuple-element.20), channel_id=1, source_target_pairs={{0,2},{1,3},{2,0},{3,1},{4,6},{5,7},{6,4},{7,5},{8,10},{9,11},{10,... | collective-permute-start | bytes 688136 | tf_op jit(solution)/shard_map/ppermute | solution.py:19
  26.7 18.9 %collective-permute-start.12 = (f32[448,128]{1,0:T(8,128)S(1)}, f32[448,128]{1,0:T(8,128)S(1)}, u32[]{:S(2)}, u32[]{:S(2)}) collective-permute-start(f32[448,128]{1,0:T(8,128)S(1)} %get-tuple-element.23), channel_id=1, source_target_pairs={{0,4},{4,0},{8,12},{12,8},{1,5},{5,1},{9,13},{13,9},{2,6},{6,2},{1... | collective-permute-start | bytes 688136 | tf_op jit(solution)/shard_map/ppermute | solution.py:19
  28.5 8.4 %collective-permute-start = (bf16[8,7296]{1,0:T(8,128)(2,1)S(1)}, bf16[8,7296]{1,0:T(8,128)(2,1)S(1)}, u32[]{:S(2)}, u32[]{:S(2)}) collective-permute-start(bf16[8,7296]{1,0:T(8,128)(2,1)S(1)} %get-tuple-element.11), channel_id=1, source_target_pairs={{0,4},{4,0},{8,12},{12,8},{1,5},{5,1},{9,13},{13,9},{2,6},{6,2},{1... | collective-permute-start | bytes 350216 | tf_op jit(solution)/shard_map/ppermute | solution.py:19
  28.8 8.1 %collective-permute-start.1 = (bf16[8,7296]{1,0:T(8,128)(2,1)S(1)}, bf16[8,7296]{1,0:T(8,128)(2,1)S(1)}, u32[]{:S(2)}, u32[]{:S(2)}) collective-permute-start(bf16[8,7296]{1,0:T(8,128)(2,1)S(1)} %get-tuple-element.12), channel_id=1, source_target_pairs={{0,8},{4,12},{8,0},{12,4},{1,9},{5,13},{9,1},{13,5},{2,10},{6,14},... | collective-permute-start | bytes 350216 | tf_op jit(solution)/shard_map/ppermute | solution.py:19
  31.1 10.0 %collective-permute-start.2 = (bf16[8,7296]{1,0:T(8,128)(2,1)S(1)}, bf16[8,7296]{1,0:T(8,128)(2,1)S(1)}, u32[]{:S(2)}, u32[]{:S(2)}) collective-permute-start(bf16[8,7296]{1,0:T(8,128)(2,1)S(1)} %get-tuple-element.13), channel_id=1, source_target_pairs={{0,12},{4,8},{8,4},{12,0},{1,13},{5,9},{9,5},{13,1},{2,14},{6,10},... | collective-permute-start | bytes 350216 | tf_op jit(solution)/shard_map/ppermute | solution.py:19
  41.1 7.4 %collective-permute-start.3 = (bf16[32,2304]{1,0:T(8,128)(2,1)S(1)}, bf16[32,2304]{1,0:T(8,128)(2,1)S(1)}, u32[]{:S(2)}, u32[]{:S(2)}) collective-permute-start(bf16[32,2304]{1,0:T(8,128)(2,1)S(1)} %get-tuple-element.15), channel_id=1, source_target_pairs={{0,1},{1,0},{2,3},{3,2},{4,5},{5,4},{6,7},{7,6},{8,9},{9,8},{10,11... | collective-permute-start | bytes 442376 | tf_op jit(solution)/shard_map/ppermute | solution.py:19
  44.4 16.5 %collective-permute-start.7 = (f32[448,128]{1,0:T(8,128)S(1)}, f32[448,128]{1,0:T(8,128)S(1)}, u32[]{:S(2)}, u32[]{:S(2)}) collective-permute-start(f32[448,128]{1,0:T(8,128)S(1)} %get-tuple-element.18), channel_id=1, source_target_pairs={{0,2},{1,3},{2,0},{3,1},{4,6},{5,7},{6,4},{7,5},{8,10},{9,11},{10,... | collective-permute-start | bytes 688136 | tf_op jit(solution)/shard_map/ppermute | solution.py:19
  45.5 15.3 %collective-permute-start.9 = (f32[448,128]{1,0:T(8,128)S(1)}, f32[448,128]{1,0:T(8,128)S(1)}, u32[]{:S(2)}, u32[]{:S(2)}) collective-permute-start(f32[448,128]{1,0:T(8,128)S(1)} %get-tuple-element.22), channel_id=1, source_target_pairs={{0,4},{4,0},{8,12},{12,8},{1,5},{5,1},{9,13},{13,9},{2,6},{6,2},{1... | collective-permute-start | bytes 688136 | tf_op jit(solution)/shard_map/ppermute | solution.py:19
  46.6 14.3 %collective-permute-start.13 = (f32[448,128]{1,0:T(8,128)S(1)}, f32[448,128]{1,0:T(8,128)S(1)}, u32[]{:S(2)}, u32[]{:S(2)}) collective-permute-start(f32[448,128]{1,0:T(8,128)S(1)} %add_add_fusion), channel_id=1, source_target_pairs={{0,8},{4,12},{8,0},{12,4},{1,9},{5,13},{9,1},{13,5},{2,10},{6,14},... | collective-permute-start | bytes 688136 | tf_op jit(solution)/shard_map/ppermute | solution.py:19
  48.2 6.5 %collective-permute-start.4 = (bf16[32,2304]{1,0:T(8,128)(2,1)S(1)}, bf16[32,2304]{1,0:T(8,128)(2,1)S(1)}, u32[]{:S(2)}, u32[]{:S(2)}) collective-permute-start(bf16[32,2304]{1,0:T(8,128)(2,1)S(1)} %get-tuple-element.16), channel_id=1, source_target_pairs={{0,2},{1,3},{2,0},{3,1},{4,6},{5,7},{6,4},{7,5},{8,10},{9,11},{10,... | collective-permute-start | bytes 442376 | tf_op jit(solution)/shard_map/ppermute | solution.py:19
  48.5 9.8 %collective-permute-start.5 = (bf16[32,2304]{1,0:T(8,128)(2,1)S(1)}, bf16[32,2304]{1,0:T(8,128)(2,1)S(1)}, u32[]{:S(2)}, u32[]{:S(2)}) collective-permute-start(bf16[32,2304]{1,0:T(8,128)(2,1)S(1)} %get-tuple-element.17), channel_id=1, source_target_pairs={{0,3},{1,2},{2,1},{3,0},{4,7},{5,6},{6,5},{7,4},{8,11},{9,10},{10,... | collective-permute-start | bytes 442376 | tf_op jit(solution)/shard_map/ppermute | solution.py:19

commit v2 on v1

--- a/solution.py
+++ b/solution.py
@@ -11,7 +11,7 @@
 SBAND = 128
 CAP = 8
 LANES = 128
-VMEM_LIMIT = 32 * 1024 * 1024
+VMEM_LIMIT = 16 * 1024 * 1024
 
 
 def exchange(value, axis, distance):
@@ -19,8 +19,7 @@
     return lax.ppermute(value, axis, [(i, i ^ distance) for i in range(size)])
 
 
-def call(kernel, out_shape, *operands, flops, nbytes, grid_spec=None):
-    where = {"grid_spec": grid_spec} if grid_spec is not None else {}
+def call(kernel, out_shape, *operands, flops, nbytes, **where):
     return pl.pallas_call(
         kernel,
         out_shape=out_shape,
@@ -30,10 +29,23 @@
     )(*operands)
 
 
-def select_kernel(ids_ref, tokens_ref, *out_refs):
+def parts_of(features):
+    step = -(-features // (4 * LANES)) * LANES
+    return [slice(b, min(b + step, features)) for b in range(0, features, step)]
+
+
+def select_kernel(ids_ref, tokens_ref, *refs):
+    out_refs, held, sems = refs[:-2], refs[-2], refs[-1]
     me = lax.axis_index("expert")
     experts = len(out_refs)
     rows, features = tokens_ref.shape
+    parts = parts_of(features)
+    copies = [
+        pltpu.make_async_copy(tokens_ref.at[:, part], held.at[:, part], sems.at[i])
+        for i, part in enumerate(parts)
+    ]
+    for copy in copies:
+        copy.start()
     ids = ids_ref[...]
     members = [
         jnp.max((ids == (me ^ k)).astype(jnp.float32), axis=0, keepdims=True)
@@ -54,12 +66,14 @@
         axis=0,
     )
     flags = jnp.broadcast_to(jnp.sum(picks, axis=1, keepdims=True), (experts * CAP, LANES))
-    chosen = jnp.dot(
-        picks.astype(jnp.bfloat16), tokens_ref[...], preferred_element_type=jnp.float32
-    )
+    picks = picks.astype(jnp.bfloat16)
     for k, out_ref in enumerate(out_refs):
-        out_ref[:, :features] = chosen[k * CAP : (k + 1) * CAP].astype(jnp.bfloat16)
         out_ref[:, features:] = flags[k * CAP : (k + 1) * CAP].astype(jnp.bfloat16)
+    for copy, part in zip(copies, parts):
+        copy.wait()
+        chosen = jnp.dot(picks, held[:, part], preferred_element_type=jnp.float32)
+        for k, out_ref in enumerate(out_refs):
+            out_ref[:, part] = chosen[k * CAP : (k + 1) * CAP].astype(jnp.bfloat16)
 
 
 def split_kernel(*refs, peers):
@@ -99,26 +113,59 @@
     out_ref[0] = product * (2.0 / count)
 
 
-def pair_kernel(mine_ref, other_ref, out_ref):
+def pair_kernel(mine_ref, other_ref, *refs, experts, peers, order, aligned):
+    out_refs, mine, other, sems = refs[:-3], refs[-3], refs[-2], refs[-1]
     features = mine_ref.shape[1]
-    block = 4 * LANES
-    lead = jnp.concatenate([mine_ref[:, :SBAND], other_ref[:, :SBAND]], axis=0)
-    for begin in range(0, features, block):
-        part = slice(begin, min(begin + block, features))
-        rows = jnp.concatenate([mine_ref[:, part], other_ref[:, part]], axis=0)
-        out_ref[part] = lax.dot_general(
+    parts = parts_of(features)
+    copies = [
+        (
+            pltpu.make_async_copy(mine_ref.at[:, part], mine.at[:, part], sems.at[0, i]),
+            pltpu.make_async_copy(other_ref.at[:, part], other.at[:, part], sems.at[1, i]),
+        )
+        for i, part in enumerate(parts)
+    ]
+    for pair in copies:
+        for copy in pair:
+            copy.start()
+    for pair in copies:
+        for copy in pair:
+            copy.wait()
+    lead = jnp.concatenate([mine[:, :SBAND], other[:, :SBAND]], axis=0)
+
+    def product(columns):
+        rows = jnp.concatenate([mine[:, columns], other[:, columns]], axis=0)
+        return lax.dot_general(
             rows, lead, (((0,), (0,)), ((), ())), preferred_element_type=jnp.float32
         )
+
+    if not aligned:
+        for part in parts:
+            out_refs[0][part] = product(part)
+        return
+    e = lax.axis_index("expert")
+    d = lax.axis_index("dp")
+    share = features // (experts * peers)
+    half = LANES // 2
+    window = share + half * (share // half % 2)
+    for i, m in enumerate(order):
+        for j, k in enumerate(range(0, peers, 2)):
+            start = ((e ^ m) * peers + (d ^ k)) * (share // half)
+            odd = start % 2
+            found = product(pl.ds(pl.multiple_of((start - odd) * half, LANES), window))
+            if window > share:
+                found = jnp.where(odd == 1, found[half:], found[:share])
+            out_refs[i * (peers // 2) + j][...] = found
 
 
 def on_device(tokens, expert_ids):
     tok_rows, features = tokens.shape
     experts = lax.axis_size("expert")
     peers = lax.axis_size("dp")
-    e = lax.axis_index("expert")
-    d = lax.axis_index("dp")
     width = features // peers
     share = features // (experts * peers)
+    steps = len(parts_of(features))
+    whole = pl.BlockSpec(memory_space=pltpu.HBM)
+    inside = pl.BlockSpec(memory_space=pltpu.VMEM)
 
     other = exchange(tokens, "dp", 1)
 
@@ -129,28 +176,50 @@
         tokens,
         flops=2 * experts * CAP * tok_rows * features,
         nbytes=2 * (tok_rows + experts * CAP) * features,
-    )
-    arrived = [outgoing[0]] + [exchange(outgoing[k], "expert", k) for k in range(1, experts)]
-
-    pair = call(
-        pair_kernel,
-        jax.ShapeDtypeStruct((features, SBAND), jnp.float32),
+        in_specs=[inside, whole],
+        scratch_shapes=[
+            pltpu.VMEM((tok_rows, features), jnp.bfloat16),
+            pltpu.SemaphoreType.DMA((steps,)),
+        ],
+    )
+    outgoing, other = lax.optimization_barrier((outgoing, other))
+
+    order = list(range(3, experts, 2)) + list(range(2, experts, 2)) + [1, 0]
+    aligned = share % (LANES // 2) == 0
+    blocks = call(
+        functools.partial(
+            pair_kernel, experts=experts, peers=peers, order=order, aligned=aligned
+        ),
+        [jax.ShapeDtypeStruct((share, SBAND), jnp.float32)] * (experts * peers // 2)
+        if aligned
+        else [jax.ShapeDtypeStruct((features, SBAND), jnp.float32)],
         tokens,
         other,
         flops=4 * tok_rows * features * SBAND,
         nbytes=4 * tok_rows * features + 4 * features * SBAND,
-    )
-
-    def block(m, k):
-        start = ((e ^ m) * peers + (d ^ k)) * share
-        return lax.dynamic_slice_in_dim(pair, start, share, axis=0)
-
-    def over_dp(m):
-        far = [exchange(block(m, k), "dp", k) for k in range(2, peers, 2)]
-        return sum(far, block(m, 0))
-
-    order = list(range(3, experts, 2)) + list(range(2, experts, 2)) + [1, 0]
-    part = {m: over_dp(m) for m in order}
+        in_specs=[whole, whole],
+        scratch_shapes=[
+            pltpu.VMEM((tok_rows, features), jnp.bfloat16),
+            pltpu.VMEM((tok_rows, features), jnp.bfloat16),
+            pltpu.SemaphoreType.DMA((2, steps)),
+        ],
+    )
+    if not aligned:
+        e, d = lax.axis_index("expert"), lax.axis_index("dp")
+        blocks = [
+            lax.dynamic_slice_in_dim(
+                blocks[0], ((e ^ m) * peers + (d ^ k)) * share, share, axis=0
+            )
+            for m in order
+            for k in range(0, peers, 2)
+        ]
+    outgoing, blocks = lax.optimization_barrier((outgoing, blocks))
+
+    part = {}
+    for i, m in enumerate(order):
+        own, *sent = blocks[i * (peers // 2) : (i + 1) * (peers // 2)]
+        part[m] = sum([exchange(x, "dp", 2 * k + 2) for k, x in enumerate(sent)], own)
+    arrived = [outgoing[0]] + [exchange(outgoing[k], "expert", k) for k in range(1, experts)]
     for m in range(2, experts, 2):
         part[m] = part[m] + exchange(part[m + 1], "expert", 1)
     summed = part[0] + exchange(part[1], "expert", 1)

time: 62.8 us -> 45.2 us (0.72)
  waiting for transfers between devices: 29.5 us -> 17.4 us
  local copies, waits for them, and re-layouts: 6.77 us -> 2.19 us
  other arithmetic: 3.82 us -> 0.85 us
  starting transfers between devices: 17.5 us -> 18.7 us
  Pallas kernels: 4.21 us -> 5.09 us
    ppermute x14, waiting for transfers between devices: 29.5 us -> 17.4 us  [exchange(): return lax.ppermute(value, axis, [(i, i ^ distance) for i in range(size)])]
    unnamed x12 -> x6, local copies, waits for them, and re-layouts: 6.02 us -> 2.19 us
    ppermute x14, starting transfers between devices: 17.5 us -> 18.7 us  [exchange(): return lax.ppermute(value, axis, [(i, i ^ distance) for i in range(size)])]
    add x1 -> x2, other arithmetic: 1.13 us -> 0.06 us  [on_device(): sum([exchange(x, 'dp', 2 * k + 2) for k, x in enumerate(sent)], own)]
    add x1, other arithmetic: 0.99 us -> 0.04 us  [on_device(): part[m] = part[m] + exchange(part[m + 1], 'expert', 1)]
    mul x1, other arithmetic: 1.7 us -> 0.75 us  [on_device(): shared_out = summed * (2.0 / (tok_rows * experts * peers))]
    pallas_call x4, Pallas kernels: 4.21 us -> 5.09 us  [call(): pl.pallas_call(kernel, out_shape=out_shape, compiler_params=pltpu.Compile...]
    dynamic_slice x1 -> x0, local copies, waits for them, and re-layouts: 0.75 us -> none  [block(): return lax.dynamic_slice_in_dim(pair, start, share, axis=0)]
  transfers between devices with their start and end apart: 14 -> 14, of which waited for: 7 -> 6; matrix products, arithmetic and copies ran while one was open for 3% -> 0% of each run, Pallas kernels for 5% -> 8%
where the time goes in v2:
time: 45.2 us; the launch traced here: 45 us
  starting transfers between devices  18.7 us (41%)
  waiting for transfers between devices  17.4 us (38%)
  Pallas kernels  5.09 us (11%)
  local copies, waits for them, and re-layouts  2.19 us (5%)
  other arithmetic  0.85 us (2%)
  between operations  0.68 us (2%)
    ppermute x14, starting transfers between devices, exchange(): return lax.ppermute(value, axis, [(i, i ^ distance) for i in range(size)])  18.7 us
    ppermute x14, waiting for transfers between devices, exchange(): return lax.ppermute(value, axis, [(i, i ^ distance) for i in range(size)])  17.4 us
    pallas_call x4, Pallas kernels, call(): pl.pallas_call(kernel, out_shape=out_shape, compiler_params=pltpu.Compile...  5.09 us
    unnamed x6, local copies, waits for them, and re-layouts  2.19 us
  transfers between devices with their start and end apart: 14, of which 6 were waited for; matrix products, arithmetic and copies ran while one was open for 0% of the time, Pallas kernels for 8%

profile of v2, /device:TPU:1, one launch (start us, length us, event | category | flops | bytes accessed | tf_op | source)
XLA Modules:
  0.0 45.0 jit_solution(18184451606648287925)
XLA Ops:
  0.8 1.5 %copy-done = bf16[128,7168]{1,0:T(8,128)(2,1)S(1)} copy-done((bf16[128,7168]{1,0:T(8,128)(2,1)S(1)}, bf16[128,7168]{1,0:T(8,128)(2,1)}, u32[]{:S(2)}) %copy-start) | copy-done | bytes 1835032
  2.3 0.7 %copy-done.2 = s32[128,8]{0,1:T(8,128)S(1)} copy-done((s32[128,8]{0,1:T(8,128)S(1)}, s32[128,8]{0,1:T(8,128)}, u32[]{:S(2)}) %copy-start.2) | copy-done | bytes 4120
  2.9 1.3 %shard_map.41 = (bf16[8,7296]{1,0:T(8,128)(2,1)S(1)}, bf16[8,7296]{1,0:T(8,128)(2,1)S(1)}, bf16[8,7296]{1,0:T(8,128)(2,1)S(1)}, bf16[8,7296]{1,0:T(8,128)(2,1)S(1)}) custom-call(s32[8,128]{1,0:T(8,128)S(1)} %bitcast.1, bf16[128,7168]{1,0:T(8,128)(2,1)S(1)} %copy-done), custom_call_target="tpu_custom_call" | custom-call | flops 58720256 | bytes 2293760 | tf_op jit(solution)/shard_map/pallas_call | solution.py:23
  4.2 0.5 %collective-permute-done.other_ref = bf16[128,7168]{1,0:T(8,128)(2,1)S(1)} collective-permute-done((bf16[128,7168]{1,0:T(8,128)(2,1)}, bf16[128,7168]{1,0:T(8,128)(2,1)S(1)}, u32[]{:S(2)}, u32[]{:S(2)}) %collective-permute-start) | collective-permute-done | bytes 1835040 | tf_op jit(solution)/shard_map/ppermute | solution.py:19
  4.7 1.3 %shard_map.42 = (f32[448,128]{1,0:T(8,128)S(1)}, f32[448,128]{1,0:T(8,128)S(1)}, f32[448,128]{1,0:T(8,128)S(1)}, f32[448,128]{1,0:T(8,128)S(1)}, f32[448,128]{1,...) custom-call(bf16[128,7168]{1,0:T(8,128)(2,1)S(1)} %copy-done.1, ...), custom_call_target="tpu_custom_call" | custom-call | flops 469762048 | bytes 7340032 | tf_op jit(solution)/shard_map/pallas_call | solution.py:23
  6.0 2.5 %collective-permute-start.11 = (f32[448,128]{1,0:T(8,128)S(1)}, f32[448,128]{1,0:T(8,128)S(1)}, u32[]{:S(2)}, u32[]{:S(2)}) collective-permute-start(f32[448,128]{1,0:T(8,128)S(1)} %get-tuple-element.67), channel_id=1, source_target_pairs={{0,2},{1,3},{2,0},{3,1},{4,6},{5,7},{6,4},{7,5},{8,10},{9,11},{10,... | collective-permute-start | bytes 688136 | tf_op jit(solution)/shard_map/ppermute | solution.py:19
  8.5 1.3 %collective-permute-start.1 = (bf16[8,7296]{1,0:T(8,128)(2,1)S(1)}, bf16[8,7296]{1,0:T(8,128)(2,1)S(1)}, u32[]{:S(2)}, u32[]{:S(2)}) collective-permute-start(bf16[8,7296]{1,0:T(8,128)(2,1)S(1)} %get-tuple-element.53), channel_id=1, source_target_pairs={{0,4},{4,0},{8,12},{12,8},{1,5},{5,1},{9,13},{13,9},{2,6},{6,2},{1... | collective-permute-start | bytes 350216 | tf_op jit(solution)/shard_map/ppermute | solution.py:19
  9.8 0.3 collective-permute-start.8
  10.0 1.2 %collective-permute-start.10 = (f32[448,128]{1,0:T(8,128)S(1)}, f32[448,128]{1,0:T(8,128)S(1)}, u32[]{:S(2)}, u32[]{:S(2)}) collective-permute-start(f32[448,128]{1,0:T(8,128)S(1)} %get-tuple-element.65), channel_id=1, source_target_pairs={{0,2},{1,3},{2,0},{3,1},{4,6},{5,7},{6,4},{7,5},{8,10},{9,11},{10,... | collective-permute-start | bytes 688136 | tf_op jit(solution)/shard_map/ppermute | solution.py:19
  11.2 3.0 %collective-permute-done.11 = f32[448,128]{1,0:T(8,128)S(1)} collective-permute-done((f32[448,128]{1,0:T(8,128)S(1)}, f32[448,128]{1,0:T(8,128)S(1)}, u32[]{:S(2)}, u32[]{:S(2)}) %collective-permute-start.11) | collective-permute-done | bytes 229408 | tf_op jit(solution)/shard_map/ppermute | solution.py:19
  14.2 1.3 %collective-permute-start.12 = (f32[448,128]{1,0:T(8,128)S(1)}, f32[448,128]{1,0:T(8,128)S(1)}, u32[]{:S(2)}, u32[]{:S(2)}) collective-permute-start(f32[448,128]{1,0:T(8,128)S(1)} %add.25), channel_id=1, source_target_pairs={{0,4},{4,0},{8,12},{12,8},{1,5},{5,1},{9,13},{13,9},{2,6},{6,2},{1... | collective-permute-start | bytes 688136 | tf_op jit(solution)/shard_map/ppermute | solution.py:19
  15.5 2.3 %collective-permute-start.2 = (bf16[8,7296]{1,0:T(8,128)(2,1)S(1)}, bf16[8,7296]{1,0:T(8,128)(2,1)S(1)}, u32[]{:S(2)}, u32[]{:S(2)}) collective-permute-start(bf16[8,7296]{1,0:T(8,128)(2,1)S(1)} %get-tuple-element.54), channel_id=1, source_target_pairs={{0,8},{4,12},{8,0},{12,4},{1,9},{5,13},{9,1},{13,5},{2,10},{6,14},... | collective-permute-start | bytes 350216 | tf_op jit(solution)/shard_map/ppermute | solution.py:19
  17.9 3.2 %collective-permute-done.2.refs_2_ = bf16[8,7296]{1,0:T(8,128)(2,1)S(1)} collective-permute-done((bf16[8,7296]{1,0:T(8,128)(2,1)S(1)}, bf16[8,7296]{1,0:T(8,128)(2,1)S(1)}, u32[]{:S(2)}, u32[]{:S(2)}) %collective-permute-start.2) | collective-permute-done | bytes 116768 | tf_op jit(solution)/shard_map/ppermute | solution.py:19
  21.0 1.2 %collective-permute-start.7 = (f32[448,128]{1,0:T(8,128)S(1)}, f32[448,128]{1,0:T(8,128)S(1)}, u32[]{:S(2)}, u32[]{:S(2)}) collective-permute-start(f32[448,128]{1,0:T(8,128)S(1)} %get-tuple-element.61), channel_id=1, source_target_pairs={{0,2},{1,3},{2,0},{3,1},{4,6},{5,7},{6,4},{7,5},{8,10},{9,11},{10,... | collective-permute-start | bytes 688136 | tf_op jit(solution)/shard_map/ppermute | solution.py:19
  22.3 4.0 %collective-permute-done.3.refs_3_ = bf16[8,7296]{1,0:T(8,128)(2,1)S(1)} collective-permute-done((bf16[8,7296]{1,0:T(8,128)(2,1)S(1)}, bf16[8,7296]{1,0:T(8,128)(2,1)S(1)}, u32[]{:S(2)}, u32[]{:S(2)}) %collective-permute-start.3) | collective-permute-done | bytes 116768 | tf_op jit(solution)/shard_map/ppermute | solution.py:19
  26.3 3.2 %collective-permute-start.4 = (bf16[32,2304]{1,0:T(8,128)(2,1)S(1)}, bf16[32,2304]{1,0:T(8,128)(2,1)S(1)}, u32[]{:S(2)}, u32[]{:S(2)}) collective-permute-start(bf16[32,2304]{1,0:T(8,128)(2,1)S(1)} %get-tuple-element.57), channel_id=1, source_target_pairs={{0,1},{1,0},{2,3},{3,2},{4,5},{5,4},{6,7},{7,6},{8,9},{9,8},{10,11... | collective-permute-start | bytes 442376 | tf_op jit(solution)/shard_map/ppermute | solution.py:19
  29.5 0.6 %collective-permute-start.9 = (f32[448,128]{1,0:T(8,128)S(1)}, f32[448,128]{1,0:T(8,128)S(1)}, u32[]{:S(2)}, u32[]{:S(2)}) collective-permute-start(f32[448,128]{1,0:T(8,128)S(1)} %add.22), channel_id=1, source_target_pairs={{0,4},{4,0},{8,12},{12,8},{1,5},{5,1},{9,13},{13,9},{2,6},{6,2},{1... | collective-permute-start | bytes 688136 | tf_op jit(solution)/shard_map/ppermute | solution.py:19
  30.2 2.5 %collective-permute-start.13 = (f32[448,128]{1,0:T(8,128)S(1)}, f32[448,128]{1,0:T(8,128)S(1)}, u32[]{:S(2)}, u32[]{:S(2)}) collective-permute-start(f32[448,128]{1,0:T(8,128)S(1)} %add_add_fusion), channel_id=1, source_target_pairs={{0,8},{4,12},{8,0},{12,4},{1,9},{5,13},{9,1},{13,5},{2,10},{6,14},... | collective-permute-start | bytes 688136 | tf_op jit(solution)/shard_map/ppermute | solution.py:19
  32.7 0.3 collective-permute-start.5
  33.0 1.9 %collective-permute-start.6 = (bf16[32,2304]{1,0:T(8,128)(2,1)S(1)}, bf16[32,2304]{1,0:T(8,128)(2,1)S(1)}, u32[]{:S(2)}, u32[]{:S(2)}) collective-permute-start(bf16[32,2304]{1,0:T(8,128)(2,1)S(1)} %get-tuple-element.59), channel_id=1, source_target_pairs={{0,3},{1,2},{2,1},{3,0},{4,7},{5,6},{6,5},{7,4},{8,11},{9,10},{10,... | collective-permute-start | bytes 442376 | tf_op jit(solution)/shard_map/ppermute | solution.py:19
  34.9 2.6 %collective-permute-done.5.refs_2_ = bf16[32,2304]{1,0:T(8,128)(2,1)S(1)} collective-permute-done((bf16[32,2304]{1,0:T(8,128)(2,1)S(1)}, bf16[32,2304]{1,0:T(8,128)(2,1)S(1)}, u32[]{:S(2)}, u32[]{:S(2)}) %collective-permute-start.5) | collective-permute-done | bytes 147488 | tf_op jit(solution)/shard_map/ppermute | solution.py:19
  37.5 4.2 %collective-permute-done.6.refs_3_ = bf16[32,2304]{1,0:T(8,128)(2,1)S(1)} collective-permute-done((bf16[32,2304]{1,0:T(8,128)(2,1)S(1)}, bf16[32,2304]{1,0:T(8,128)(2,1)S(1)}, u32[]{:S(2)}, u32[]{:S(2)}) %collective-permute-start.6) | collective-permute-done | bytes 147488 | tf_op jit(solution)/shard_map/ppermute | solution.py:19
  41.7 2.5 %shard_map.44 = f32[1,384,1792]{2,1,0:T(8,128)} custom-call(bf16[32,2304]{1,0:T(8,128)(2,1)S(1)} %get-tuple-element.56.refs_0_, bf16[32,2304]{1,0:T(8,128)(2,1)S(1)} %collective-permute-done.4.refs_1_, bf16[32,2304]{1,0:T(8,128)(2,1)S(1)} %collective-permute-done.5.refs_2_, bf16[32,2304]{1,0:T(8,128)(2,1)S(1)} %collective-permute-done.6.refs_3_), custom_call_target="tpu_custom_call" | custom-call | flops 176160768 | bytes 2752512 | tf_op jit(solution)/shard_map/pallas_call | solution.py:23
  44.2 0.8 %add_multiply_fusion = f32[448,128]{1,0:T(8,128)} fusion(f32[448,128]{1,0:T(8,128)S(1)} %collective-permute-done.13, f32[448,128]{1,0:T(8,128)S(1)} %collective-permute-done.9, f32[448,128]{1,0:T(8,128)S(1)} %get-tuple-element.60, f32[448,128]{1,0:T(8,128)S(1)} %collective-permute-done.7), kind=kLoop, calls=%fused_computation | loop fusion | flops 229376 | bytes 1146880 | tf_op jit(solution)/shard_map/mul | solution.py:228
  (18 shorter events, 0.3 us)
Async XLA Ops:
  0.6 4.1 %collective-permute-start = (bf16[128,7168]{1,0:T(8,128)(2,1)}, bf16[128,7168]{1,0:T(8,128)(2,1)S(1)}, u32[]{:S(2)}, u32[]{:S(2)}) collective-permute-start(bf16[128,7168]{1,0:T(8,128)(2,1)} %mine_ref.1), channel_id=1, source_target_pairs={{0,1},{1,0},{2,3},{3,2},{4,5},{5,4},{6,7},{7,6},{8,9},{9,8},{10,11... | collective-permute-start | bytes 5505032 | tf_op jit(solution)/shard_map/ppermute | solution.py:19
  0.8 1.5 %copy-start = (bf16[128,7168]{1,0:T(8,128)(2,1)S(1)}, bf16[128,7168]{1,0:T(8,128)(2,1)}, u32[]{:S(2)}) copy-start(bf16[128,7168]{1,0:T(8,128)(2,1)} %mine_ref.1) | copy-start | bytes 5505028
  2.3 0.7 %copy-start.2 = (s32[128,8]{0,1:T(8,128)S(1)}, s32[128,8]{0,1:T(8,128)}, u32[]{:S(2)}) copy-start(s32[128,8]{0,1:T(8,128)} %param.3) | copy-start | bytes 12292
  2.9 1.8 %copy-start.1 = (bf16[128,7168]{1,0:T(8,128)(2,1)S(1)}, bf16[128,7168]{1,0:T(8,128)(2,1)}, u32[]{:S(2)}) copy-start(bf16[128,7168]{1,0:T(8,128)(2,1)} %mine_ref.1) | copy-start | bytes 5505028
  6.0 8.2 %collective-permute-start.11 = (f32[448,128]{1,0:T(8,128)S(1)}, f32[448,128]{1,0:T(8,128)S(1)}, u32[]{:S(2)}, u32[]{:S(2)}) collective-permute-start(f32[448,128]{1,0:T(8,128)S(1)} %get-tuple-element.67), channel_id=1, source_target_pairs={{0,2},{1,3},{2,0},{3,1},{4,6},{5,7},{6,4},{7,5},{8,10},{9,11},{10,... | collective-permute-start | bytes 688136 | tf_op jit(solution)/shard_map/ppermute | solution.py:19
  8.5 9.4 %collective-permute-start.1 = (bf16[8,7296]{1,0:T(8,128)(2,1)S(1)}, bf16[8,7296]{1,0:T(8,128)(2,1)S(1)}, u32[]{:S(2)}, u32[]{:S(2)}) collective-permute-start(bf16[8,7296]{1,0:T(8,128)(2,1)S(1)} %get-tuple-element.53), channel_id=1, source_target_pairs={{0,4},{4,0},{8,12},{12,8},{1,5},{5,1},{9,13},{13,9},{2,6},{6,2},{1... | collective-permute-start | bytes 350216 | tf_op jit(solution)/shard_map/ppermute | solution.py:19
  9.8 19.7 %collective-permute-start.8 = (f32[448,128]{1,0:T(8,128)S(1)}, f32[448,128]{1,0:T(8,128)S(1)}, u32[]{:S(2)}, u32[]{:S(2)}) collective-permute-start(f32[448,128]{1,0:T(8,128)S(1)} %get-tuple-element.63), channel_id=1, source_target_pairs={{0,2},{1,3},{2,0},{3,1},{4,6},{5,7},{6,4},{7,5},{8,10},{9,11},{10,... | collective-permute-start | bytes 688136 | tf_op jit(solution)/shard_map/ppermute | solution.py:19
  10.0 20.1 %collective-permute-start.10 = (f32[448,128]{1,0:T(8,128)S(1)}, f32[448,128]{1,0:T(8,128)S(1)}, u32[]{:S(2)}, u32[]{:S(2)}) collective-permute-start(f32[448,128]{1,0:T(8,128)S(1)} %get-tuple-element.65), channel_id=1, source_target_pairs={{0,2},{1,3},{2,0},{3,1},{4,6},{5,7},{6,4},{7,5},{8,10},{9,11},{10,... | collective-permute-start | bytes 688136 | tf_op jit(solution)/shard_map/ppermute | solution.py:19
  14.2 15.9 %collective-permute-start.12 = (f32[448,128]{1,0:T(8,128)S(1)}, f32[448,128]{1,0:T(8,128)S(1)}, u32[]{:S(2)}, u32[]{:S(2)}) collective-permute-start(f32[448,128]{1,0:T(8,128)S(1)} %add.25), channel_id=1, source_target_pairs={{0,4},{4,0},{8,12},{12,8},{1,5},{5,1},{9,13},{13,9},{2,6},{6,2},{1... | collective-permute-start | bytes 688136 | tf_op jit(solution)/shard_map/ppermute | solution.py:19
  15.5 5.5 %collective-permute-start.2 = (bf16[8,7296]{1,0:T(8,128)(2,1)S(1)}, bf16[8,7296]{1,0:T(8,128)(2,1)S(1)}, u32[]{:S(2)}, u32[]{:S(2)}) collective-permute-start(bf16[8,7296]{1,0:T(8,128)(2,1)S(1)} %get-tuple-element.54), channel_id=1, source_target_pairs={{0,8},{4,12},{8,0},{12,4},{1,9},{5,13},{9,1},{13,5},{2,10},{6,14},... | collective-permute-start | bytes 350216 | tf_op jit(solution)/shard_map/ppermute | solution.py:19
  17.9 8.4 %collective-permute-start.3 = (bf16[8,7296]{1,0:T(8,128)(2,1)S(1)}, bf16[8,7296]{1,0:T(8,128)(2,1)S(1)}, u32[]{:S(2)}, u32[]{:S(2)}) collective-permute-start(bf16[8,7296]{1,0:T(8,128)(2,1)S(1)} %get-tuple-element.55), channel_id=1, source_target_pairs={{0,12},{4,8},{8,4},{12,0},{1,13},{5,9},{9,5},{13,1},{2,14},{6,10},... | collective-permute-start | bytes 350216 | tf_op jit(solution)/shard_map/ppermute | solution.py:19
  21.0 23.2 %collective-permute-start.7 = (f32[448,128]{1,0:T(8,128)S(1)}, f32[448,128]{1,0:T(8,128)S(1)}, u32[]{:S(2)}, u32[]{:S(2)}) collective-permute-start(f32[448,128]{1,0:T(8,128)S(1)} %get-tuple-element.61), channel_id=1, source_target_pairs={{0,2},{1,3},{2,0},{3,1},{4,6},{5,7},{6,4},{7,5},{8,10},{9,11},{10,... | collective-permute-start | bytes 688136 | tf_op jit(solution)/shard_map/ppermute | solution.py:19
  26.3 6.6 %collective-permute-start.4 = (bf16[32,2304]{1,0:T(8,128)(2,1)S(1)}, bf16[32,2304]{1,0:T(8,128)(2,1)S(1)}, u32[]{:S(2)}, u32[]{:S(2)}) collective-permute-start(bf16[32,2304]{1,0:T(8,128)(2,1)S(1)} %get-tuple-element.57), channel_id=1, source_target_pairs={{0,1},{1,0},{2,3},{3,2},{4,5},{5,4},{6,7},{7,6},{8,9},{9,8},{10,11... | collective-permute-start | bytes 442376 | tf_op jit(solution)/shard_map/ppermute | solution.py:19
  29.5 14.7 %collective-permute-start.9 = (f32[448,128]{1,0:T(8,128)S(1)}, f32[448,128]{1,0:T(8,128)S(1)}, u32[]{:S(2)}, u32[]{:S(2)}) collective-permute-start(f32[448,128]{1,0:T(8,128)S(1)} %add.22), channel_id=1, source_target_pairs={{0,4},{4,0},{8,12},{12,8},{1,5},{5,1},{9,13},{13,9},{2,6},{6,2},{1... | collective-permute-start | bytes 688136 | tf_op jit(solution)/shard_map/ppermute | solution.py:19
  30.2 14.0 %collective-permute-start.13 = (f32[448,128]{1,0:T(8,128)S(1)}, f32[448,128]{1,0:T(8,128)S(1)}, u32[]{:S(2)}, u32[]{:S(2)}) collective-permute-start(f32[448,128]{1,0:T(8,128)S(1)} %add_add_fusion), channel_id=1, source_target_pairs={{0,8},{4,12},{8,0},{12,4},{1,9},{5,13},{9,1},{13,5},{2,10},{6,14},... | collective-permute-start | bytes 688136 | tf_op jit(solution)/shard_map/ppermute | solution.py:19
  32.7 4.8 %collective-permute-start.5 = (bf16[32,2304]{1,0:T(8,128)(2,1)S(1)}, bf16[32,2304]{1,0:T(8,128)(2,1)S(1)}, u32[]{:S(2)}, u32[]{:S(2)}) collective-permute-start(bf16[32,2304]{1,0:T(8,128)(2,1)S(1)} %get-tuple-element.58), channel_id=1, source_target_pairs={{0,2},{1,3},{2,0},{3,1},{4,6},{5,7},{6,4},{7,5},{8,10},{9,11},{10,... | collective-permute-start | bytes 442376 | tf_op jit(solution)/shard_map/ppermute | solution.py:19
  33.0 8.8 %collective-permute-start.6 = (bf16[32,2304]{1,0:T(8,128)(2,1)S(1)}, bf16[32,2304]{1,0:T(8,128)(2,1)S(1)}, u32[]{:S(2)}, u32[]{:S(2)}) collective-permute-start(bf16[32,2304]{1,0:T(8,128)(2,1)S(1)} %get-tuple-element.59), channel_id=1, source_target_pairs={{0,3},{1,2},{2,1},{3,0},{4,7},{5,6},{6,5},{7,4},{8,11},{9,10},{10,... | collective-permute-start | bytes 442376 | tf_op jit(solution)/shard_map/ppermute | solution.py:19

commit v3 on v1

v3 whole, which is shorter than its diff:
```python
import functools

import jax
import jax.numpy as jnp
from jax import lax
from jax.experimental import pallas as pl
from jax.experimental.pallas import tpu as pltpu
from jax.sharding import PartitionSpec as P

BAND = 384
SBAND = 128
CAP = 8
LANES = 128
PAD = 16
VMEM_LIMIT = 16 * 1024 * 1024


def exchange(value, axis, distance):
    size = lax.axis_size(axis)
    return lax.ppermute(value, axis, [(i, i ^ distance) for i in range(size)])


def tie(value, after):
    return value if after is None else lax.optimization_barrier((value, after))[0]


def pass_on(value, distance):
    experts, peers = lax.axis_size("expert"), lax.axis_size("dp")
    pairs = [
        (e * peers + d, (e ^ (distance + d % 2)) * peers + d)
        for e in range(experts)
        for d in range(peers)
        if distance + d % 2
    ]
    return lax.ppermute(value, ("expert", "dp"), pairs)


def call(kernel, out_shape, *operands, flops, nbytes, **where):
    return pl.pallas_call(
        kernel,
        out_shape=out_shape,
        compiler_params=pltpu.CompilerParams(vmem_limit_bytes=VMEM_LIMIT),
        cost_estimate=pl.CostEstimate(flops=flops, bytes_accessed=nbytes, transcendentals=0),
        **where,
    )(*operands)


def parts_of(features):
    step = -(-features // (4 * LANES)) * LANES
    return [slice(b, min(b + step, features)) for b in range(0, features, step)]


def split_kernel(*refs, peers):
    in_refs, out_refs = refs[: -1 - peers // 2], refs[-1 - peers // 2 :]
    me = lax.axis_index("dp")
    features = in_refs[0].shape[1] - LANES
    width = features // peers

    def stacked(columns):
        return jnp.concatenate([ref[:, columns] for ref in in_refs], axis=0)

    def columns_of(k):
        return stacked(pl.ds(pl.multiple_of((me ^ k) * width, LANES), width))

    band = stacked(slice(0, BAND))
    flag = stacked(slice(features, features + LANES))
    for ref, pieces in zip(out_refs, [[0], [1]] + [[k, k + 1] for k in range(2, peers, 2)]):
        for i, k in enumerate(pieces):
            ref[:, i * width : (i + 1) * width] = columns_of(k)
        end = len(pieces) * width
        ref[:, end : end + BAND] = band
        ref[:, end + BAND :] = flag


def hessian_kernel(*refs, width):
    in_refs, out_ref = refs[:-1], refs[-1]
    step = out_ref.shape[1]
    begin = pl.program_id(0) * step

    def tail(ref, start, size):
        start = pl.multiple_of(ref.shape[1] - BAND - LANES + start, LANES)
        return ref[:, pl.ds(start, size)]

    rows = jnp.concatenate([ref[:, :width] for ref in in_refs], axis=0)
    band = jnp.concatenate([tail(ref, begin, step) for ref in in_refs], axis=0)
    count = sum(
        jnp.sum(tail(ref, BAND, LANES).astype(jnp.float32), axis=0, keepdims=True)[:, :1]
        for ref in in_refs
    )
    product = lax.dot_general(
        band, rows, (((0,), (0,)), ((), ())), preferred_element_type=jnp.float32
    )
    out_ref[0] = product * (2.0 / count)


def select(ids, expert):
    tokens = ids.shape[1]
    member = jnp.max((ids == expert).astype(jnp.float32), axis=0, keepdims=True)
    earlier = (
        lax.broadcasted_iota(jnp.int32, (tokens, tokens), 0)
        < lax.broadcasted_iota(jnp.int32, (tokens, tokens), 1)
    ).astype(jnp.bfloat16)
    rank = jnp.dot(member.astype(jnp.bfloat16), earlier, preferred_element_type=jnp.float32)
    slot = lax.broadcasted_iota(jnp.int32, (2 * CAP, tokens), 0).astype(jnp.float32)
    return jnp.where(slot == rank, member, 0.0)


def fetch_kernel(ids_ref, tokens_ref, held_ids_ref, held_ref, sems):
    copies = [
        pltpu.make_async_copy(ids_ref, held_ids_ref, sems.at[0]),
        pltpu.make_async_copy(tokens_ref, held_ref, sems.at[1]),
    ]
    for copy in copies:
        copy.start()
    for copy in copies:
        copy.wait()


def pair_kernel(
    ids_ref, other_ids_ref, mine_ref, other_ref, *out_refs, experts, peers, wanted, aligned
):
    out_refs, row_refs = out_refs[: -experts // 2], out_refs[-experts // 2 :]
    features = mine_ref.shape[1]
    e = lax.axis_index("expert")
    d = lax.axis_index("dp")

    def both(columns):
        return jnp.concatenate([mine_ref[:, columns], other_ref[:, columns]], axis=0)

    lead = both(slice(0, SBAND))

    def product(columns):
        return lax.dot_general(
            both(columns), lead, (((0,), (0,)), ((), ())), preferred_element_type=jnp.float32
        )

    if aligned:
        share = features // (experts * peers)
        half = LANES // 2
        window = share + half * (share // half % 2)
        for out_ref, pairs in zip(out_refs, wanted):
            for i, (m, k) in enumerate(pairs):
                start = ((e ^ m) * peers + (d ^ k)) * (share // half)
                odd = start % 2
                found = product(pl.ds(pl.multiple_of((start - odd) * half, LANES), window))
                if window > share:
                    found = jnp.where(odd == 1, found[half:], found[:share])
                out_ref[i * share : (i + 1) * share] = found
            filled = len(pairs) * share
            if out_ref.shape[0] > filled:
                out_ref[filled:] = jnp.zeros_like(out_ref[filled:])
    else:
        for part in parts_of(features):
            out_refs[0][part] = product(part)

    ids = jnp.concatenate([ids_ref[...], other_ids_ref[...]], axis=1)
    picks = jnp.concatenate(
        [select(ids, e ^ (k + d % 2)) for k in range(0, experts, 2)], axis=0
    )
    flags = jnp.broadcast_to(jnp.sum(picks, axis=1, keepdims=True), (picks.shape[0], LANES))
    picks = picks.astype(jnp.bfloat16)
    for part in parts_of(features):
        chosen = jnp.dot(picks, both(part), preferred_element_type=jnp.float32)
        for i, ref in enumerate(row_refs):
            ref[:, part] = chosen[2 * CAP * i : 2 * CAP * (i + 1)].astype(jnp.bfloat16)
    for i, ref in enumerate(row_refs):
        ref[:, features:] = flags[2 * CAP * i : 2 * CAP * (i + 1)].astype(jnp.bfloat16)


def on_device(tokens, expert_ids):
    tok_rows, features = tokens.shape
    experts = lax.axis_size("expert")
    peers = lax.axis_size("dp")
    width = features // peers
    share = features // (experts * peers)
    anywhere = pl.BlockSpec(memory_space=pl.ANY)
    inside = pl.BlockSpec(memory_space=pltpu.VMEM)

    ids = expert_ids.T
    other = exchange(tokens, "dp", 1)
    other_ids = exchange(ids, "dp", 1)
    ids, mine = call(
        fetch_kernel,
        [
            jax.ShapeDtypeStruct(ids.shape, ids.dtype),
            jax.ShapeDtypeStruct(tokens.shape, tokens.dtype),
        ],
        ids,
        tokens,
        flops=0,
        nbytes=4 * tok_rows * features,
        in_specs=[anywhere, anywhere],
        out_specs=[inside, inside],
        scratch_shapes=[pltpu.SemaphoreType.DMA((2,))],
    )
    ids, mine, other, other_ids = lax.optimization_barrier((ids, mine, other, other_ids))

    even = range(0, peers, 2)
    far = range(2, experts, 2)
    groups = [[m + 1 for m in far], [*far], [1], [0]]
    wanted = [[(m, k) for m in group] for group in groups for k in even]
    aligned = share % (LANES // 2) == 0
    sizes = [len(pairs) * share for pairs in wanted]
    for i in range(1, peers // 2):
        sizes[i] += PAD
    found = call(
        functools.partial(
            pair_kernel, experts=experts, peers=peers, wanted=wanted, aligned=aligned
        ),
        [
            jax.ShapeDtypeStruct((size, SBAND), jnp.float32)
            for size in (sizes if aligned else [features])
        ]
        + [jax.ShapeDtypeStruct((2 * CAP, features + LANES), jnp.bfloat16)] * (experts // 2),
        ids,
        other_ids,
        mine,
        other,
        flops=4 * tok_rows * features * (SBAND + experts * CAP),
        nbytes=4 * tok_rows * features + 4 * features * SBAND,
    )
    blocks, outgoing = found[: -experts // 2], found[-experts // 2 :]
    if not aligned:
        e, d = lax.axis_index("expert"), lax.axis_index("dp")
        blocks = [
            jnp.concatenate(
                [
                    lax.dynamic_slice_in_dim(
                        blocks[0], ((e ^ m) * peers + (d ^ k)) * share, share, axis=0
                    )
                    for m, k in pairs
                ],
                axis=0,
            )
            for pairs in wanted
        ]
    def over_dp(i, after=None):
        own, *sent = blocks[i * (peers // 2) : (i + 1) * (peers // 2)]
        got = [exchange(tie(x, after), "dp", 2 * k + 2) for k, x in enumerate(sent)]
        return sum([x[: own.shape[0]] for x in got], own)

    near = exchange(over_dp(0), "expert", 1)
    paired = over_dp(1) + near
    beside_sum = exchange(over_dp(2), "expert", 1)
    own = over_dp(3, near) + beside_sum

    arrived = [pass_on(outgoing[k], 2 * k) for k in range(experts // 2)]
    arrived[0] = jnp.where(lax.axis_index("dp") % 2 == 0, outgoing[0], arrived[0])

    rows = experts * CAP
    tail = BAND + LANES
    mine, give, *packed = call(
        functools.partial(split_kernel, peers=peers),
        [jax.ShapeDtypeStruct((rows, width + tail), jnp.bfloat16)] * 2
        + [jax.ShapeDtypeStruct((rows, 2 * width + tail), jnp.bfloat16)] * (peers // 2 - 1),
        *arrived,
        flops=0,
        nbytes=4 * rows * features,
    )
    across = [exchange(x, "dp", 2 * k + 2) for k, x in enumerate(packed)]
    beside = exchange(jnp.concatenate([give] + [x[:, width:] for x in across]), "dp", 1)
    gathered = [mine, *across, beside]
    steps = BAND // LANES
    routed_out = call(
        functools.partial(hessian_kernel, width=width),
        jax.ShapeDtypeStruct((1, BAND, width), jnp.float32),
        *gathered,
        flops=2 * BAND * width * rows * peers,
        nbytes=4 * BAND * width,
        grid_spec=pl.GridSpec(
            grid=(steps,),
            in_specs=[pl.BlockSpec(x.shape, lambda i: (0, 0)) for x in gathered],
            out_specs=pl.BlockSpec((1, BAND // steps, width), lambda i: (0, i, 0)),
        ),
    )
    paired = tie(paired, packed)
    others = [
        exchange(paired[i * share : (i + 1) * share], "expert", m) for i, m in enumerate(far)
    ]
    summed = sum(others, lax.optimization_barrier(own))
    shared_out = summed * (2.0 / (tok_rows * experts * peers))
    return routed_out, shared_out


def solution(mesh):
    in_specs = (P(("groups", "expert", "dp"), None), P(("groups", "expert", "dp"), None))
    out_specs = (P(("groups", "expert"), None, "dp"), P(("groups", "expert", "dp"), None))
    return jax.shard_map(
        on_device, mesh=mesh, in_specs=in_specs, out_specs=out_specs, check_vma=False
    )
```

time: 62.8 us -> 42.2 us (0.67)
  the two profiles are of different devices: /device:TPU:1 before, /device:TPU:24 now
where the time goes in v3:
time: 42.2 us; the launch traced here: 42 us
  waiting for transfers between devices  24.9 us (59%)
  starting transfers between devices  9.11 us (22%)
  Pallas kernels  4.16 us (10%)
  local copies, waits for them, and re-layouts  2.2 us (5%)
  other arithmetic  0.92 us (2%)
  between operations  0.73 us (2%)
    ppermute x11, waiting for transfers between devices, exchange(): return lax.ppermute(value, axis, [(i, i ^ distance) for i in range(size)])  17 us
    ppermute x11, starting transfers between devices, exchange(): return lax.ppermute(value, axis, [(i, i ^ distance) for i in range(size)])  8.02 us
    ppermute x2, waiting for transfers between devices, pass_on(): return lax.ppermute(value, ('expert', 'dp'), pairs)  7.91 us
    pallas_call x4, Pallas kernels, call(): pl.pallas_call(kernel, out_shape=out_shape, compiler_params=pltpu.Compile...  4.16 us
    unnamed x4, local copies, waits for them, and re-layouts  2.19 us
    ppermute x2, starting transfers between devices, pass_on(): return lax.ppermute(value, ('expert', 'dp'), pairs)  1.09 us
  transfers between devices with their start and end apart: 13, of which 8 were waited for; matrix products, arithmetic and copies ran while one was open for 2% of the time, Pallas kernels for 0%

profile of v3, /device:TPU:24, one launch (start us, length us, event | category | flops | bytes accessed | tf_op | source)
XLA Modules:
  0.0 42.0 jit_solution(11097597370123139663)
XLA Ops:
  0.7 0.5 %collective-permute-start.1 = (s32[8,128]{1,0:T(8,128)}, s32[8,128]{1,0:T(8,128)S(1)}, u32[]{:S(2)}, u32[]{:S(2)}) collective-permute-start(s32[8,128]{1,0:T(8,128)} %bitcast.1), channel_id=1, source_target_pairs={{0,1},{1,0},{2,3},{3,2},{4,5},{5,4},{6,7},{7,6},{8,9},{9,8},{10,11... | collective-permute-start | bytes 12296 | tf_op jit(solution)/shard_map/ppermute | solution.py:20
  1.2 1.5 %copy-done = bf16[128,7168]{1,0:T(8,128)(2,1)S(1)} copy-done((bf16[128,7168]{1,0:T(8,128)(2,1)S(1)}, bf16[128,7168]{1,0:T(8,128)(2,1)}, u32[]{:S(2)}) %copy-start) | copy-done | bytes 1835032
  2.7 0.7 %copy-done.1 = s32[128,8]{0,1:T(8,128)S(1)} copy-done((s32[128,8]{0,1:T(8,128)S(1)}, s32[128,8]{0,1:T(8,128)}, u32[]{:S(2)}) %copy-start.1) | copy-done | bytes 4120
  3.4 0.1 shard_map.41
  3.5 1.1 %collective-permute-done.1.other_ids_ref = s32[8,128]{1,0:T(8,128)S(1)} collective-permute-done((s32[8,128]{1,0:T(8,128)}, s32[8,128]{1,0:T(8,128)S(1)}, u32[]{:S(2)}, u32[]{:S(2)}) %collective-permute-start.1) | collective-permute-done | bytes 4128 | tf_op jit(solution)/shard_map/ppermute | solution.py:20
  4.7 1.5 %shard_map.42 = (f32[448,128]{1,0:T(8,128)S(1)}, f32[464,128]{1,0:T(8,128)S(1)}, f32[448,128]{1,0:T(8,128)S(1)}, f32[448,128]{1,0:T(8,128)S(1)}, f32[448,128]{1,...) custom-call(s32[8,128]{1,0:T(8,128)S(1)} %get-tuple-element.25.ids_r, ...), custom_call_target="tpu_custom_call" | custom-call | flops 587202560 | bytes 7340032 | tf_op jit(solution)/shard_map/pallas_call | solution.py:39
  6.2 1.6 %collective-permute-start.6 = (f32[464,128]{1,0:T(8,128)S(1)}, f32[464,128]{1,0:T(8,128)S(1)}, u32[]{:S(2)}, u32[]{:S(2)}) collective-permute-start(f32[464,128]{1,0:T(8,128)S(1)} %get-tuple-element.37), channel_id=1, source_target_pairs={{0,2},{1,3},{2,0},{3,1},{4,6},{5,7},{6,4},{7,5},{8,10},{9,11},{10,... | collective-permute-start | bytes 712712 | tf_op jit(solution)/shard_map/ppermute | solution.py:20
  7.7 0.5 %collective-permute-start.11 = (f32[448,128]{1,0:T(8,128)S(1)}, f32[448,128]{1,0:T(8,128)S(1)}, u32[]{:S(2)}, u32[]{:S(2)}) collective-permute-start(f32[448,128]{1,0:T(8,128)S(1)} %get-tuple-element.42), channel_id=1, source_target_pairs={{0,2},{1,3},{2,0},{3,1},{4,6},{5,7},{6,4},{7,5},{8,10},{9,11},{10,... | collective-permute-start | bytes 688136 | tf_op jit(solution)/shard_map/ppermute | solution.py:20
  8.2 0.7 %collective-permute-start.2 = (bf16[16,7296]{1,0:T(8,128)(2,1)S(1)}, bf16[16,7296]{1,0:T(8,128)(2,1)S(1)}, u32[]{:S(2)}, u32[]{:S(2)}) collective-permute-start(bf16[16,7296]{1,0:T(8,128)(2,1)S(1)} %get-tuple-element.29), channel_id=1, source_target_pairs={{1,5},{3,7},{5,1},{7,3},{9,13},{11,15},{13,9},{15,11},{17,21},{19,... | collective-permute-start | bytes 700424 | tf_op jit(solution)/shard_map/ppermute | solution.py:35
  8.9 0.4 %collective-permute-start.3 = (bf16[16,7296]{1,0:T(8,128)(2,1)S(1)}, bf16[16,7296]{1,0:T(8,128)(2,1)S(1)}, u32[]{:S(2)}, u32[]{:S(2)}) collective-permute-start(bf16[16,7296]{1,0:T(8,128)(2,1)S(1)} %get-tuple-element.30), channel_id=1, source_target_pairs={{0,8},{1,13},{2,10},{3,15},{4,12},{5,9},{6,14},{7,11},{8,0},{9,5},... | collective-permute-start | bytes 700424 | tf_op jit(solution)/shard_map/ppermute | solution.py:35
  9.3 1.5 %collective-permute-start.9 = (f32[448,128]{1,0:T(8,128)S(1)}, f32[448,128]{1,0:T(8,128)S(1)}, u32[]{:S(2)}, u32[]{:S(2)}) collective-permute-start(f32[448,128]{1,0:T(8,128)S(1)} %get-tuple-element.40), channel_id=1, source_target_pairs={{0,2},{1,3},{2,0},{3,1},{4,6},{5,7},{6,4},{7,5},{8,10},{9,11},{10,... | collective-permute-start | bytes 688136 | tf_op jit(solution)/shard_map/ppermute | solution.py:20
  10.8 4.0 %collective-permute-done.6 = f32[464,128]{1,0:T(8,128)S(1)} collective-permute-done((f32[464,128]{1,0:T(8,128)S(1)}, f32[464,128]{1,0:T(8,128)S(1)}, u32[]{:S(2)}, u32[]{:S(2)}) %collective-permute-start.6) | collective-permute-done | bytes 237600 | tf_op jit(solution)/shard_map/ppermute | solution.py:20
  14.9 0.5 %collective-permute-start.7 = (f32[448,128]{1,0:T(8,128)S(1)}, f32[448,128]{1,0:T(8,128)S(1)}, u32[]{:S(2)}, u32[]{:S(2)}) collective-permute-start(f32[448,128]{1,0:T(8,128)S(1)} %slice_add_fusion), channel_id=1, source_target_pairs={{0,4},{4,0},{8,12},{12,8},{1,5},{5,1},{9,13},{13,9},{2,6},{6,2},{1... | collective-permute-start | bytes 688136 | tf_op jit(solution)/shard_map/ppermute | solution.py:20
  15.4 7.9 %collective-permute-done.3.refs_1_ = bf16[16,7296]{1,0:T(8,128)(2,1)S(1)} collective-permute-done((bf16[16,7296]{1,0:T(8,128)(2,1)S(1)}, bf16[16,7296]{1,0:T(8,128)(2,1)S(1)}, u32[]{:S(2)}, u32[]{:S(2)}) %collective-permute-start.3) | collective-permute-done | bytes 233504 | tf_op jit(solution)/shard_map/ppermute | solution.py:35
  23.4 1.6 %collective-permute-start.4 = (bf16[32,4096]{1,0:T(8,128)(2,1)S(1)}, bf16[32,4096]{1,0:T(8,128)(2,1)S(1)}, u32[]{:S(2)}, u32[]{:S(2)}) collective-permute-start(bf16[32,4096]{1,0:T(8,128)(2,1)S(1)} %get-tuple-element.32), channel_id=1, source_target_pairs={{0,2},{1,3},{2,0},{3,1},{4,6},{5,7},{6,4},{7,5},{8,10},{9,11},{10,... | collective-permute-start | bytes 786440 | tf_op jit(solution)/shard_map/ppermute | solution.py:20
  25.0 0.1 collective-permute-start.10
  25.1 0.1 collective-permute-done.7
  25.3 1.6 %collective-permute-start.8 = (f32[448,128]{1,0:T(8,128)S(1)}, f32[448,128]{1,0:T(8,128)S(1)}, u32[]{:S(2)}, u32[]{:S(2)}) collective-permute-start(f32[448,128]{1,0:T(8,128)S(1)} %get-tuple-element.38), channel_id=1, source_target_pairs={{0,2},{1,3},{2,0},{3,1},{4,6},{5,7},{6,4},{7,5},{8,10},{9,11},{10,... | collective-permute-start | bytes 688136 | tf_op jit(solution)/shard_map/ppermute | solution.py:20
  26.9 4.7 %collective-permute-done.4.refs_1_ = bf16[32,4096]{1,0:T(8,128)(2,1)S(1)} collective-permute-done((bf16[32,4096]{1,0:T(8,128)(2,1)S(1)}, bf16[32,4096]{1,0:T(8,128)(2,1)S(1)}, u32[]{:S(2)}, u32[]{:S(2)}) %collective-permute-start.4) | collective-permute-done | bytes 262176 | tf_op jit(solution)/shard_map/ppermute | solution.py:20
  31.7 2.3 %collective-permute-done.10 = f32[448,128]{1,0:T(8,128)S(1)} collective-permute-done((f32[448,128]{1,0:T(8,128)S(1)}, f32[448,128]{1,0:T(8,128)S(1)}, u32[]{:S(2)}, u32[]{:S(2)}) %collective-permute-start.10) | collective-permute-done | bytes 229408 | tf_op jit(solution)/shard_map/ppermute | solution.py:20
  34.0 0.7 %collective-permute-done.8 = f32[448,128]{1,0:T(8,128)S(1)} collective-permute-done((f32[448,128]{1,0:T(8,128)S(1)}, f32[448,128]{1,0:T(8,128)S(1)}, u32[]{:S(2)}, u32[]{:S(2)}) %collective-permute-start.8) | collective-permute-done | bytes 229408 | tf_op jit(solution)/shard_map/ppermute | solution.py:20
  34.8 4.0 %collective-permute-done.12 = f32[448,128]{1,0:T(8,128)S(1)} collective-permute-done((f32[448,128]{1,0:T(8,128)S(1)}, f32[448,128]{1,0:T(8,128)S(1)}, u32[]{:S(2)}, u32[]{:S(2)}) %collective-permute-start.12) | collective-permute-done | bytes 229408 | tf_op jit(solution)/shard_map/ppermute | solution.py:20
  38.8 0.7 %add_multiply_fusion = f32[448,128]{1,0:T(8,128)} fusion(f32[448,128]{1,0:T(8,128)S(1)} %add_add_fusion.1, f32[448,128]{1,0:T(8,128)S(1)} %collective-permute-done.12), kind=kLoop, calls=%fused_computation.3 | loop fusion | flops 114688 | bytes 688128 | tf_op jit(solution)/shard_map/mul | solution.py:281
  39.5 2.5 %shard_map.44 = f32[1,384,1792]{2,1,0:T(8,128)} custom-call(bf16[32,2304]{1,0:T(8,128)(2,1)S(1)} %get-tuple-element.31.refs_0_, bf16[32,4096]{1,0:T(8,128)(2,1)S(1)} %collective-permute-done.4.refs_1_, bf16[64,2304]{1,0:T(8,128)(2,1)S(1)} %collective-permute-done.5.refs_2_), custom_call_target="tpu_custom_call" | custom-call | flops 176160768 | bytes 2752512 | tf_op jit(solution)/shard_map/pallas_call | solution.py:39
  (18 shorter events, 0.5 us)
Async XLA Ops:
  0.6 4.1 %collective-permute-start = (bf16[128,7168]{1,0:T(8,128)(2,1)}, bf16[128,7168]{1,0:T(8,128)(2,1)S(1)}, u32[]{:S(2)}, u32[]{:S(2)}) collective-permute-start(bf16[128,7168]{1,0:T(8,128)(2,1)} %tokens_ref.1), channel_id=1, source_target_pairs={{0,1},{1,0},{2,3},{3,2},{4,5},{5,4},{6,7},{7,6},{8,9},{9,8},{10,11... | collective-permute-start | bytes 5505032 | tf_op jit(solution)/shard_map/ppermute | solution.py:20
  0.7 4.0 %collective-permute-start.1 = (s32[8,128]{1,0:T(8,128)}, s32[8,128]{1,0:T(8,128)S(1)}, u32[]{:S(2)}, u32[]{:S(2)}) collective-permute-start(s32[8,128]{1,0:T(8,128)} %bitcast.1), channel_id=1, source_target_pairs={{0,1},{1,0},{2,3},{3,2},{4,5},{5,4},{6,7},{7,6},{8,9},{9,8},{10,11... | collective-permute-start | bytes 12296 | tf_op jit(solution)/shard_map/ppermute | solution.py:20
  1.2 1.5 %copy-start = (bf16[128,7168]{1,0:T(8,128)(2,1)S(1)}, bf16[128,7168]{1,0:T(8,128)(2,1)}, u32[]{:S(2)}) copy-start(bf16[128,7168]{1,0:T(8,128)(2,1)} %tokens_ref.1) | copy-start | bytes 5505028
  2.7 0.7 %copy-start.1 = (s32[128,8]{0,1:T(8,128)S(1)}, s32[128,8]{0,1:T(8,128)}, u32[]{:S(2)}) copy-start(s32[128,8]{0,1:T(8,128)} %param.3) | copy-start | bytes 12292
  6.2 8.7 %collective-permute-start.6 = (f32[464,128]{1,0:T(8,128)S(1)}, f32[464,128]{1,0:T(8,128)S(1)}, u32[]{:S(2)}, u32[]{:S(2)}) collective-permute-start(f32[464,128]{1,0:T(8,128)S(1)} %get-tuple-element.37), channel_id=1, source_target_pairs={{0,2},{1,3},{2,0},{3,1},{4,6},{5,7},{6,4},{7,5},{8,10},{9,11},{10,... | collective-permute-start | bytes 712712 | tf_op jit(solution)/shard_map/ppermute | solution.py:20
  7.7 17.4 %collective-permute-start.11 = (f32[448,128]{1,0:T(8,128)S(1)}, f32[448,128]{1,0:T(8,128)S(1)}, u32[]{:S(2)}, u32[]{:S(2)}) collective-permute-start(f32[448,128]{1,0:T(8,128)S(1)} %get-tuple-element.42), channel_id=1, source_target_pairs={{0,2},{1,3},{2,0},{3,1},{4,6},{5,7},{6,4},{7,5},{8,10},{9,11},{10,... | collective-permute-start | bytes 688136 | tf_op jit(solution)/shard_map/ppermute | solution.py:20
  8.2 7.2 %collective-permute-start.2 = (bf16[16,7296]{1,0:T(8,128)(2,1)S(1)}, bf16[16,7296]{1,0:T(8,128)(2,1)S(1)}, u32[]{:S(2)}, u32[]{:S(2)}) collective-permute-start(bf16[16,7296]{1,0:T(8,128)(2,1)S(1)} %get-tuple-element.29), channel_id=1, source_target_pairs={{1,5},{3,7},{5,1},{7,3},{9,13},{11,15},{13,9},{15,11},{17,21},{19,... | collective-permute-start | bytes 700424 | tf_op jit(solution)/shard_map/ppermute | solution.py:35
  8.9 14.4 %collective-permute-start.3 = (bf16[16,7296]{1,0:T(8,128)(2,1)S(1)}, bf16[16,7296]{1,0:T(8,128)(2,1)S(1)}, u32[]{:S(2)}, u32[]{:S(2)}) collective-permute-start(bf16[16,7296]{1,0:T(8,128)(2,1)S(1)} %get-tuple-element.30), channel_id=1, source_target_pairs={{0,8},{1,13},{2,10},{3,15},{4,12},{5,9},{6,14},{7,11},{8,0},{9,5},... | collective-permute-start | bytes 700424 | tf_op jit(solution)/shard_map/ppermute | solution.py:35
  9.3 15.7 %collective-permute-start.9 = (f32[448,128]{1,0:T(8,128)S(1)}, f32[448,128]{1,0:T(8,128)S(1)}, u32[]{:S(2)}, u32[]{:S(2)}) collective-permute-start(f32[448,128]{1,0:T(8,128)S(1)} %get-tuple-element.40), channel_id=1, source_target_pairs={{0,2},{1,3},{2,0},{3,1},{4,6},{5,7},{6,4},{7,5},{8,10},{9,11},{10,... | collective-permute-start | bytes 688136 | tf_op jit(solution)/shard_map/ppermute | solution.py:20
  14.9 10.3 %collective-permute-start.7 = (f32[448,128]{1,0:T(8,128)S(1)}, f32[448,128]{1,0:T(8,128)S(1)}, u32[]{:S(2)}, u32[]{:S(2)}) collective-permute-start(f32[448,128]{1,0:T(8,128)S(1)} %slice_add_fusion), channel_id=1, source_target_pairs={{0,4},{4,0},{8,12},{12,8},{1,5},{5,1},{9,13},{13,9},{2,6},{6,2},{1... | collective-permute-start | bytes 688136 | tf_op jit(solution)/shard_map/ppermute | solution.py:20
  23.4 8.2 %collective-permute-start.4 = (bf16[32,4096]{1,0:T(8,128)(2,1)S(1)}, bf16[32,4096]{1,0:T(8,128)(2,1)S(1)}, u32[]{:S(2)}, u32[]{:S(2)}) collective-permute-start(bf16[32,4096]{1,0:T(8,128)(2,1)S(1)} %get-tuple-element.32), channel_id=1, source_target_pairs={{0,2},{1,3},{2,0},{3,1},{4,6},{5,7},{6,4},{7,5},{8,10},{9,11},{10,... | collective-permute-start | bytes 786440 | tf_op jit(solution)/shard_map/ppermute | solution.py:20
  25.0 9.0 %collective-permute-start.10 = (f32[448,128]{1,0:T(8,128)S(1)}, f32[448,128]{1,0:T(8,128)S(1)}, u32[]{:S(2)}, u32[]{:S(2)}) collective-permute-start(f32[448,128]{1,0:T(8,128)S(1)} %add.28), channel_id=1, source_target_pairs={{0,4},{4,0},{8,12},{12,8},{1,5},{5,1},{9,13},{13,9},{2,6},{6,2},{1... | collective-permute-start | bytes 688136 | tf_op jit(solution)/shard_map/ppermute | solution.py:20
  25.3 13.5 %collective-permute-start.12 = (f32[448,128]{1,0:T(8,128)S(1)}, f32[448,128]{1,0:T(8,128)S(1)}, u32[]{:S(2)}, u32[]{:S(2)}) collective-permute-start(f32[448,128]{1,0:T(8,128)S(1)} %add_add_fusion), channel_id=1, source_target_pairs={{0,8},{4,12},{8,0},{12,4},{1,9},{5,13},{9,1},{13,5},{2,10},{6,14},... | collective-permute-start | bytes 688136 | tf_op jit(solution)/shard_map/ppermute | solution.py:20
  25.3 9.4 %collective-permute-start.8 = (f32[448,128]{1,0:T(8,128)S(1)}, f32[448,128]{1,0:T(8,128)S(1)}, u32[]{:S(2)}, u32[]{:S(2)}) collective-permute-start(f32[448,128]{1,0:T(8,128)S(1)} %get-tuple-element.38), channel_id=1, source_target_pairs={{0,2},{1,3},{2,0},{3,1},{4,6},{5,7},{6,4},{7,5},{8,10},{9,11},{10,... | collective-permute-start | bytes 688136 | tf_op jit(solution)/shard_map/ppermute | solution.py:20
  31.6 7.8 %collective-permute-start.5 = (bf16[64,2304]{1,0:T(8,128)(2,1)S(1)}, bf16[64,2304]{1,0:T(8,128)(2,1)S(1)}, u32[]{:S(2)}, u32[]{:S(2)}) collective-permute-start(bf16[64,2304]{1,0:T(8,128)(2,1)S(1)} %pad_maximum_fusion), channel_id=1, source_target_pairs={{0,1},{1,0},{2,3},{3,2},{4,5},{5,4},{6,7},{7,6},{8,9},{9,8},{10,11... | collective-permute-start | bytes 884744 | tf_op jit(solution)/shard_map/ppermute | solution.py:20

commit v4 on v3

--- a/solution.py
+++ b/solution.py
@@ -72,25 +72,34 @@
         ref[:, end + BAND :] = flag
 
 
-def hessian_kernel(*refs, width):
-    in_refs, out_ref = refs[:-1], refs[-1]
-    step = out_ref.shape[1]
-    begin = pl.program_id(0) * step
+def hessian_kernel(*refs):
+    row_refs, (routed_ref, routed, sems) = refs[:-3], refs[-3:]
+    _, band_size, width = routed_ref.shape
+    copies = []
+
+    def send(source, target):
+        copies.append(pltpu.make_async_copy(source, target, sems.at[len(copies)]))
+        copies[-1].start()
 
     def tail(ref, start, size):
-        start = pl.multiple_of(ref.shape[1] - BAND - LANES + start, LANES)
-        return ref[:, pl.ds(start, size)]
-
-    rows = jnp.concatenate([ref[:, :width] for ref in in_refs], axis=0)
-    band = jnp.concatenate([tail(ref, begin, step) for ref in in_refs], axis=0)
+        start += ref.shape[1] - BAND - LANES
+        return ref[:, start : start + size]
+
+    rows = jnp.concatenate([ref[:, :width] for ref in row_refs], axis=0)
+    band = jnp.concatenate([tail(ref, 0, BAND) for ref in row_refs], axis=0)
     count = sum(
         jnp.sum(tail(ref, BAND, LANES).astype(jnp.float32), axis=0, keepdims=True)[:, :1]
-        for ref in in_refs
-    )
-    product = lax.dot_general(
-        band, rows, (((0,), (0,)), ((), ())), preferred_element_type=jnp.float32
-    )
-    out_ref[0] = product * (2.0 / count)
+        for ref in row_refs
+    )
+    for begin in range(0, band_size, LANES):
+        part = slice(begin, begin + LANES)
+        product = lax.dot_general(
+            band[:, part], rows, (((0,), (0,)), ((), ())), preferred_element_type=jnp.float32
+        )
+        routed[part] = product * (2.0 / count)
+        send(routed.at[part], routed_ref.at[0, part])
+    for copy in copies:
+        copy.wait()
 
 
 def select(ids, expert):
@@ -239,8 +248,9 @@
         got = [exchange(tie(x, after), "dp", 2 * k + 2) for k, x in enumerate(sent)]
         return sum([x[: own.shape[0]] for x in got], own)
 
-    near = exchange(over_dp(0), "expert", 1)
-    paired = over_dp(1) + near
+    odd = over_dp(0)
+    near = exchange(odd, "expert", 1)
+    paired = over_dp(1, odd) + near
     beside_sum = exchange(over_dp(2), "expert", 1)
     own = over_dp(3, near) + beside_sum
 
@@ -260,18 +270,18 @@
     across = [exchange(x, "dp", 2 * k + 2) for k, x in enumerate(packed)]
     beside = exchange(jnp.concatenate([give] + [x[:, width:] for x in across]), "dp", 1)
     gathered = [mine, *across, beside]
-    steps = BAND // LANES
     routed_out = call(
-        functools.partial(hessian_kernel, width=width),
+        hessian_kernel,
         jax.ShapeDtypeStruct((1, BAND, width), jnp.float32),
         *gathered,
         flops=2 * BAND * width * rows * peers,
         nbytes=4 * BAND * width,
-        grid_spec=pl.GridSpec(
-            grid=(steps,),
-            in_specs=[pl.BlockSpec(x.shape, lambda i: (0, 0)) for x in gathered],
-            out_specs=pl.BlockSpec((1, BAND // steps, width), lambda i: (0, i, 0)),
-        ),
+        in_specs=[inside] * len(gathered),
+        out_specs=anywhere,
+        scratch_shapes=[
+            pltpu.VMEM((BAND, width), jnp.float32),
+            pltpu.SemaphoreType.DMA((BAND // LANES,)),
+        ],
     )
     paired = tie(paired, packed)
     others = [

time: 42.2 us -> 40.3 us (0.955)
  starting transfers between devices: 9.11 us -> 7.92 us
  Pallas kernels: 4.16 us -> 3.54 us
    ppermute x2, waiting for transfers between devices: 7.91 us -> 5.72 us  [pass_on(): return lax.ppermute(value, ('expert', 'dp'), pairs)]
    ppermute x11, waiting for transfers between devices: 17 us -> 19.1 us  [exchange(): return lax.ppermute(value, axis, [(i, i ^ distance) for i in range(size)])]
    ppermute x11, starting transfers between devices: 8.02 us -> 6.85 us  [exchange(): return lax.ppermute(value, axis, [(i, i ^ distance) for i in range(size)])]
    pallas_call x4, Pallas kernels: 4.16 us -> 3.54 us  [call(): pl.pallas_call(kernel, out_shape=out_shape, compiler_params=pltpu.Compile...]
  transfers between devices with their start and end apart: 13 -> 13, of which waited for: 8 -> 9; matrix products, arithmetic and copies ran while one was open for 2% -> 2% of each run, Pallas kernels for 0% -> 0%
where the time goes in v4:
time: 40.3 us; the launch traced here: 40.1 us
  waiting for transfers between devices  24.8 us (62%)
  starting transfers between devices  7.92 us (20%)
  Pallas kernels  3.54 us (9%)
  local copies, waits for them, and re-layouts  2.2 us (5%)
  other arithmetic  0.91 us (2%)
  between operations  0.72 us (2%)
    ppermute x11, waiting for transfers between devices, exchange(): return lax.ppermute(value, axis, [(i, i ^ distance) for i in range(size)])  19.1 us
    ppermute x11, starting transfers between devices, exchange(): return lax.ppermute(value, axis, [(i, i ^ distance) for i in range(size)])  6.85 us
    ppermute x2, waiting for transfers between devices, pass_on(): return lax.ppermute(value, ('expert', 'dp'), pairs)  5.72 us
    pallas_call x4, Pallas kernels, call(): pl.pallas_call(kernel, out_shape=out_shape, compiler_params=pltpu.Compile...  3.54 us
    unnamed x4, local copies, waits for them, and re-layouts  2.19 us
    ppermute x2, starting transfers between devices, pass_on(): return lax.ppermute(value, ('expert', 'dp'), pairs)  1.07 us
  transfers between devices with their start and end apart: 13, of which 9 were waited for; matrix products, arithmetic and copies ran while one was open for 2% of the time, Pallas kernels for 0%

profile of v4, /device:TPU:24, one launch (start us, length us, event | category | flops | bytes accessed | tf_op | source)
XLA Modules:
  0.0 40.1 jit_solution(4648382282784375330)
XLA Ops:
  0.7 0.5 %collective-permute-start.1 = (s32[8,128]{1,0:T(8,128)}, s32[8,128]{1,0:T(8,128)S(1)}, u32[]{:S(2)}, u32[]{:S(2)}) collective-permute-start(s32[8,128]{1,0:T(8,128)} %bitcast.1), channel_id=1, source_target_pairs={{0,1},{1,0},{2,3},{3,2},{4,5},{5,4},{6,7},{7,6},{8,9},{9,8},{10,11... | collective-permute-start | bytes 12296 | tf_op jit(solution)/shard_map/ppermute | solution.py:20
  1.2 1.5 %copy-done = bf16[128,7168]{1,0:T(8,128)(2,1)S(1)} copy-done((bf16[128,7168]{1,0:T(8,128)(2,1)S(1)}, bf16[128,7168]{1,0:T(8,128)(2,1)}, u32[]{:S(2)}) %copy-start) | copy-done | bytes 1835032
  2.7 0.7 %copy-done.1 = s32[128,8]{0,1:T(8,128)S(1)} copy-done((s32[128,8]{0,1:T(8,128)S(1)}, s32[128,8]{0,1:T(8,128)}, u32[]{:S(2)}) %copy-start.1) | copy-done | bytes 4120
  3.4 0.1 shard_map.41
  3.5 1.1 %collective-permute-done.1.other_ids_ref = s32[8,128]{1,0:T(8,128)S(1)} collective-permute-done((s32[8,128]{1,0:T(8,128)}, s32[8,128]{1,0:T(8,128)S(1)}, u32[]{:S(2)}, u32[]{:S(2)}) %collective-permute-start.1) | collective-permute-done | bytes 4128 | tf_op jit(solution)/shard_map/ppermute | solution.py:20
  4.7 1.5 %shard_map.42 = (f32[448,128]{1,0:T(8,128)S(1)}, f32[464,128]{1,0:T(8,128)S(1)}, f32[448,128]{1,0:T(8,128)S(1)}, f32[448,128]{1,0:T(8,128)S(1)}, f32[448,128]{1,...) custom-call(s32[8,128]{1,0:T(8,128)S(1)} %get-tuple-element.26.ids_r, ...), custom_call_target="tpu_custom_call" | custom-call | flops 587202560 | bytes 7340032 | tf_op jit(solution)/shard_map/pallas_call | solution.py:39
  6.2 1.5 %collective-permute-start.6 = (f32[464,128]{1,0:T(8,128)S(1)}, f32[464,128]{1,0:T(8,128)S(1)}, u32[]{:S(2)}, u32[]{:S(2)}) collective-permute-start(f32[464,128]{1,0:T(8,128)S(1)} %get-tuple-element.38), channel_id=1, source_target_pairs={{0,2},{1,3},{2,0},{3,1},{4,6},{5,7},{6,4},{7,5},{8,10},{9,11},{10,... | collective-permute-start | bytes 712712 | tf_op jit(solution)/shard_map/ppermute | solution.py:20
  7.7 0.7 %collective-permute-start.2 = (bf16[16,7296]{1,0:T(8,128)(2,1)S(1)}, bf16[16,7296]{1,0:T(8,128)(2,1)S(1)}, u32[]{:S(2)}, u32[]{:S(2)}) collective-permute-start(bf16[16,7296]{1,0:T(8,128)(2,1)S(1)} %get-tuple-element.30), channel_id=1, source_target_pairs={{1,5},{3,7},{5,1},{7,3},{9,13},{11,15},{13,9},{15,11},{17,21},{19,... | collective-permute-start | bytes 700424 | tf_op jit(solution)/shard_map/ppermute | solution.py:35
  8.4 0.4 %collective-permute-start.3 = (bf16[16,7296]{1,0:T(8,128)(2,1)S(1)}, bf16[16,7296]{1,0:T(8,128)(2,1)S(1)}, u32[]{:S(2)}, u32[]{:S(2)}) collective-permute-start(bf16[16,7296]{1,0:T(8,128)(2,1)S(1)} %get-tuple-element.31), channel_id=1, source_target_pairs={{0,8},{1,13},{2,10},{3,15},{4,12},{5,9},{6,14},{7,11},{8,0},{9,5},... | collective-permute-start | bytes 700424 | tf_op jit(solution)/shard_map/ppermute | solution.py:35
  8.8 0.6 %collective-permute-start.9 = (f32[448,128]{1,0:T(8,128)S(1)}, f32[448,128]{1,0:T(8,128)S(1)}, u32[]{:S(2)}, u32[]{:S(2)}) collective-permute-start(f32[448,128]{1,0:T(8,128)S(1)} %get-tuple-element.41), channel_id=1, source_target_pairs={{0,2},{1,3},{2,0},{3,1},{4,6},{5,7},{6,4},{7,5},{8,10},{9,11},{10,... | collective-permute-start | bytes 688136 | tf_op jit(solution)/shard_map/ppermute | solution.py:20
  9.3 5.3 %collective-permute-done.6 = f32[464,128]{1,0:T(8,128)S(1)} collective-permute-done((f32[464,128]{1,0:T(8,128)S(1)}, f32[464,128]{1,0:T(8,128)S(1)}, u32[]{:S(2)}, u32[]{:S(2)}) %collective-permute-start.6) | collective-permute-done | bytes 237600 | tf_op jit(solution)/shard_map/ppermute | solution.py:20
  14.7 0.4 collective-permute-start.7
  15.1 1.8 %collective-permute-start.11 = (f32[448,128]{1,0:T(8,128)S(1)}, f32[448,128]{1,0:T(8,128)S(1)}, u32[]{:S(2)}, u32[]{:S(2)}) collective-permute-start(f32[448,128]{1,0:T(8,128)S(1)} %get-tuple-element.44), channel_id=1, source_target_pairs={{0,2},{1,3},{2,0},{3,1},{4,6},{5,7},{6,4},{7,5},{8,10},{9,11},{10,... | collective-permute-start | bytes 688136 | tf_op jit(solution)/shard_map/ppermute | solution.py:20
  16.9 5.7 %collective-permute-done.3.refs_1_ = bf16[16,7296]{1,0:T(8,128)(2,1)S(1)} collective-permute-done((bf16[16,7296]{1,0:T(8,128)(2,1)S(1)}, bf16[16,7296]{1,0:T(8,128)(2,1)S(1)}, u32[]{:S(2)}, u32[]{:S(2)}) %collective-permute-start.3) | collective-permute-done | bytes 233504 | tf_op jit(solution)/shard_map/ppermute | solution.py:35
  22.7 0.6 %collective-permute-start.4 = (bf16[32,4096]{1,0:T(8,128)(2,1)S(1)}, bf16[32,4096]{1,0:T(8,128)(2,1)S(1)}, u32[]{:S(2)}, u32[]{:S(2)}) collective-permute-start(bf16[32,4096]{1,0:T(8,128)(2,1)S(1)} %get-tuple-element.33), channel_id=1, source_target_pairs={{0,2},{1,3},{2,0},{3,1},{4,6},{5,7},{6,4},{7,5},{8,10},{9,11},{10,... | collective-permute-start | bytes 786440 | tf_op jit(solution)/shard_map/ppermute | solution.py:20
  23.4 0.8 %collective-permute-done.11 = f32[448,128]{1,0:T(8,128)S(1)} collective-permute-done((f32[448,128]{1,0:T(8,128)S(1)}, f32[448,128]{1,0:T(8,128)S(1)}, u32[]{:S(2)}, u32[]{:S(2)}) %collective-permute-start.11) | collective-permute-done | bytes 229408 | tf_op jit(solution)/shard_map/ppermute | solution.py:20
  24.3 0.8 %collective-permute-done.7 = f32[448,128]{1,0:T(8,128)S(1)} collective-permute-done((f32[448,128]{1,0:T(8,128)S(1)}, f32[448,128]{1,0:T(8,128)S(1)}, u32[]{:S(2)}, u32[]{:S(2)}) %collective-permute-start.7) | collective-permute-done | bytes 229408 | tf_op jit(solution)/shard_map/ppermute | solution.py:20
  25.2 1.1 %collective-permute-start.8 = (f32[448,128]{1,0:T(8,128)S(1)}, f32[448,128]{1,0:T(8,128)S(1)}, u32[]{:S(2)}, u32[]{:S(2)}) collective-permute-start(f32[448,128]{1,0:T(8,128)S(1)} %get-tuple-element.39), channel_id=1, source_target_pairs={{0,2},{1,3},{2,0},{3,1},{4,6},{5,7},{6,4},{7,5},{8,10},{9,11},{10,... | collective-permute-start | bytes 688136 | tf_op jit(solution)/shard_map/ppermute | solution.py:20
  26.4 5.5 %collective-permute-done.4.refs_1_ = bf16[32,4096]{1,0:T(8,128)(2,1)S(1)} collective-permute-done((bf16[32,4096]{1,0:T(8,128)(2,1)S(1)}, bf16[32,4096]{1,0:T(8,128)(2,1)S(1)}, u32[]{:S(2)}, u32[]{:S(2)}) %collective-permute-start.4) | collective-permute-done | bytes 262176 | tf_op jit(solution)/shard_map/ppermute | solution.py:20
  32.0 0.4 collective-permute-done.10
  32.3 2.1 %collective-permute-done.8 = f32[448,128]{1,0:T(8,128)S(1)} collective-permute-done((f32[448,128]{1,0:T(8,128)S(1)}, f32[448,128]{1,0:T(8,128)S(1)}, u32[]{:S(2)}, u32[]{:S(2)}) %collective-permute-start.8) | collective-permute-done | bytes 229408 | tf_op jit(solution)/shard_map/ppermute | solution.py:20
  34.5 3.1 %collective-permute-done.12 = f32[448,128]{1,0:T(8,128)S(1)} collective-permute-done((f32[448,128]{1,0:T(8,128)S(1)}, f32[448,128]{1,0:T(8,128)S(1)}, u32[]{:S(2)}, u32[]{:S(2)}) %collective-permute-start.12) | collective-permute-done | bytes 229408 | tf_op jit(solution)/shard_map/ppermute | solution.py:20
  37.5 0.7 %add_multiply_fusion = f32[448,128]{1,0:T(8,128)} fusion(f32[448,128]{1,0:T(8,128)S(1)} %add_add_fusion.1, f32[448,128]{1,0:T(8,128)S(1)} %collective-permute-done.12), kind=kLoop, calls=%fused_computation.3 | loop fusion | flops 114688 | bytes 688128 | tf_op jit(solution)/shard_map/mul | solution.py:291
  38.2 1.9 %shard_map.44 = f32[1,384,1792]{2,1,0:T(8,128)} custom-call(bf16[32,2304]{1,0:T(8,128)(2,1)S(1)} %get-tuple-element.32.refs_0_, bf16[32,4096]{1,0:T(8,128)(2,1)S(1)} %collective-permute-done.4.refs_1_, bf16[64,2304]{1,0:T(8,128)(2,1)S(1)} %collective-permute-done.5.refs_2_), custom_call_target="tpu_custom_call" | custom-call | flops 176160768 | bytes 2752512 | tf_op jit(solution)/shard_map/pallas_call | solution.py:39
  (18 shorter events, 0.5 us)
Async XLA Ops:
  0.6 4.1 %collective-permute-start = (bf16[128,7168]{1,0:T(8,128)(2,1)}, bf16[128,7168]{1,0:T(8,128)(2,1)S(1)}, u32[]{:S(2)}, u32[]{:S(2)}) collective-permute-start(bf16[128,7168]{1,0:T(8,128)(2,1)} %tokens_ref.1), channel_id=1, source_target_pairs={{0,1},{1,0},{2,3},{3,2},{4,5},{5,4},{6,7},{7,6},{8,9},{9,8},{10,11... | collective-permute-start | bytes 5505032 | tf_op jit(solution)/shard_map/ppermute | solution.py:20
  0.7 4.0 %collective-permute-start.1 = (s32[8,128]{1,0:T(8,128)}, s32[8,128]{1,0:T(8,128)S(1)}, u32[]{:S(2)}, u32[]{:S(2)}) collective-permute-start(s32[8,128]{1,0:T(8,128)} %bitcast.1), channel_id=1, source_target_pairs={{0,1},{1,0},{2,3},{3,2},{4,5},{5,4},{6,7},{7,6},{8,9},{9,8},{10,11... | collective-permute-start | bytes 12296 | tf_op jit(solution)/shard_map/ppermute | solution.py:20
  1.2 1.5 %copy-start = (bf16[128,7168]{1,0:T(8,128)(2,1)S(1)}, bf16[128,7168]{1,0:T(8,128)(2,1)}, u32[]{:S(2)}) copy-start(bf16[128,7168]{1,0:T(8,128)(2,1)} %tokens_ref.1) | copy-start | bytes 5505028
  2.7 0.7 %copy-start.1 = (s32[128,8]{0,1:T(8,128)S(1)}, s32[128,8]{0,1:T(8,128)}, u32[]{:S(2)}) copy-start(s32[128,8]{0,1:T(8,128)} %param.3) | copy-start | bytes 12292
  6.2 8.5 %collective-permute-start.6 = (f32[464,128]{1,0:T(8,128)S(1)}, f32[464,128]{1,0:T(8,128)S(1)}, u32[]{:S(2)}, u32[]{:S(2)}) collective-permute-start(f32[464,128]{1,0:T(8,128)S(1)} %get-tuple-element.38), channel_id=1, source_target_pairs={{0,2},{1,3},{2,0},{3,1},{4,6},{5,7},{6,4},{7,5},{8,10},{9,11},{10,... | collective-permute-start | bytes 712712 | tf_op jit(solution)/shard_map/ppermute | solution.py:20
  7.7 9.2 %collective-permute-start.2 = (bf16[16,7296]{1,0:T(8,128)(2,1)S(1)}, bf16[16,7296]{1,0:T(8,128)(2,1)S(1)}, u32[]{:S(2)}, u32[]{:S(2)}) collective-permute-start(bf16[16,7296]{1,0:T(8,128)(2,1)S(1)} %get-tuple-element.30), channel_id=1, source_target_pairs={{1,5},{3,7},{5,1},{7,3},{9,13},{11,15},{13,9},{15,11},{17,21},{19,... | collective-permute-start | bytes 700424 | tf_op jit(solution)/shard_map/ppermute | solution.py:35
  8.4 14.3 %collective-permute-start.3 = (bf16[16,7296]{1,0:T(8,128)(2,1)S(1)}, bf16[16,7296]{1,0:T(8,128)(2,1)S(1)}, u32[]{:S(2)}, u32[]{:S(2)}) collective-permute-start(bf16[16,7296]{1,0:T(8,128)(2,1)S(1)} %get-tuple-element.31), channel_id=1, source_target_pairs={{0,8},{1,13},{2,10},{3,15},{4,12},{5,9},{6,14},{7,11},{8,0},{9,5},... | collective-permute-start | bytes 700424 | tf_op jit(solution)/shard_map/ppermute | solution.py:35
  8.8 14.5 %collective-permute-start.9 = (f32[448,128]{1,0:T(8,128)S(1)}, f32[448,128]{1,0:T(8,128)S(1)}, u32[]{:S(2)}, u32[]{:S(2)}) collective-permute-start(f32[448,128]{1,0:T(8,128)S(1)} %get-tuple-element.41), channel_id=1, source_target_pairs={{0,2},{1,3},{2,0},{3,1},{4,6},{5,7},{6,4},{7,5},{8,10},{9,11},{10,... | collective-permute-start | bytes 688136 | tf_op jit(solution)/shard_map/ppermute | solution.py:20
  14.7 10.4 %collective-permute-start.7 = (f32[448,128]{1,0:T(8,128)S(1)}, f32[448,128]{1,0:T(8,128)S(1)}, u32[]{:S(2)}, u32[]{:S(2)}) collective-permute-start(f32[448,128]{1,0:T(8,128)S(1)} %slice_add_fusion), channel_id=1, source_target_pairs={{0,4},{4,0},{8,12},{12,8},{1,5},{5,1},{9,13},{13,9},{2,6},{6,2},{1... | collective-permute-start | bytes 688136 | tf_op jit(solution)/shard_map/ppermute | solution.py:20
  15.1 9.2 %collective-permute-start.11 = (f32[448,128]{1,0:T(8,128)S(1)}, f32[448,128]{1,0:T(8,128)S(1)}, u32[]{:S(2)}, u32[]{:S(2)}) collective-permute-start(f32[448,128]{1,0:T(8,128)S(1)} %get-tuple-element.44), channel_id=1, source_target_pairs={{0,2},{1,3},{2,0},{3,1},{4,6},{5,7},{6,4},{7,5},{8,10},{9,11},{10,... | collective-permute-start | bytes 688136 | tf_op jit(solution)/shard_map/ppermute | solution.py:20
  22.7 9.1 %collective-permute-start.4 = (bf16[32,4096]{1,0:T(8,128)(2,1)S(1)}, bf16[32,4096]{1,0:T(8,128)(2,1)S(1)}, u32[]{:S(2)}, u32[]{:S(2)}) collective-permute-start(bf16[32,4096]{1,0:T(8,128)(2,1)S(1)} %get-tuple-element.33), channel_id=1, source_target_pairs={{0,2},{1,3},{2,0},{3,1},{4,6},{5,7},{6,4},{7,5},{8,10},{9,11},{10,... | collective-permute-start | bytes 786440 | tf_op jit(solution)/shard_map/ppermute | solution.py:20
  23.4 9.0 %collective-permute-start.10 = (f32[448,128]{1,0:T(8,128)S(1)}, f32[448,128]{1,0:T(8,128)S(1)}, u32[]{:S(2)}, u32[]{:S(2)}) collective-permute-start(f32[448,128]{1,0:T(8,128)S(1)} %add.28), channel_id=1, source_target_pairs={{0,4},{4,0},{8,12},{12,8},{1,5},{5,1},{9,13},{13,9},{2,6},{6,2},{1... | collective-permute-start | bytes 688136 | tf_op jit(solution)/shard_map/ppermute | solution.py:20
  25.1 12.4 %collective-permute-start.12 = (f32[448,128]{1,0:T(8,128)S(1)}, f32[448,128]{1,0:T(8,128)S(1)}, u32[]{:S(2)}, u32[]{:S(2)}) collective-permute-start(f32[448,128]{1,0:T(8,128)S(1)} %add_add_fusion), channel_id=1, source_target_pairs={{0,8},{4,12},{8,0},{12,4},{1,9},{5,13},{9,1},{13,5},{2,10},{6,14},... | collective-permute-start | bytes 688136 | tf_op jit(solution)/shard_map/ppermute | solution.py:20
  25.2 9.2 %collective-permute-start.8 = (f32[448,128]{1,0:T(8,128)S(1)}, f32[448,128]{1,0:T(8,128)S(1)}, u32[]{:S(2)}, u32[]{:S(2)}) collective-permute-start(f32[448,128]{1,0:T(8,128)S(1)} %get-tuple-element.39), channel_id=1, source_target_pairs={{0,2},{1,3},{2,0},{3,1},{4,6},{5,7},{6,4},{7,5},{8,10},{9,11},{10,... | collective-permute-start | bytes 688136 | tf_op jit(solution)/shard_map/ppermute | solution.py:20
  31.9 6.4 %collective-permute-start.5 = (bf16[64,2304]{1,0:T(8,128)(2,1)S(1)}, bf16[64,2304]{1,0:T(8,128)(2,1)S(1)}, u32[]{:S(2)}, u32[]{:S(2)}) collective-permute-start(bf16[64,2304]{1,0:T(8,128)(2,1)S(1)} %pad_maximum_fusion), channel_id=1, source_target_pairs={{0,1},{1,0},{2,3},{3,2},{4,5},{5,4},{6,7},{7,6},{8,9},{9,8},{10,11... | collective-permute-start | bytes 884744 | tf_op jit(solution)/shard_map/ppermute | solution.py:20

commit v5 on v4

--- a/solution.py
+++ b/solution.py
@@ -72,8 +72,8 @@
         ref[:, end + BAND :] = flag
 
 
-def hessian_kernel(*refs):
-    row_refs, (routed_ref, routed, sems) = refs[:-3], refs[-3:]
+def finish_kernel(*refs):
+    row_refs, (sum_ref, routed_ref, shared_ref, routed, sems) = refs[:-5], refs[-5:]
     _, band_size, width = routed_ref.shape
     copies = []
 
@@ -98,6 +98,7 @@
         )
         routed[part] = product * (2.0 / count)
         send(routed.at[part], routed_ref.at[0, part])
+    send(sum_ref, shared_ref)
     for copy in copies:
         copy.wait()
 
@@ -270,25 +271,29 @@
     across = [exchange(x, "dp", 2 * k + 2) for k, x in enumerate(packed)]
     beside = exchange(jnp.concatenate([give] + [x[:, width:] for x in across]), "dp", 1)
     gathered = [mine, *across, beside]
-    routed_out = call(
-        hessian_kernel,
-        jax.ShapeDtypeStruct((1, BAND, width), jnp.float32),
-        *gathered,
-        flops=2 * BAND * width * rows * peers,
-        nbytes=4 * BAND * width,
-        in_specs=[inside] * len(gathered),
-        out_specs=anywhere,
-        scratch_shapes=[
-            pltpu.VMEM((BAND, width), jnp.float32),
-            pltpu.SemaphoreType.DMA((BAND // LANES,)),
-        ],
-    )
     paired = tie(paired, packed)
     others = [
         exchange(paired[i * share : (i + 1) * share], "expert", m) for i, m in enumerate(far)
     ]
     summed = sum(others, lax.optimization_barrier(own))
     shared_out = summed * (2.0 / (tok_rows * experts * peers))
+    routed_out, shared_out = call(
+        finish_kernel,
+        [
+            jax.ShapeDtypeStruct((1, BAND, width), jnp.float32),
+            jax.ShapeDtypeStruct((share, SBAND), jnp.float32),
+        ],
+        *gathered,
+        shared_out,
+        flops=2 * BAND * width * rows * peers,
+        nbytes=4 * BAND * width,
+        in_specs=[inside] * (len(gathered) + 1),
+        out_specs=[anywhere, anywhere],
+        scratch_shapes=[
+            pltpu.VMEM((BAND, width), jnp.float32),
+            pltpu.SemaphoreType.DMA((BAND // LANES + 1,)),
+        ],
+    )
     return routed_out, shared_out
 
 

time: 40.3 us -> 39.7 us (0.985)
  other arithmetic: 0.91 us -> 0.23 us
    mul x1, other arithmetic: 0.71 us -> 0.03 us  [on_device(): shared_out = summed * (2.0 / (tok_rows * experts * peers))]
  transfers between devices with their start and end apart: 13 -> 13, of which waited for: 9 -> 9; matrix products, arithmetic and copies ran while one was open for 2% -> 1% of each run, Pallas kernels for 0% -> 0%
where the time goes in v5:
time: 39.7 us; the launch traced here: 39.5 us
  waiting for transfers between devices  24.8 us (62%)
  starting transfers between devices  7.92 us (20%)
  Pallas kernels  3.62 us (9%)
  local copies, waits for them, and re-layouts  2.2 us (6%)
  between operations  0.73 us (2%)
    ppermute x11, waiting for transfers between devices, exchange(): return lax.ppermute(value, axis, [(i, i ^ distance) for i in range(size)])  19.1 us
    ppermute x11, starting transfers between devices, exchange(): return lax.ppermute(value, axis, [(i, i ^ distance) for i in range(size)])  6.85 us
    ppermute x2, waiting for transfers between devices, pass_on(): return lax.ppermute(value, ('expert', 'dp'), pairs)  5.72 us
    pallas_call x4, Pallas kernels, call(): pl.pallas_call(kernel, out_shape=out_shape, compiler_params=pltpu.Compile...  3.62 us
    unnamed x4, local copies, waits for them, and re-layouts  2.19 us
    ppermute x2, starting transfers between devices, pass_on(): return lax.ppermute(value, ('expert', 'dp'), pairs)  1.07 us
  transfers between devices with their start and end apart: 13, of which 9 were waited for; matrix products, arithmetic and copies ran while one was open for 1% of the time, Pallas kernels for 0%

profile of v5, /device:TPU:24, one launch (start us, length us, event | category | flops | bytes accessed | tf_op | source)
XLA Modules:
  0.0 39.5 jit_solution(2039722278070864016)
XLA Ops:
  0.7 0.5 %collective-permute-start.1 = (s32[8,128]{1,0:T(8,128)}, s32[8,128]{1,0:T(8,128)S(1)}, u32[]{:S(2)}, u32[]{:S(2)}) collective-permute-start(s32[8,128]{1,0:T(8,128)} %bitcast.1), channel_id=1, source_target_pairs={{0,1},{1,0},{2,3},{3,2},{4,5},{5,4},{6,7},{7,6},{8,9},{9,8},{10,11... | collective-permute-start | bytes 12296 | tf_op jit(solution)/shard_map/ppermute | solution.py:20
  1.2 1.5 %copy-done = bf16[128,7168]{1,0:T(8,128)(2,1)S(1)} copy-done((bf16[128,7168]{1,0:T(8,128)(2,1)S(1)}, bf16[128,7168]{1,0:T(8,128)(2,1)}, u32[]{:S(2)}) %copy-start) | copy-done | bytes 1835032
  2.7 0.7 %copy-done.1 = s32[128,8]{0,1:T(8,128)S(1)} copy-done((s32[128,8]{0,1:T(8,128)S(1)}, s32[128,8]{0,1:T(8,128)}, u32[]{:S(2)}) %copy-start.1) | copy-done | bytes 4120
  3.4 0.1 shard_map.41
  3.5 1.1 %collective-permute-done.1.other_ids_ref = s32[8,128]{1,0:T(8,128)S(1)} collective-permute-done((s32[8,128]{1,0:T(8,128)}, s32[8,128]{1,0:T(8,128)S(1)}, u32[]{:S(2)}, u32[]{:S(2)}) %collective-permute-start.1) | collective-permute-done | bytes 4128 | tf_op jit(solution)/shard_map/ppermute | solution.py:20
  4.7 1.5 %shard_map.42 = (f32[448,128]{1,0:T(8,128)S(1)}, f32[464,128]{1,0:T(8,128)S(1)}, f32[448,128]{1,0:T(8,128)S(1)}, f32[448,128]{1,0:T(8,128)S(1)}, f32[448,128]{1,...) custom-call(s32[8,128]{1,0:T(8,128)S(1)} %get-tuple-element.26.ids_r, ...), custom_call_target="tpu_custom_call" | custom-call | flops 587202560 | bytes 7340032 | tf_op jit(solution)/shard_map/pallas_call | solution.py:39
  6.2 1.5 %collective-permute-start.6 = (f32[464,128]{1,0:T(8,128)S(1)}, f32[464,128]{1,0:T(8,128)S(1)}, u32[]{:S(2)}, u32[]{:S(2)}) collective-permute-start(f32[464,128]{1,0:T(8,128)S(1)} %get-tuple-element.38), channel_id=1, source_target_pairs={{0,2},{1,3},{2,0},{3,1},{4,6},{5,7},{6,4},{7,5},{8,10},{9,11},{10,... | collective-permute-start | bytes 712712 | tf_op jit(solution)/shard_map/ppermute | solution.py:20
  7.7 0.7 %collective-permute-start.2 = (bf16[16,7296]{1,0:T(8,128)(2,1)S(1)}, bf16[16,7296]{1,0:T(8,128)(2,1)S(1)}, u32[]{:S(2)}, u32[]{:S(2)}) collective-permute-start(bf16[16,7296]{1,0:T(8,128)(2,1)S(1)} %get-tuple-element.30), channel_id=1, source_target_pairs={{1,5},{3,7},{5,1},{7,3},{9,13},{11,15},{13,9},{15,11},{17,21},{19,... | collective-permute-start | bytes 700424 | tf_op jit(solution)/shard_map/ppermute | solution.py:35
  8.4 0.4 %collective-permute-start.3 = (bf16[16,7296]{1,0:T(8,128)(2,1)S(1)}, bf16[16,7296]{1,0:T(8,128)(2,1)S(1)}, u32[]{:S(2)}, u32[]{:S(2)}) collective-permute-start(bf16[16,7296]{1,0:T(8,128)(2,1)S(1)} %get-tuple-element.31), channel_id=1, source_target_pairs={{0,8},{1,13},{2,10},{3,15},{4,12},{5,9},{6,14},{7,11},{8,0},{9,5},... | collective-permute-start | bytes 700424 | tf_op jit(solution)/shard_map/ppermute | solution.py:35
  8.8 0.6 %collective-permute-start.9 = (f32[448,128]{1,0:T(8,128)S(1)}, f32[448,128]{1,0:T(8,128)S(1)}, u32[]{:S(2)}, u32[]{:S(2)}) collective-permute-start(f32[448,128]{1,0:T(8,128)S(1)} %get-tuple-element.41), channel_id=1, source_target_pairs={{0,2},{1,3},{2,0},{3,1},{4,6},{5,7},{6,4},{7,5},{8,10},{9,11},{10,... | collective-permute-start | bytes 688136 | tf_op jit(solution)/shard_map/ppermute | solution.py:20
  9.3 5.3 %collective-permute-done.6 = f32[464,128]{1,0:T(8,128)S(1)} collective-permute-done((f32[464,128]{1,0:T(8,128)S(1)}, f32[464,128]{1,0:T(8,128)S(1)}, u32[]{:S(2)}, u32[]{:S(2)}) %collective-permute-start.6) | collective-permute-done | bytes 237600 | tf_op jit(solution)/shard_map/ppermute | solution.py:20
  14.7 0.4 collective-permute-start.7
  15.1 1.8 %collective-permute-start.11 = (f32[448,128]{1,0:T(8,128)S(1)}, f32[448,128]{1,0:T(8,128)S(1)}, u32[]{:S(2)}, u32[]{:S(2)}) collective-permute-start(f32[448,128]{1,0:T(8,128)S(1)} %get-tuple-element.44), channel_id=1, source_target_pairs={{0,2},{1,3},{2,0},{3,1},{4,6},{5,7},{6,4},{7,5},{8,10},{9,11},{10,... | collective-permute-start | bytes 688136 | tf_op jit(solution)/shard_map/ppermute | solution.py:20
  16.9 5.7 %collective-permute-done.3.refs_1_ = bf16[16,7296]{1,0:T(8,128)(2,1)S(1)} collective-permute-done((bf16[16,7296]{1,0:T(8,128)(2,1)S(1)}, bf16[16,7296]{1,0:T(8,128)(2,1)S(1)}, u32[]{:S(2)}, u32[]{:S(2)}) %collective-permute-start.3) | collective-permute-done | bytes 233504 | tf_op jit(solution)/shard_map/ppermute | solution.py:35
  22.7 0.6 %collective-permute-start.4 = (bf16[32,4096]{1,0:T(8,128)(2,1)S(1)}, bf16[32,4096]{1,0:T(8,128)(2,1)S(1)}, u32[]{:S(2)}, u32[]{:S(2)}) collective-permute-start(bf16[32,4096]{1,0:T(8,128)(2,1)S(1)} %get-tuple-element.33), channel_id=1, source_target_pairs={{0,2},{1,3},{2,0},{3,1},{4,6},{5,7},{6,4},{7,5},{8,10},{9,11},{10,... | collective-permute-start | bytes 786440 | tf_op jit(solution)/shard_map/ppermute | solution.py:20
  23.4 0.1 collective-permute-start.10
  23.4 0.8 %collective-permute-done.11 = f32[448,128]{1,0:T(8,128)S(1)} collective-permute-done((f32[448,128]{1,0:T(8,128)S(1)}, f32[448,128]{1,0:T(8,128)S(1)}, u32[]{:S(2)}, u32[]{:S(2)}) %collective-permute-start.11) | collective-permute-done | bytes 229408 | tf_op jit(solution)/shard_map/ppermute | solution.py:20
  24.3 0.8 %collective-permute-done.7 = f32[448,128]{1,0:T(8,128)S(1)} collective-permute-done((f32[448,128]{1,0:T(8,128)S(1)}, f32[448,128]{1,0:T(8,128)S(1)}, u32[]{:S(2)}, u32[]{:S(2)}) %collective-permute-start.7) | collective-permute-done | bytes 229408 | tf_op jit(solution)/shard_map/ppermute | solution.py:20
  25.2 1.1 %collective-permute-start.8 = (f32[448,128]{1,0:T(8,128)S(1)}, f32[448,128]{1,0:T(8,128)S(1)}, u32[]{:S(2)}, u32[]{:S(2)}) collective-permute-start(f32[448,128]{1,0:T(8,128)S(1)} %get-tuple-element.39), channel_id=1, source_target_pairs={{0,2},{1,3},{2,0},{3,1},{4,6},{5,7},{6,4},{7,5},{8,10},{9,11},{10,... | collective-permute-start | bytes 688136 | tf_op jit(solution)/shard_map/ppermute | solution.py:20
  26.4 5.5 %collective-permute-done.4.refs_1_ = bf16[32,4096]{1,0:T(8,128)(2,1)S(1)} collective-permute-done((bf16[32,4096]{1,0:T(8,128)(2,1)S(1)}, bf16[32,4096]{1,0:T(8,128)(2,1)S(1)}, u32[]{:S(2)}, u32[]{:S(2)}) %collective-permute-start.4) | collective-permute-done | bytes 262176 | tf_op jit(solution)/shard_map/ppermute | solution.py:20
  32.0 0.4 collective-permute-done.10
  32.3 2.1 %collective-permute-done.8 = f32[448,128]{1,0:T(8,128)S(1)} collective-permute-done((f32[448,128]{1,0:T(8,128)S(1)}, f32[448,128]{1,0:T(8,128)S(1)}, u32[]{:S(2)}, u32[]{:S(2)}) %collective-permute-start.8) | collective-permute-done | bytes 229408 | tf_op jit(solution)/shard_map/ppermute | solution.py:20
  34.5 3.1 %collective-permute-done.12 = f32[448,128]{1,0:T(8,128)S(1)} collective-permute-done((f32[448,128]{1,0:T(8,128)S(1)}, f32[448,128]{1,0:T(8,128)S(1)}, u32[]{:S(2)}, u32[]{:S(2)}) %collective-permute-start.12) | collective-permute-done | bytes 229408 | tf_op jit(solution)/shard_map/ppermute | solution.py:20
  37.6 2.0 %shard_map.44 = (f32[1,384,1792]{2,1,0:T(8,128)}, f32[448,128]{1,0:T(8,128)}) custom-call(bf16[32,2304]{1,0:T(8,128)(2,1)S(1)} %get-tuple-element.32.refs_0_, bf16[32,4096]{1,0:T(8,128)(2,1)S(1)} %collective-permute-done.4.refs_1_, bf16[64,2304]{1,0:T(8,128)(2,1)S(1)} %collective-permute-done.5.refs_2_, f32[448,128]{1,0:T(8,128)S(1)} %add_multiply_fusion.refs_3_), custom_call_target="tpu_custom_call" | custom-call | flops 176160768 | bytes 2752512 | tf_op jit(solution)/shard_map/pallas_call | solution.py:39
  (18 shorter events, 0.5 us)
Async XLA Ops:
  0.6 4.1 %collective-permute-start = (bf16[128,7168]{1,0:T(8,128)(2,1)}, bf16[128,7168]{1,0:T(8,128)(2,1)S(1)}, u32[]{:S(2)}, u32[]{:S(2)}) collective-permute-start(bf16[128,7168]{1,0:T(8,128)(2,1)} %tokens_ref.1), channel_id=1, source_target_pairs={{0,1},{1,0},{2,3},{3,2},{4,5},{5,4},{6,7},{7,6},{8,9},{9,8},{10,11... | collective-permute-start | bytes 5505032 | tf_op jit(solution)/shard_map/ppermute | solution.py:20
  0.7 4.0 %collective-permute-start.1 = (s32[8,128]{1,0:T(8,128)}, s32[8,128]{1,0:T(8,128)S(1)}, u32[]{:S(2)}, u32[]{:S(2)}) collective-permute-start(s32[8,128]{1,0:T(8,128)} %bitcast.1), channel_id=1, source_target_pairs={{0,1},{1,0},{2,3},{3,2},{4,5},{5,4},{6,7},{7,6},{8,9},{9,8},{10,11... | collective-permute-start | bytes 12296 | tf_op jit(solution)/shard_map/ppermute | solution.py:20
  1.2 1.5 %copy-start = (bf16[128,7168]{1,0:T(8,128)(2,1)S(1)}, bf16[128,7168]{1,0:T(8,128)(2,1)}, u32[]{:S(2)}) copy-start(bf16[128,7168]{1,0:T(8,128)(2,1)} %tokens_ref.1) | copy-start | bytes 5505028
  2.7 0.7 %copy-start.1 = (s32[128,8]{0,1:T(8,128)S(1)}, s32[128,8]{0,1:T(8,128)}, u32[]{:S(2)}) copy-start(s32[128,8]{0,1:T(8,128)} %param.3) | copy-start | bytes 12292
  6.2 8.5 %collective-permute-start.6 = (f32[464,128]{1,0:T(8,128)S(1)}, f32[464,128]{1,0:T(8,128)S(1)}, u32[]{:S(2)}, u32[]{:S(2)}) collective-permute-start(f32[464,128]{1,0:T(8,128)S(1)} %get-tuple-element.38), channel_id=1, source_target_pairs={{0,2},{1,3},{2,0},{3,1},{4,6},{5,7},{6,4},{7,5},{8,10},{9,11},{10,... | collective-permute-start | bytes 712712 | tf_op jit(solution)/shard_map/ppermute | solution.py:20
  7.7 9.2 %collective-permute-start.2 = (bf16[16,7296]{1,0:T(8,128)(2,1)S(1)}, bf16[16,7296]{1,0:T(8,128)(2,1)S(1)}, u32[]{:S(2)}, u32[]{:S(2)}) collective-permute-start(bf16[16,7296]{1,0:T(8,128)(2,1)S(1)} %get-tuple-element.30), channel_id=1, source_target_pairs={{1,5},{3,7},{5,1},{7,3},{9,13},{11,15},{13,9},{15,11},{17,21},{19,... | collective-permute-start | bytes 700424 | tf_op jit(solution)/shard_map/ppermute | solution.py:35
  8.4 14.3 %collective-permute-start.3 = (bf16[16,7296]{1,0:T(8,128)(2,1)S(1)}, bf16[16,7296]{1,0:T(8,128)(2,1)S(1)}, u32[]{:S(2)}, u32[]{:S(2)}) collective-permute-start(bf16[16,7296]{1,0:T(8,128)(2,1)S(1)} %get-tuple-element.31), channel_id=1, source_target_pairs={{0,8},{1,13},{2,10},{3,15},{4,12},{5,9},{6,14},{7,11},{8,0},{9,5},... | collective-permute-start | bytes 700424 | tf_op jit(solution)/shard_map/ppermute | solution.py:35
  8.8 14.5 %collective-permute-start.9 = (f32[448,128]{1,0:T(8,128)S(1)}, f32[448,128]{1,0:T(8,128)S(1)}, u32[]{:S(2)}, u32[]{:S(2)}) collective-permute-start(f32[448,128]{1,0:T(8,128)S(1)} %get-tuple-element.41), channel_id=1, source_target_pairs={{0,2},{1,3},{2,0},{3,1},{4,6},{5,7},{6,4},{7,5},{8,10},{9,11},{10,... | collective-permute-start | bytes 688136 | tf_op jit(solution)/shard_map/ppermute | solution.py:20
  14.7 10.4 %collective-permute-start.7 = (f32[448,128]{1,0:T(8,128)S(1)}, f32[448,128]{1,0:T(8,128)S(1)}, u32[]{:S(2)}, u32[]{:S(2)}) collective-permute-start(f32[448,128]{1,0:T(8,128)S(1)} %slice_add_fusion), channel_id=1, source_target_pairs={{0,4},{4,0},{8,12},{12,8},{1,5},{5,1},{9,13},{13,9},{2,6},{6,2},{1... | collective-permute-start | bytes 688136 | tf_op jit(solution)/shard_map/ppermute | solution.py:20
  15.1 9.2 %collective-permute-start.11 = (f32[448,128]{1,0:T(8,128)S(1)}, f32[448,128]{1,0:T(8,128)S(1)}, u32[]{:S(2)}, u32[]{:S(2)}) collective-permute-start(f32[448,128]{1,0:T(8,128)S(1)} %get-tuple-element.44), channel_id=1, source_target_pairs={{0,2},{1,3},{2,0},{3,1},{4,6},{5,7},{6,4},{7,5},{8,10},{9,11},{10,... | collective-permute-start | bytes 688136 | tf_op jit(solution)/shard_map/ppermute | solution.py:20
  22.7 9.1 %collective-permute-start.4 = (bf16[32,4096]{1,0:T(8,128)(2,1)S(1)}, bf16[32,4096]{1,0:T(8,128)(2,1)S(1)}, u32[]{:S(2)}, u32[]{:S(2)}) collective-permute-start(bf16[32,4096]{1,0:T(8,128)(2,1)S(1)} %get-tuple-element.33), channel_id=1, source_target_pairs={{0,2},{1,3},{2,0},{3,1},{4,6},{5,7},{6,4},{7,5},{8,10},{9,11},{10,... | collective-permute-start | bytes 786440 | tf_op jit(solution)/shard_map/ppermute | solution.py:20
  23.4 9.0 %collective-permute-start.10 = (f32[448,128]{1,0:T(8,128)S(1)}, f32[448,128]{1,0:T(8,128)S(1)}, u32[]{:S(2)}, u32[]{:S(2)}) collective-permute-start(f32[448,128]{1,0:T(8,128)S(1)} %add.28), channel_id=1, source_target_pairs={{0,4},{4,0},{8,12},{12,8},{1,5},{5,1},{9,13},{13,9},{2,6},{6,2},{1... | collective-permute-start | bytes 688136 | tf_op jit(solution)/shard_map/ppermute | solution.py:20
  25.1 12.4 %collective-permute-start.12 = (f32[448,128]{1,0:T(8,128)S(1)}, f32[448,128]{1,0:T(8,128)S(1)}, u32[]{:S(2)}, u32[]{:S(2)}) collective-permute-start(f32[448,128]{1,0:T(8,128)S(1)} %add_add_fusion), channel_id=1, source_target_pairs={{0,8},{4,12},{8,0},{12,4},{1,9},{5,13},{9,1},{13,5},{2,10},{6,14},... | collective-permute-start | bytes 688136 | tf_op jit(solution)/shard_map/ppermute | solution.py:20
  25.2 9.2 %collective-permute-start.8 = (f32[448,128]{1,0:T(8,128)S(1)}, f32[448,128]{1,0:T(8,128)S(1)}, u32[]{:S(2)}, u32[]{:S(2)}) collective-permute-start(f32[448,128]{1,0:T(8,128)S(1)} %get-tuple-element.39), channel_id=1, source_target_pairs={{0,2},{1,3},{2,0},{3,1},{4,6},{5,7},{6,4},{7,5},{8,10},{9,11},{10,... | collective-permute-start | bytes 688136 | tf_op jit(solution)/shard_map/ppermute | solution.py:20
  31.9 5.7 %collective-permute-start.5 = (bf16[64,2304]{1,0:T(8,128)(2,1)S(1)}, bf16[64,2304]{1,0:T(8,128)(2,1)S(1)}, u32[]{:S(2)}, u32[]{:S(2)}) collective-permute-start(bf16[64,2304]{1,0:T(8,128)(2,1)S(1)} %pad_maximum_fusion), channel_id=1, source_target_pairs={{0,1},{1,0},{2,3},{3,2},{4,5},{5,4},{6,7},{7,6},{8,9},{9,8},{10,11... | collective-permute-start | bytes 884744 | tf_op jit(solution)/shard_map/ppermute | solution.py:20

commit v6 on v5

--- a/solution.py
+++ b/solution.py
@@ -111,23 +111,38 @@
         < lax.broadcasted_iota(jnp.int32, (tokens, tokens), 1)
     ).astype(jnp.bfloat16)
     rank = jnp.dot(member.astype(jnp.bfloat16), earlier, preferred_element_type=jnp.float32)
-    slot = lax.broadcasted_iota(jnp.int32, (2 * CAP, tokens), 0).astype(jnp.float32)
+    slot = lax.broadcasted_iota(jnp.int32, (CAP, tokens), 0).astype(jnp.float32)
     return jnp.where(slot == rank, member, 0.0)
 
 
-def fetch_kernel(ids_ref, tokens_ref, held_ids_ref, held_ref, sems):
+def picks_of(ids_ref, experts):
+    e, d = lax.axis_index("expert"), lax.axis_index("dp")
+    picks = [select(ids_ref[...], e ^ (k + d % 2)) for k in range(0, experts, 2)]
+    picks = jnp.concatenate(picks, axis=0)
+    flags = jnp.broadcast_to(jnp.sum(picks, axis=1, keepdims=True), (picks.shape[0], LANES))
+    return picks.astype(jnp.bfloat16), flags
+
+
+def fetch_kernel(ids_ref, tokens_ref, held_ref, rows_ref, sems):
+    features = tokens_ref.shape[1]
+    parts = parts_of(features)
     copies = [
-        pltpu.make_async_copy(ids_ref, held_ids_ref, sems.at[0]),
-        pltpu.make_async_copy(tokens_ref, held_ref, sems.at[1]),
+        pltpu.make_async_copy(tokens_ref.at[:, part], held_ref.at[:, part], sems.at[i])
+        for i, part in enumerate(parts)
     ]
     for copy in copies:
         copy.start()
-    for copy in copies:
+    picks, flags = picks_of(ids_ref, 2 * rows_ref.shape[0] // CAP)
+    rows_ref[:, features:] = flags
+    for copy, part in zip(copies, parts):
         copy.wait()
+        rows_ref[:, part] = jnp.dot(
+            picks, held_ref[:, part], preferred_element_type=jnp.float32
+        )
 
 
 def pair_kernel(
-    ids_ref, other_ids_ref, mine_ref, other_ref, *out_refs, experts, peers, wanted, aligned
+    other_ids_ref, rows_ref, mine_ref, other_ref, *out_refs, experts, peers, wanted, aligned
 ):
     out_refs, row_refs = out_refs[: -experts // 2], out_refs[-experts // 2 :]
     features = mine_ref.shape[1]
@@ -163,18 +178,17 @@
         for part in parts_of(features):
             out_refs[0][part] = product(part)
 
-    ids = jnp.concatenate([ids_ref[...], other_ids_ref[...]], axis=1)
-    picks = jnp.concatenate(
-        [select(ids, e ^ (k + d % 2)) for k in range(0, experts, 2)], axis=0
-    )
-    flags = jnp.broadcast_to(jnp.sum(picks, axis=1, keepdims=True), (picks.shape[0], LANES))
-    picks = picks.astype(jnp.bfloat16)
+    picks, flags = picks_of(other_ids_ref, experts)
+
+    def put(columns, found):
+        for i, ref in enumerate(row_refs):
+            part = slice(i * CAP, (i + 1) * CAP)
+            both_rows = jnp.concatenate([rows_ref[part, columns], found[part]], axis=0)
+            ref[:, columns] = both_rows.astype(jnp.bfloat16)
+
     for part in parts_of(features):
-        chosen = jnp.dot(picks, both(part), preferred_element_type=jnp.float32)
-        for i, ref in enumerate(row_refs):
-            ref[:, part] = chosen[2 * CAP * i : 2 * CAP * (i + 1)].astype(jnp.bfloat16)
-    for i, ref in enumerate(row_refs):
-        ref[:, features:] = flags[2 * CAP * i : 2 * CAP * (i + 1)].astype(jnp.bfloat16)
+        put(part, jnp.dot(picks, other_ref[:, part], preferred_element_type=jnp.float32))
+    put(slice(features, features + LANES), flags)
 
 
 def on_device(tokens, expert_ids):
@@ -189,21 +203,23 @@
     ids = expert_ids.T
     other = exchange(tokens, "dp", 1)
     other_ids = exchange(ids, "dp", 1)
-    ids, mine = call(
+    mine, own_rows = call(
         fetch_kernel,
         [
-            jax.ShapeDtypeStruct(ids.shape, ids.dtype),
             jax.ShapeDtypeStruct(tokens.shape, tokens.dtype),
+            jax.ShapeDtypeStruct((experts * CAP // 2, features + LANES), jnp.float32),
         ],
         ids,
         tokens,
         flops=0,
         nbytes=4 * tok_rows * features,
-        in_specs=[anywhere, anywhere],
+        in_specs=[inside, anywhere],
         out_specs=[inside, inside],
-        scratch_shapes=[pltpu.SemaphoreType.DMA((2,))],
-    )
-    ids, mine, other, other_ids = lax.optimization_barrier((ids, mine, other, other_ids))
+        scratch_shapes=[pltpu.SemaphoreType.DMA((len(parts_of(features)),))],
+    )
+    own_rows, mine, other, other_ids = lax.optimization_barrier(
+        (own_rows, mine, other, other_ids)
+    )
 
     even = range(0, peers, 2)
     far = range(2, experts, 2)
@@ -222,8 +238,8 @@
             for size in (sizes if aligned else [features])
         ]
         + [jax.ShapeDtypeStruct((2 * CAP, features + LANES), jnp.bfloat16)] * (experts // 2),
-        ids,
         other_ids,
+        own_rows,
         mine,
         other,
         flops=4 * tok_rows * features * (SBAND + experts * CAP),

time: 39.7 us -> 39.4 us (level)
  waiting for transfers between devices: 24.8 us -> 23.9 us
  Pallas kernels: 3.62 us -> 4.34 us
    ppermute x11, waiting for transfers between devices: 19.1 us -> 18.2 us  [exchange(): return lax.ppermute(value, axis, [(i, i ^ distance) for i in range(size)])]
    pallas_call x4, Pallas kernels: 3.62 us -> 4.34 us  [call(): pl.pallas_call(kernel, out_shape=out_shape, compiler_params=pltpu.Compile...]
  transfers between devices with their start and end apart: 13 -> 13, of which waited for: 9 -> 9; matrix products, arithmetic and copies ran while one was open for 1% -> 1% of each run, Pallas kernels for 0% -> 3%
where the time goes in v6:
time: 39.4 us; the launch traced here: 39.2 us
  waiting for transfers between devices  23.9 us (61%)
  starting transfers between devices  7.83 us (20%)
  Pallas kernels  4.34 us (11%)
  local copies, waits for them, and re-layouts  2.2 us (6%)
  between operations  0.73 us (2%)
    ppermute x11, waiting for transfers between devices, exchange(): return lax.ppermute(value, axis, [(i, i ^ distance) for i in range(size)])  18.2 us
    ppermute x11, starting transfers between devices, exchange(): return lax.ppermute(value, axis, [(i, i ^ distance) for i in range(size)])  6.76 us
    ppermute x2, waiting for transfers between devices, pass_on(): return lax.ppermute(value, ('expert', 'dp'), pairs)  5.72 us
    pallas_call x4, Pallas kernels, call(): pl.pallas_call(kernel, out_shape=out_shape, compiler_params=pltpu.Compile...  4.34 us
    unnamed x4, local copies, waits for them, and re-layouts  2.19 us
    ppermute x2, starting transfers between devices, pass_on(): return lax.ppermute(value, ('expert', 'dp'), pairs)  1.07 us
  transfers between devices with their start and end apart: 13, of which 9 were waited for; matrix products, arithmetic and copies ran while one was open for 1% of the time, Pallas kernels for 3%

profile of v6, /device:TPU:24, one launch (start us, length us, event | category | flops | bytes accessed | tf_op | source)
XLA Modules:
  0.0 39.2 jit_solution(4859082336768019220)
XLA Ops:
  0.7 0.5 %collective-permute-start.1 = (s32[8,128]{1,0:T(8,128)}, s32[8,128]{1,0:T(8,128)S(1)}, u32[]{:S(2)}, u32[]{:S(2)}) collective-permute-start(s32[8,128]{1,0:T(8,128)} %bitcast.1), channel_id=1, source_target_pairs={{0,1},{1,0},{2,3},{3,2},{4,5},{5,4},{6,7},{7,6},{8,9},{9,8},{10,11... | collective-permute-start | bytes 12296 | tf_op jit(solution)/shard_map/ppermute | solution.py:20
  1.2 1.5 %copy-done = bf16[128,7168]{1,0:T(8,128)(2,1)S(1)} copy-done((bf16[128,7168]{1,0:T(8,128)(2,1)S(1)}, bf16[128,7168]{1,0:T(8,128)(2,1)}, u32[]{:S(2)}) %copy-start) | copy-done | bytes 1835032
  2.7 0.7 %copy-done.1 = s32[128,8]{0,1:T(8,128)S(1)} copy-done((s32[128,8]{0,1:T(8,128)S(1)}, s32[128,8]{0,1:T(8,128)}, u32[]{:S(2)}) %copy-start.1) | copy-done | bytes 4120
  3.4 1.2 %shard_map.41 = (bf16[128,7168]{1,0:T(8,128)(2,1)S(1)}, f32[16,7296]{1,0:T(8,128)S(1)}) custom-call(s32[8,128]{1,0:T(8,128)S(1)} %bitcast.2, bf16[128,7168]{1,0:T(8,128)(2,1)S(1)} %copy-done), custom_call_target="tpu_custom_call" | custom-call | bytes 3670016 | tf_op jit(solution)/shard_map/pallas_call | solution.py:39
  4.6 0.1 collective-permute-done.1.other_ids_ref
  4.7 1.2 %shard_map.42 = (f32[448,128]{1,0:T(8,128)S(1)}, f32[464,128]{1,0:T(8,128)S(1)}, f32[448,128]{1,0:T(8,128)S(1)}, f32[448,128]{1,0:T(8,128)S(1)}, f32[448,128]{1,...) custom-call(s32[8,128]{1,0:T(8,128)S(1)} %collective-permute-done.1., ...), custom_call_target="tpu_custom_call" | custom-call | flops 587202560 | bytes 7340032 | tf_op jit(solution)/shard_map/pallas_call | solution.py:39
  5.9 1.5 %collective-permute-start.6 = (f32[464,128]{1,0:T(8,128)S(1)}, f32[464,128]{1,0:T(8,128)S(1)}, u32[]{:S(2)}, u32[]{:S(2)}) collective-permute-start(f32[464,128]{1,0:T(8,128)S(1)} %get-tuple-element.38), channel_id=1, source_target_pairs={{0,2},{1,3},{2,0},{3,1},{4,6},{5,7},{6,4},{7,5},{8,10},{9,11},{10,... | collective-permute-start | bytes 712712 | tf_op jit(solution)/shard_map/ppermute | solution.py:20
  7.4 0.7 %collective-permute-start.2 = (bf16[16,7296]{1,0:T(8,128)(2,1)S(1)}, bf16[16,7296]{1,0:T(8,128)(2,1)S(1)}, u32[]{:S(2)}, u32[]{:S(2)}) collective-permute-start(bf16[16,7296]{1,0:T(8,128)(2,1)S(1)} %get-tuple-element.30), channel_id=1, source_target_pairs={{1,5},{3,7},{5,1},{7,3},{9,13},{11,15},{13,9},{15,11},{17,21},{19,... | collective-permute-start | bytes 700424 | tf_op jit(solution)/shard_map/ppermute | solution.py:35
  8.1 0.4 %collective-permute-start.3 = (bf16[16,7296]{1,0:T(8,128)(2,1)S(1)}, bf16[16,7296]{1,0:T(8,128)(2,1)S(1)}, u32[]{:S(2)}, u32[]{:S(2)}) collective-permute-start(bf16[16,7296]{1,0:T(8,128)(2,1)S(1)} %get-tuple-element.31), channel_id=1, source_target_pairs={{0,8},{1,13},{2,10},{3,15},{4,12},{5,9},{6,14},{7,11},{8,0},{9,5},... | collective-permute-start | bytes 700424 | tf_op jit(solution)/shard_map/ppermute | solution.py:35
  8.5 0.5 %collective-permute-start.9 = (f32[448,128]{1,0:T(8,128)S(1)}, f32[448,128]{1,0:T(8,128)S(1)}, u32[]{:S(2)}, u32[]{:S(2)}) collective-permute-start(f32[448,128]{1,0:T(8,128)S(1)} %get-tuple-element.41), channel_id=1, source_target_pairs={{0,2},{1,3},{2,0},{3,1},{4,6},{5,7},{6,4},{7,5},{8,10},{9,11},{10,... | collective-permute-start | bytes 688136 | tf_op jit(solution)/shard_map/ppermute | solution.py:20
  9.0 5.4 %collective-permute-done.6 = f32[464,128]{1,0:T(8,128)S(1)} collective-permute-done((f32[464,128]{1,0:T(8,128)S(1)}, f32[464,128]{1,0:T(8,128)S(1)}, u32[]{:S(2)}, u32[]{:S(2)}) %collective-permute-start.6) | collective-permute-done | bytes 237600 | tf_op jit(solution)/shard_map/ppermute | solution.py:20
  14.4 0.3 collective-permute-start.7
  14.8 1.8 %collective-permute-start.11 = (f32[448,128]{1,0:T(8,128)S(1)}, f32[448,128]{1,0:T(8,128)S(1)}, u32[]{:S(2)}, u32[]{:S(2)}) collective-permute-start(f32[448,128]{1,0:T(8,128)S(1)} %get-tuple-element.44), channel_id=1, source_target_pairs={{0,2},{1,3},{2,0},{3,1},{4,6},{5,7},{6,4},{7,5},{8,10},{9,11},{10,... | collective-permute-start | bytes 688136 | tf_op jit(solution)/shard_map/ppermute | solution.py:20
  16.6 5.7 %collective-permute-done.3.refs_1_ = bf16[16,7296]{1,0:T(8,128)(2,1)S(1)} collective-permute-done((bf16[16,7296]{1,0:T(8,128)(2,1)S(1)}, bf16[16,7296]{1,0:T(8,128)(2,1)S(1)}, u32[]{:S(2)}, u32[]{:S(2)}) %collective-permute-start.3) | collective-permute-done | bytes 233504 | tf_op jit(solution)/shard_map/ppermute | solution.py:35
  22.4 0.6 %collective-permute-start.4 = (bf16[32,4096]{1,0:T(8,128)(2,1)S(1)}, bf16[32,4096]{1,0:T(8,128)(2,1)S(1)}, u32[]{:S(2)}, u32[]{:S(2)}) collective-permute-start(bf16[32,4096]{1,0:T(8,128)(2,1)S(1)} %get-tuple-element.33), channel_id=1, source_target_pairs={{0,2},{1,3},{2,0},{3,1},{4,6},{5,7},{6,4},{7,5},{8,10},{9,11},{10,... | collective-permute-start | bytes 786440 | tf_op jit(solution)/shard_map/ppermute | solution.py:20
  23.1 0.9 %collective-permute-done.11 = f32[448,128]{1,0:T(8,128)S(1)} collective-permute-done((f32[448,128]{1,0:T(8,128)S(1)}, f32[448,128]{1,0:T(8,128)S(1)}, u32[]{:S(2)}, u32[]{:S(2)}) %collective-permute-start.11) | collective-permute-done | bytes 229408 | tf_op jit(solution)/shard_map/ppermute | solution.py:20
  24.0 0.8 %collective-permute-done.7 = f32[448,128]{1,0:T(8,128)S(1)} collective-permute-done((f32[448,128]{1,0:T(8,128)S(1)}, f32[448,128]{1,0:T(8,128)S(1)}, u32[]{:S(2)}, u32[]{:S(2)}) %collective-permute-start.7) | collective-permute-done | bytes 229408 | tf_op jit(solution)/shard_map/ppermute | solution.py:20
  24.9 0.1 collective-permute-start.12
  25.0 1.1 %collective-permute-start.8 = (f32[448,128]{1,0:T(8,128)S(1)}, f32[448,128]{1,0:T(8,128)S(1)}, u32[]{:S(2)}, u32[]{:S(2)}) collective-permute-start(f32[448,128]{1,0:T(8,128)S(1)} %get-tuple-element.39), channel_id=1, source_target_pairs={{0,2},{1,3},{2,0},{3,1},{4,6},{5,7},{6,4},{7,5},{8,10},{9,11},{10,... | collective-permute-start | bytes 688136 | tf_op jit(solution)/shard_map/ppermute | solution.py:20
  26.1 5.5 %collective-permute-done.4.refs_1_ = bf16[32,4096]{1,0:T(8,128)(2,1)S(1)} collective-permute-done((bf16[32,4096]{1,0:T(8,128)(2,1)S(1)}, bf16[32,4096]{1,0:T(8,128)(2,1)S(1)}, u32[]{:S(2)}, u32[]{:S(2)}) %collective-permute-start.4) | collective-permute-done | bytes 262176 | tf_op jit(solution)/shard_map/ppermute | solution.py:20
  31.7 0.3 collective-permute-done.10
  32.0 2.1 %collective-permute-done.8 = f32[448,128]{1,0:T(8,128)S(1)} collective-permute-done((f32[448,128]{1,0:T(8,128)S(1)}, f32[448,128]{1,0:T(8,128)S(1)}, u32[]{:S(2)}, u32[]{:S(2)}) %collective-permute-start.8) | collective-permute-done | bytes 229408 | tf_op jit(solution)/shard_map/ppermute | solution.py:20
  34.2 3.1 %collective-permute-done.12 = f32[448,128]{1,0:T(8,128)S(1)} collective-permute-done((f32[448,128]{1,0:T(8,128)S(1)}, f32[448,128]{1,0:T(8,128)S(1)}, u32[]{:S(2)}, u32[]{:S(2)}) %collective-permute-start.12) | collective-permute-done | bytes 229408 | tf_op jit(solution)/shard_map/ppermute | solution.py:20
  37.3 2.0 %shard_map.44 = (f32[1,384,1792]{2,1,0:T(8,128)}, f32[448,128]{1,0:T(8,128)}) custom-call(bf16[32,2304]{1,0:T(8,128)(2,1)S(1)} %get-tuple-element.32.refs_0_, bf16[32,4096]{1,0:T(8,128)(2,1)S(1)} %collective-permute-done.4.refs_1_, bf16[64,2304]{1,0:T(8,128)(2,1)S(1)} %collective-permute-done.5.refs_2_, f32[448,128]{1,0:T(8,128)S(1)} %add_multiply_fusion.refs_3_), custom_call_target="tpu_custom_call" | custom-call | flops 176160768 | bytes 2752512 | tf_op jit(solution)/shard_map/pallas_call | solution.py:39
  (18 shorter events, 0.5 us)
Async XLA Ops:
  0.6 4.1 %collective-permute-start = (bf16[128,7168]{1,0:T(8,128)(2,1)}, bf16[128,7168]{1,0:T(8,128)(2,1)S(1)}, u32[]{:S(2)}, u32[]{:S(2)}) collective-permute-start(bf16[128,7168]{1,0:T(8,128)(2,1)} %tokens_ref.1), channel_id=1, source_target_pairs={{0,1},{1,0},{2,3},{3,2},{4,5},{5,4},{6,7},{7,6},{8,9},{9,8},{10,11... | collective-permute-start | bytes 5505032 | tf_op jit(solution)/shard_map/ppermute | solution.py:20
  0.7 4.0 %collective-permute-start.1 = (s32[8,128]{1,0:T(8,128)}, s32[8,128]{1,0:T(8,128)S(1)}, u32[]{:S(2)}, u32[]{:S(2)}) collective-permute-start(s32[8,128]{1,0:T(8,128)} %bitcast.1), channel_id=1, source_target_pairs={{0,1},{1,0},{2,3},{3,2},{4,5},{5,4},{6,7},{7,6},{8,9},{9,8},{10,11... | collective-permute-start | bytes 12296 | tf_op jit(solution)/shard_map/ppermute | solution.py:20
  1.2 1.5 %copy-start = (bf16[128,7168]{1,0:T(8,128)(2,1)S(1)}, bf16[128,7168]{1,0:T(8,128)(2,1)}, u32[]{:S(2)}) copy-start(bf16[128,7168]{1,0:T(8,128)(2,1)} %tokens_ref.1) | copy-start | bytes 5505028
  2.7 0.7 %copy-start.1 = (s32[128,8]{0,1:T(8,128)S(1)}, s32[128,8]{0,1:T(8,128)}, u32[]{:S(2)}) copy-start(s32[128,8]{0,1:T(8,128)} %param.3) | copy-start | bytes 12292
  5.9 8.5 %collective-permute-start.6 = (f32[464,128]{1,0:T(8,128)S(1)}, f32[464,128]{1,0:T(8,128)S(1)}, u32[]{:S(2)}, u32[]{:S(2)}) collective-permute-start(f32[464,128]{1,0:T(8,128)S(1)} %get-tuple-element.38), channel_id=1, source_target_pairs={{0,2},{1,3},{2,0},{3,1},{4,6},{5,7},{6,4},{7,5},{8,10},{9,11},{10,... | collective-permute-start | bytes 712712 | tf_op jit(solution)/shard_map/ppermute | solution.py:20
  7.4 9.2 %collective-permute-start.2 = (bf16[16,7296]{1,0:T(8,128)(2,1)S(1)}, bf16[16,7296]{1,0:T(8,128)(2,1)S(1)}, u32[]{:S(2)}, u32[]{:S(2)}) collective-permute-start(bf16[16,7296]{1,0:T(8,128)(2,1)S(1)} %get-tuple-element.30), channel_id=1, source_target_pairs={{1,5},{3,7},{5,1},{7,3},{9,13},{11,15},{13,9},{15,11},{17,21},{19,... | collective-permute-start | bytes 700424 | tf_op jit(solution)/shard_map/ppermute | solution.py:35
  8.1 14.3 %collective-permute-start.3 = (bf16[16,7296]{1,0:T(8,128)(2,1)S(1)}, bf16[16,7296]{1,0:T(8,128)(2,1)S(1)}, u32[]{:S(2)}, u32[]{:S(2)}) collective-permute-start(bf16[16,7296]{1,0:T(8,128)(2,1)S(1)} %get-tuple-element.31), channel_id=1, source_target_pairs={{0,8},{1,13},{2,10},{3,15},{4,12},{5,9},{6,14},{7,11},{8,0},{9,5},... | collective-permute-start | bytes 700424 | tf_op jit(solution)/shard_map/ppermute | solution.py:35
  8.5 14.5 %collective-permute-start.9 = (f32[448,128]{1,0:T(8,128)S(1)}, f32[448,128]{1,0:T(8,128)S(1)}, u32[]{:S(2)}, u32[]{:S(2)}) collective-permute-start(f32[448,128]{1,0:T(8,128)S(1)} %get-tuple-element.41), channel_id=1, source_target_pairs={{0,2},{1,3},{2,0},{3,1},{4,6},{5,7},{6,4},{7,5},{8,10},{9,11},{10,... | collective-permute-start | bytes 688136 | tf_op jit(solution)/shard_map/ppermute | solution.py:20
  14.4 10.4 %collective-permute-start.7 = (f32[448,128]{1,0:T(8,128)S(1)}, f32[448,128]{1,0:T(8,128)S(1)}, u32[]{:S(2)}, u32[]{:S(2)}) collective-permute-start(f32[448,128]{1,0:T(8,128)S(1)} %slice_add_fusion), channel_id=1, source_target_pairs={{0,4},{4,0},{8,12},{12,8},{1,5},{5,1},{9,13},{13,9},{2,6},{6,2},{1... | collective-permute-start | bytes 688136 | tf_op jit(solution)/shard_map/ppermute | solution.py:20
  14.8 9.2 %collective-permute-start.11 = (f32[448,128]{1,0:T(8,128)S(1)}, f32[448,128]{1,0:T(8,128)S(1)}, u32[]{:S(2)}, u32[]{:S(2)}) collective-permute-start(f32[448,128]{1,0:T(8,128)S(1)} %get-tuple-element.44), channel_id=1, source_target_pairs={{0,2},{1,3},{2,0},{3,1},{4,6},{5,7},{6,4},{7,5},{8,10},{9,11},{10,... | collective-permute-start | bytes 688136 | tf_op jit(solution)/shard_map/ppermute | solution.py:20
  22.4 9.2 %collective-permute-start.4 = (bf16[32,4096]{1,0:T(8,128)(2,1)S(1)}, bf16[32,4096]{1,0:T(8,128)(2,1)S(1)}, u32[]{:S(2)}, u32[]{:S(2)}) collective-permute-start(bf16[32,4096]{1,0:T(8,128)(2,1)S(1)} %get-tuple-element.33), channel_id=1, source_target_pairs={{0,2},{1,3},{2,0},{3,1},{4,6},{5,7},{6,4},{7,5},{8,10},{9,11},{10,... | collective-permute-start | bytes 786440 | tf_op jit(solution)/shard_map/ppermute | solution.py:20
  23.1 9.0 %collective-permute-start.10 = (f32[448,128]{1,0:T(8,128)S(1)}, f32[448,128]{1,0:T(8,128)S(1)}, u32[]{:S(2)}, u32[]{:S(2)}) collective-permute-start(f32[448,128]{1,0:T(8,128)S(1)} %add.28), channel_id=1, source_target_pairs={{0,4},{4,0},{8,12},{12,8},{1,5},{5,1},{9,13},{13,9},{2,6},{6,2},{1... | collective-permute-start | bytes 688136 | tf_op jit(solution)/shard_map/ppermute | solution.py:20
  24.9 12.4 %collective-permute-start.12 = (f32[448,128]{1,0:T(8,128)S(1)}, f32[448,128]{1,0:T(8,128)S(1)}, u32[]{:S(2)}, u32[]{:S(2)}) collective-permute-start(f32[448,128]{1,0:T(8,128)S(1)} %add_add_fusion), channel_id=1, source_target_pairs={{0,8},{4,12},{8,0},{12,4},{1,9},{5,13},{9,1},{13,5},{2,10},{6,14},... | collective-permute-start | bytes 688136 | tf_op jit(solution)/shard_map/ppermute | solution.py:20
  25.0 9.2 %collective-permute-start.8 = (f32[448,128]{1,0:T(8,128)S(1)}, f32[448,128]{1,0:T(8,128)S(1)}, u32[]{:S(2)}, u32[]{:S(2)}) collective-permute-start(f32[448,128]{1,0:T(8,128)S(1)} %get-tuple-element.39), channel_id=1, source_target_pairs={{0,2},{1,3},{2,0},{3,1},{4,6},{5,7},{6,4},{7,5},{8,10},{9,11},{10,... | collective-permute-start | bytes 688136 | tf_op jit(solution)/shard_map/ppermute | solution.py:20
  31.6 5.7 %collective-permute-start.5 = (bf16[64,2304]{1,0:T(8,128)(2,1)S(1)}, bf16[64,2304]{1,0:T(8,128)(2,1)S(1)}, u32[]{:S(2)}, u32[]{:S(2)}) collective-permute-start(bf16[64,2304]{1,0:T(8,128)(2,1)S(1)} %pad_maximum_fusion), channel_id=1, source_target_pairs={{0,1},{1,0},{2,3},{3,2},{4,5},{5,4},{6,7},{7,6},{8,9},{9,8},{10,11... | collective-permute-start | bytes 884744 | tf_op jit(solution)/shard_map/ppermute | solution.py:20

commit v7 on v6

--- a/solution.py
+++ b/solution.py
@@ -85,6 +85,7 @@
         start += ref.shape[1] - BAND - LANES
         return ref[:, start : start + size]
 
+    send(sum_ref, shared_ref)
     rows = jnp.concatenate([ref[:, :width] for ref in row_refs], axis=0)
     band = jnp.concatenate([tail(ref, 0, BAND) for ref in row_refs], axis=0)
     count = sum(
@@ -98,7 +99,6 @@
         )
         routed[part] = product * (2.0 / count)
         send(routed.at[part], routed_ref.at[0, part])
-    send(sum_ref, shared_ref)
     for copy in copies:
         copy.wait()
 

time: 39.4 us -> 39.3 us (level)
  no operation moved by 1% of the time
where the time goes in v7:
time: 39.3 us; the launch traced here: 39.2 us
  waiting for transfers between devices  23.9 us (61%)
  starting transfers between devices  7.83 us (20%)
  Pallas kernels  4.27 us (11%)
  local copies, waits for them, and re-layouts  2.2 us (6%)
  between operations  0.73 us (2%)
    ppermute x11, waiting for transfers between devices, exchange(): return lax.ppermute(value, axis, [(i, i ^ distance) for i in range(size)])  18.2 us
    ppermute x11, starting transfers between devices, exchange(): return lax.ppermute(value, axis, [(i, i ^ distance) for i in range(size)])  6.76 us
    ppermute x2, waiting for transfers between devices, pass_on(): return lax.ppermute(value, ('expert', 'dp'), pairs)  5.72 us
    pallas_call x4, Pallas kernels, call(): pl.pallas_call(kernel, out_shape=out_shape, compiler_params=pltpu.Compile...  4.27 us
    unnamed x4, local copies, waits for them, and re-layouts  2.19 us
    ppermute x2, starting transfers between devices, pass_on(): return lax.ppermute(value, ('expert', 'dp'), pairs)  1.07 us
  transfers between devices with their start and end apart: 13, of which 9 were waited for; matrix products, arithmetic and copies ran while one was open for 1% of the time, Pallas kernels for 3%

profile of v7, /device:TPU:24, one launch (start us, length us, event | category | flops | bytes accessed | tf_op | source)
XLA Modules:
  0.0 39.2 jit_solution(12274918116625249088)
XLA Ops:
  0.7 0.5 %collective-permute-start.1 = (s32[8,128]{1,0:T(8,128)}, s32[8,128]{1,0:T(8,128)S(1)}, u32[]{:S(2)}, u32[]{:S(2)}) collective-permute-start(s32[8,128]{1,0:T(8,128)} %bitcast.1), channel_id=1, source_target_pairs={{0,1},{1,0},{2,3},{3,2},{4,5},{5,4},{6,7},{7,6},{8,9},{9,8},{10,11... | collective-permute-start | bytes 12296 | tf_op jit(solution)/shard_map/ppermute | solution.py:20
  1.2 1.5 %copy-done = bf16[128,7168]{1,0:T(8,128)(2,1)S(1)} copy-done((bf16[128,7168]{1,0:T(8,128)(2,1)S(1)}, bf16[128,7168]{1,0:T(8,128)(2,1)}, u32[]{:S(2)}) %copy-start) | copy-done | bytes 1835032
  2.7 0.7 %copy-done.1 = s32[128,8]{0,1:T(8,128)S(1)} copy-done((s32[128,8]{0,1:T(8,128)S(1)}, s32[128,8]{0,1:T(8,128)}, u32[]{:S(2)}) %copy-start.1) | copy-done | bytes 4120
  3.4 1.2 %shard_map.41 = (bf16[128,7168]{1,0:T(8,128)(2,1)S(1)}, f32[16,7296]{1,0:T(8,128)S(1)}) custom-call(s32[8,128]{1,0:T(8,128)S(1)} %bitcast.2, bf16[128,7168]{1,0:T(8,128)(2,1)S(1)} %copy-done), custom_call_target="tpu_custom_call" | custom-call | bytes 3670016 | tf_op jit(solution)/shard_map/pallas_call | solution.py:39
  4.6 0.1 collective-permute-done.1.other_ids_ref
  4.7 1.2 %shard_map.42 = (f32[448,128]{1,0:T(8,128)S(1)}, f32[464,128]{1,0:T(8,128)S(1)}, f32[448,128]{1,0:T(8,128)S(1)}, f32[448,128]{1,0:T(8,128)S(1)}, f32[448,128]{1,...) custom-call(s32[8,128]{1,0:T(8,128)S(1)} %collective-permute-done.1., ...), custom_call_target="tpu_custom_call" | custom-call | flops 587202560 | bytes 7340032 | tf_op jit(solution)/shard_map/pallas_call | solution.py:39
  5.9 1.5 %collective-permute-start.6 = (f32[464,128]{1,0:T(8,128)S(1)}, f32[464,128]{1,0:T(8,128)S(1)}, u32[]{:S(2)}, u32[]{:S(2)}) collective-permute-start(f32[464,128]{1,0:T(8,128)S(1)} %get-tuple-element.38), channel_id=1, source_target_pairs={{0,2},{1,3},{2,0},{3,1},{4,6},{5,7},{6,4},{7,5},{8,10},{9,11},{10,... | collective-permute-start | bytes 712712 | tf_op jit(solution)/shard_map/ppermute | solution.py:20
  7.4 0.7 %collective-permute-start.2 = (bf16[16,7296]{1,0:T(8,128)(2,1)S(1)}, bf16[16,7296]{1,0:T(8,128)(2,1)S(1)}, u32[]{:S(2)}, u32[]{:S(2)}) collective-permute-start(bf16[16,7296]{1,0:T(8,128)(2,1)S(1)} %get-tuple-element.30), channel_id=1, source_target_pairs={{1,5},{3,7},{5,1},{7,3},{9,13},{11,15},{13,9},{15,11},{17,21},{19,... | collective-permute-start | bytes 700424 | tf_op jit(solution)/shard_map/ppermute | solution.py:35
  8.1 0.4 %collective-permute-start.3 = (bf16[16,7296]{1,0:T(8,128)(2,1)S(1)}, bf16[16,7296]{1,0:T(8,128)(2,1)S(1)}, u32[]{:S(2)}, u32[]{:S(2)}) collective-permute-start(bf16[16,7296]{1,0:T(8,128)(2,1)S(1)} %get-tuple-element.31), channel_id=1, source_target_pairs={{0,8},{1,13},{2,10},{3,15},{4,12},{5,9},{6,14},{7,11},{8,0},{9,5},... | collective-permute-start | bytes 700424 | tf_op jit(solution)/shard_map/ppermute | solution.py:35
  8.5 0.5 %collective-permute-start.9 = (f32[448,128]{1,0:T(8,128)S(1)}, f32[448,128]{1,0:T(8,128)S(1)}, u32[]{:S(2)}, u32[]{:S(2)}) collective-permute-start(f32[448,128]{1,0:T(8,128)S(1)} %get-tuple-element.41), channel_id=1, source_target_pairs={{0,2},{1,3},{2,0},{3,1},{4,6},{5,7},{6,4},{7,5},{8,10},{9,11},{10,... | collective-permute-start | bytes 688136 | tf_op jit(solution)/shard_map/ppermute | solution.py:20
  9.0 5.4 %collective-permute-done.6 = f32[464,128]{1,0:T(8,128)S(1)} collective-permute-done((f32[464,128]{1,0:T(8,128)S(1)}, f32[464,128]{1,0:T(8,128)S(1)}, u32[]{:S(2)}, u32[]{:S(2)}) %collective-permute-start.6) | collective-permute-done | bytes 237600 | tf_op jit(solution)/shard_map/ppermute | solution.py:20
  14.4 0.3 collective-permute-start.7
  14.8 1.8 %collective-permute-start.11 = (f32[448,128]{1,0:T(8,128)S(1)}, f32[448,128]{1,0:T(8,128)S(1)}, u32[]{:S(2)}, u32[]{:S(2)}) collective-permute-start(f32[448,128]{1,0:T(8,128)S(1)} %get-tuple-element.44), channel_id=1, source_target_pairs={{0,2},{1,3},{2,0},{3,1},{4,6},{5,7},{6,4},{7,5},{8,10},{9,11},{10,... | collective-permute-start | bytes 688136 | tf_op jit(solution)/shard_map/ppermute | solution.py:20
  16.6 5.7 %collective-permute-done.3.refs_1_ = bf16[16,7296]{1,0:T(8,128)(2,1)S(1)} collective-permute-done((bf16[16,7296]{1,0:T(8,128)(2,1)S(1)}, bf16[16,7296]{1,0:T(8,128)(2,1)S(1)}, u32[]{:S(2)}, u32[]{:S(2)}) %collective-permute-start.3) | collective-permute-done | bytes 233504 | tf_op jit(solution)/shard_map/ppermute | solution.py:35
  22.4 0.6 %collective-permute-start.4 = (bf16[32,4096]{1,0:T(8,128)(2,1)S(1)}, bf16[32,4096]{1,0:T(8,128)(2,1)S(1)}, u32[]{:S(2)}, u32[]{:S(2)}) collective-permute-start(bf16[32,4096]{1,0:T(8,128)(2,1)S(1)} %get-tuple-element.33), channel_id=1, source_target_pairs={{0,2},{1,3},{2,0},{3,1},{4,6},{5,7},{6,4},{7,5},{8,10},{9,11},{10,... | collective-permute-start | bytes 786440 | tf_op jit(solution)/shard_map/ppermute | solution.py:20
  23.1 0.1 collective-permute-start.10
  23.1 0.9 %collective-permute-done.11 = f32[448,128]{1,0:T(8,128)S(1)} collective-permute-done((f32[448,128]{1,0:T(8,128)S(1)}, f32[448,128]{1,0:T(8,128)S(1)}, u32[]{:S(2)}, u32[]{:S(2)}) %collective-permute-start.11) | collective-permute-done | bytes 229408 | tf_op jit(solution)/shard_map/ppermute | solution.py:20
  24.0 0.8 %collective-permute-done.7 = f32[448,128]{1,0:T(8,128)S(1)} collective-permute-done((f32[448,128]{1,0:T(8,128)S(1)}, f32[448,128]{1,0:T(8,128)S(1)}, u32[]{:S(2)}, u32[]{:S(2)}) %collective-permute-start.7) | collective-permute-done | bytes 229408 | tf_op jit(solution)/shard_map/ppermute | solution.py:20
  25.0 1.1 %collective-permute-start.8 = (f32[448,128]{1,0:T(8,128)S(1)}, f32[448,128]{1,0:T(8,128)S(1)}, u32[]{:S(2)}, u32[]{:S(2)}) collective-permute-start(f32[448,128]{1,0:T(8,128)S(1)} %get-tuple-element.39), channel_id=1, source_target_pairs={{0,2},{1,3},{2,0},{3,1},{4,6},{5,7},{6,4},{7,5},{8,10},{9,11},{10,... | collective-permute-start | bytes 688136 | tf_op jit(solution)/shard_map/ppermute | solution.py:20
  26.1 5.5 %collective-permute-done.4.refs_1_ = bf16[32,4096]{1,0:T(8,128)(2,1)S(1)} collective-permute-done((bf16[32,4096]{1,0:T(8,128)(2,1)S(1)}, bf16[32,4096]{1,0:T(8,128)(2,1)S(1)}, u32[]{:S(2)}, u32[]{:S(2)}) %collective-permute-start.4) | collective-permute-done | bytes 262176 | tf_op jit(solution)/shard_map/ppermute | solution.py:20
  31.7 0.3 collective-permute-done.10
  32.0 2.1 %collective-permute-done.8 = f32[448,128]{1,0:T(8,128)S(1)} collective-permute-done((f32[448,128]{1,0:T(8,128)S(1)}, f32[448,128]{1,0:T(8,128)S(1)}, u32[]{:S(2)}, u32[]{:S(2)}) %collective-permute-start.8) | collective-permute-done | bytes 229408 | tf_op jit(solution)/shard_map/ppermute | solution.py:20
  34.2 3.1 %collective-permute-done.12 = f32[448,128]{1,0:T(8,128)S(1)} collective-permute-done((f32[448,128]{1,0:T(8,128)S(1)}, f32[448,128]{1,0:T(8,128)S(1)}, u32[]{:S(2)}, u32[]{:S(2)}) %collective-permute-start.12) | collective-permute-done | bytes 229408 | tf_op jit(solution)/shard_map/ppermute | solution.py:20
  37.3 1.9 %shard_map.44 = (f32[1,384,1792]{2,1,0:T(8,128)}, f32[448,128]{1,0:T(8,128)}) custom-call(bf16[32,2304]{1,0:T(8,128)(2,1)S(1)} %get-tuple-element.32.refs_0_, bf16[32,4096]{1,0:T(8,128)(2,1)S(1)} %collective-permute-done.4.refs_1_, bf16[64,2304]{1,0:T(8,128)(2,1)S(1)} %collective-permute-done.5.refs_2_, f32[448,128]{1,0:T(8,128)S(1)} %add_multiply_fusion.refs_3_), custom_call_target="tpu_custom_call" | custom-call | flops 176160768 | bytes 2752512 | tf_op jit(solution)/shard_map/pallas_call | solution.py:39
  (18 shorter events, 0.5 us)
Async XLA Ops:
  0.6 4.1 %collective-permute-start = (bf16[128,7168]{1,0:T(8,128)(2,1)}, bf16[128,7168]{1,0:T(8,128)(2,1)S(1)}, u32[]{:S(2)}, u32[]{:S(2)}) collective-permute-start(bf16[128,7168]{1,0:T(8,128)(2,1)} %tokens_ref.1), channel_id=1, source_target_pairs={{0,1},{1,0},{2,3},{3,2},{4,5},{5,4},{6,7},{7,6},{8,9},{9,8},{10,11... | collective-permute-start | bytes 5505032 | tf_op jit(solution)/shard_map/ppermute | solution.py:20
  0.7 4.0 %collective-permute-start.1 = (s32[8,128]{1,0:T(8,128)}, s32[8,128]{1,0:T(8,128)S(1)}, u32[]{:S(2)}, u32[]{:S(2)}) collective-permute-start(s32[8,128]{1,0:T(8,128)} %bitcast.1), channel_id=1, source_target_pairs={{0,1},{1,0},{2,3},{3,2},{4,5},{5,4},{6,7},{7,6},{8,9},{9,8},{10,11... | collective-permute-start | bytes 12296 | tf_op jit(solution)/shard_map/ppermute | solution.py:20
  1.2 1.5 %copy-start = (bf16[128,7168]{1,0:T(8,128)(2,1)S(1)}, bf16[128,7168]{1,0:T(8,128)(2,1)}, u32[]{:S(2)}) copy-start(bf16[128,7168]{1,0:T(8,128)(2,1)} %tokens_ref.1) | copy-start | bytes 5505028
  2.7 0.7 %copy-start.1 = (s32[128,8]{0,1:T(8,128)S(1)}, s32[128,8]{0,1:T(8,128)}, u32[]{:S(2)}) copy-start(s32[128,8]{0,1:T(8,128)} %param.3) | copy-start | bytes 12292
  5.9 8.5 %collective-permute-start.6 = (f32[464,128]{1,0:T(8,128)S(1)}, f32[464,128]{1,0:T(8,128)S(1)}, u32[]{:S(2)}, u32[]{:S(2)}) collective-permute-start(f32[464,128]{1,0:T(8,128)S(1)} %get-tuple-element.38), channel_id=1, source_target_pairs={{0,2},{1,3},{2,0},{3,1},{4,6},{5,7},{6,4},{7,5},{8,10},{9,11},{10,... | collective-permute-start | bytes 712712 | tf_op jit(solution)/shard_map/ppermute | solution.py:20
  7.4 9.2 %collective-permute-start.2 = (bf16[16,7296]{1,0:T(8,128)(2,1)S(1)}, bf16[16,7296]{1,0:T(8,128)(2,1)S(1)}, u32[]{:S(2)}, u32[]{:S(2)}) collective-permute-start(bf16[16,7296]{1,0:T(8,128)(2,1)S(1)} %get-tuple-element.30), channel_id=1, source_target_pairs={{1,5},{3,7},{5,1},{7,3},{9,13},{11,15},{13,9},{15,11},{17,21},{19,... | collective-permute-start | bytes 700424 | tf_op jit(solution)/shard_map/ppermute | solution.py:35
  8.1 14.3 %collective-permute-start.3 = (bf16[16,7296]{1,0:T(8,128)(2,1)S(1)}, bf16[16,7296]{1,0:T(8,128)(2,1)S(1)}, u32[]{:S(2)}, u32[]{:S(2)}) collective-permute-start(bf16[16,7296]{1,0:T(8,128)(2,1)S(1)} %get-tuple-element.31), channel_id=1, source_target_pairs={{0,8},{1,13},{2,10},{3,15},{4,12},{5,9},{6,14},{7,11},{8,0},{9,5},... | collective-permute-start | bytes 700424 | tf_op jit(solution)/shard_map/ppermute | solution.py:35
  8.5 14.5 %collective-permute-start.9 = (f32[448,128]{1,0:T(8,128)S(1)}, f32[448,128]{1,0:T(8,128)S(1)}, u32[]{:S(2)}, u32[]{:S(2)}) collective-permute-start(f32[448,128]{1,0:T(8,128)S(1)} %get-tuple-element.41), channel_id=1, source_target_pairs={{0,2},{1,3},{2,0},{3,1},{4,6},{5,7},{6,4},{7,5},{8,10},{9,11},{10,... | collective-permute-start | bytes 688136 | tf_op jit(solution)/shard_map/ppermute | solution.py:20
  14.4 10.4 %collective-permute-start.7 = (f32[448,128]{1,0:T(8,128)S(1)}, f32[448,128]{1,0:T(8,128)S(1)}, u32[]{:S(2)}, u32[]{:S(2)}) collective-permute-start(f32[448,128]{1,0:T(8,128)S(1)} %slice_add_fusion), channel_id=1, source_target_pairs={{0,4},{4,0},{8,12},{12,8},{1,5},{5,1},{9,13},{13,9},{2,6},{6,2},{1... | collective-permute-start | bytes 688136 | tf_op jit(solution)/shard_map/ppermute | solution.py:20
  14.8 9.2 %collective-permute-start.11 = (f32[448,128]{1,0:T(8,128)S(1)}, f32[448,128]{1,0:T(8,128)S(1)}, u32[]{:S(2)}, u32[]{:S(2)}) collective-permute-start(f32[448,128]{1,0:T(8,128)S(1)} %get-tuple-element.44), channel_id=1, source_target_pairs={{0,2},{1,3},{2,0},{3,1},{4,6},{5,7},{6,4},{7,5},{8,10},{9,11},{10,... | collective-permute-start | bytes 688136 | tf_op jit(solution)/shard_map/ppermute | solution.py:20
  22.4 9.2 %collective-permute-start.4 = (bf16[32,4096]{1,0:T(8,128)(2,1)S(1)}, bf16[32,4096]{1,0:T(8,128)(2,1)S(1)}, u32[]{:S(2)}, u32[]{:S(2)}) collective-permute-start(bf16[32,4096]{1,0:T(8,128)(2,1)S(1)} %get-tuple-element.33), channel_id=1, source_target_pairs={{0,2},{1,3},{2,0},{3,1},{4,6},{5,7},{6,4},{7,5},{8,10},{9,11},{10,... | collective-permute-start | bytes 786440 | tf_op jit(solution)/shard_map/ppermute | solution.py:20
  23.1 9.0 %collective-permute-start.10 = (f32[448,128]{1,0:T(8,128)S(1)}, f32[448,128]{1,0:T(8,128)S(1)}, u32[]{:S(2)}, u32[]{:S(2)}) collective-permute-start(f32[448,128]{1,0:T(8,128)S(1)} %add.28), channel_id=1, source_target_pairs={{0,4},{4,0},{8,12},{12,8},{1,5},{5,1},{9,13},{13,9},{2,6},{6,2},{1... | collective-permute-start | bytes 688136 | tf_op jit(solution)/shard_map/ppermute | solution.py:20
  24.9 12.4 %collective-permute-start.12 = (f32[448,128]{1,0:T(8,128)S(1)}, f32[448,128]{1,0:T(8,128)S(1)}, u32[]{:S(2)}, u32[]{:S(2)}) collective-permute-start(f32[448,128]{1,0:T(8,128)S(1)} %add_add_fusion), channel_id=1, source_target_pairs={{0,8},{4,12},{8,0},{12,4},{1,9},{5,13},{9,1},{13,5},{2,10},{6,14},... | collective-permute-start | bytes 688136 | tf_op jit(solution)/shard_map/ppermute | solution.py:20
  25.0 9.2 %collective-permute-start.8 = (f32[448,128]{1,0:T(8,128)S(1)}, f32[448,128]{1,0:T(8,128)S(1)}, u32[]{:S(2)}, u32[]{:S(2)}) collective-permute-start(f32[448,128]{1,0:T(8,128)S(1)} %get-tuple-element.39), channel_id=1, source_target_pairs={{0,2},{1,3},{2,0},{3,1},{4,6},{5,7},{6,4},{7,5},{8,10},{9,11},{10,... | collective-permute-start | bytes 688136 | tf_op jit(solution)/shard_map/ppermute | solution.py:20
  31.6 5.7 %collective-permute-start.5 = (bf16[64,2304]{1,0:T(8,128)(2,1)S(1)}, bf16[64,2304]{1,0:T(8,128)(2,1)S(1)}, u32[]{:S(2)}, u32[]{:S(2)}) collective-permute-start(bf16[64,2304]{1,0:T(8,128)(2,1)S(1)} %pad_maximum_fusion), channel_id=1, source_target_pairs={{0,1},{1,0},{2,3},{3,2},{4,5},{5,4},{6,7},{7,6},{8,9},{9,8},{10,11... | collective-permute-start | bytes 884744 | tf_op jit(solution)/shard_map/ppermute | solution.py:20

commit v8 on v7

--- a/solution.py
+++ b/solution.py
@@ -148,6 +148,8 @@
     features = mine_ref.shape[1]
     e = lax.axis_index("expert")
     d = lax.axis_index("dp")
+
+    picks, flags = picks_of(other_ids_ref, experts)
 
     def both(columns):
         return jnp.concatenate([mine_ref[:, columns], other_ref[:, columns]], axis=0)
@@ -178,7 +180,6 @@
         for part in parts_of(features):
             out_refs[0][part] = product(part)
 
-    picks, flags = picks_of(other_ids_ref, experts)
 
     def put(columns, found):
         for i, ref in enumerate(row_refs):

time: 39.3 us -> 39.3 us (level)
  no operation moved by 1% of the time
where the time goes in v8:
time: 39.3 us; the launch traced here: 39.1 us
  waiting for transfers between devices  23.9 us (61%)
  starting transfers between devices  7.86 us (20%)
  Pallas kernels  4.16 us (11%)
  local copies, waits for them, and re-layouts  2.2 us (6%)
  between operations  0.74 us (2%)
    ppermute x11, waiting for transfers between devices, exchange(): return lax.ppermute(value, axis, [(i, i ^ distance) for i in range(size)])  18.2 us
    ppermute x11, starting transfers between devices, exchange(): return lax.ppermute(value, axis, [(i, i ^ distance) for i in range(size)])  6.78 us
    ppermute x2, waiting for transfers between devices, pass_on(): return lax.ppermute(value, ('expert', 'dp'), pairs)  5.71 us
    pallas_call x4, Pallas kernels, call(): pl.pallas_call(kernel, out_shape=out_shape, compiler_params=pltpu.Compile...  4.16 us
    unnamed x4, local copies, waits for them, and re-layouts  2.19 us
    ppermute x2, starting transfers between devices, pass_on(): return lax.ppermute(value, ('expert', 'dp'), pairs)  1.08 us
  transfers between devices with their start and end apart: 13, of which 9 were waited for; matrix products, arithmetic and copies ran while one was open for 1% of the time, Pallas kernels for 3%

profile of v8, /device:TPU:24, one launch (start us, length us, event | category | flops | bytes accessed | tf_op | source)
XLA Modules:
  0.0 39.1 jit_solution(6925954336185043009)
XLA Ops:
  0.7 0.5 %collective-permute-start.1 = (s32[8,128]{1,0:T(8,128)}, s32[8,128]{1,0:T(8,128)S(1)}, u32[]{:S(2)}, u32[]{:S(2)}) collective-permute-start(s32[8,128]{1,0:T(8,128)} %bitcast.1), channel_id=1, source_target_pairs={{0,1},{1,0},{2,3},{3,2},{4,5},{5,4},{6,7},{7,6},{8,9},{9,8},{10,11... | collective-permute-start | bytes 12296 | tf_op jit(solution)/shard_map/ppermute | solution.py:20
  1.2 1.5 %copy-done = bf16[128,7168]{1,0:T(8,128)(2,1)S(1)} copy-done((bf16[128,7168]{1,0:T(8,128)(2,1)S(1)}, bf16[128,7168]{1,0:T(8,128)(2,1)}, u32[]{:S(2)}) %copy-start) | copy-done | bytes 1835032
  2.7 0.7 %copy-done.1 = s32[128,8]{0,1:T(8,128)S(1)} copy-done((s32[128,8]{0,1:T(8,128)S(1)}, s32[128,8]{0,1:T(8,128)}, u32[]{:S(2)}) %copy-start.1) | copy-done | bytes 4120
  3.4 1.2 %shard_map.41 = (bf16[128,7168]{1,0:T(8,128)(2,1)S(1)}, f32[16,7296]{1,0:T(8,128)S(1)}) custom-call(s32[8,128]{1,0:T(8,128)S(1)} %bitcast.2, bf16[128,7168]{1,0:T(8,128)(2,1)S(1)} %copy-done), custom_call_target="tpu_custom_call" | custom-call | bytes 3670016 | tf_op jit(solution)/shard_map/pallas_call | solution.py:39
  4.6 0.1 collective-permute-done.1.other_ids_ref
  4.7 1.1 %shard_map.42 = (f32[448,128]{1,0:T(8,128)S(1)}, f32[464,128]{1,0:T(8,128)S(1)}, f32[448,128]{1,0:T(8,128)S(1)}, f32[448,128]{1,0:T(8,128)S(1)}, f32[448,128]{1,...) custom-call(s32[8,128]{1,0:T(8,128)S(1)} %collective-permute-done.1., ...), custom_call_target="tpu_custom_call" | custom-call | flops 587202560 | bytes 7340032 | tf_op jit(solution)/shard_map/pallas_call | solution.py:39
  5.8 1.6 %collective-permute-start.6 = (f32[464,128]{1,0:T(8,128)S(1)}, f32[464,128]{1,0:T(8,128)S(1)}, u32[]{:S(2)}, u32[]{:S(2)}) collective-permute-start(f32[464,128]{1,0:T(8,128)S(1)} %get-tuple-element.38), channel_id=1, source_target_pairs={{0,2},{1,3},{2,0},{3,1},{4,6},{5,7},{6,4},{7,5},{8,10},{9,11},{10,... | collective-permute-start | bytes 712712 | tf_op jit(solution)/shard_map/ppermute | solution.py:20
  7.3 0.7 %collective-permute-start.2 = (bf16[16,7296]{1,0:T(8,128)(2,1)S(1)}, bf16[16,7296]{1,0:T(8,128)(2,1)S(1)}, u32[]{:S(2)}, u32[]{:S(2)}) collective-permute-start(bf16[16,7296]{1,0:T(8,128)(2,1)S(1)} %get-tuple-element.30), channel_id=1, source_target_pairs={{1,5},{3,7},{5,1},{7,3},{9,13},{11,15},{13,9},{15,11},{17,21},{19,... | collective-permute-start | bytes 700424 | tf_op jit(solution)/shard_map/ppermute | solution.py:35
  8.0 0.4 %collective-permute-start.3 = (bf16[16,7296]{1,0:T(8,128)(2,1)S(1)}, bf16[16,7296]{1,0:T(8,128)(2,1)S(1)}, u32[]{:S(2)}, u32[]{:S(2)}) collective-permute-start(bf16[16,7296]{1,0:T(8,128)(2,1)S(1)} %get-tuple-element.31), channel_id=1, source_target_pairs={{0,8},{1,13},{2,10},{3,15},{4,12},{5,9},{6,14},{7,11},{8,0},{9,5},... | collective-permute-start | bytes 700424 | tf_op jit(solution)/shard_map/ppermute | solution.py:35
  8.4 0.5 %collective-permute-start.9 = (f32[448,128]{1,0:T(8,128)S(1)}, f32[448,128]{1,0:T(8,128)S(1)}, u32[]{:S(2)}, u32[]{:S(2)}) collective-permute-start(f32[448,128]{1,0:T(8,128)S(1)} %get-tuple-element.41), channel_id=1, source_target_pairs={{0,2},{1,3},{2,0},{3,1},{4,6},{5,7},{6,4},{7,5},{8,10},{9,11},{10,... | collective-permute-start | bytes 688136 | tf_op jit(solution)/shard_map/ppermute | solution.py:20
  8.9 5.4 %collective-permute-done.6 = f32[464,128]{1,0:T(8,128)S(1)} collective-permute-done((f32[464,128]{1,0:T(8,128)S(1)}, f32[464,128]{1,0:T(8,128)S(1)}, u32[]{:S(2)}, u32[]{:S(2)}) %collective-permute-start.6) | collective-permute-done | bytes 237600 | tf_op jit(solution)/shard_map/ppermute | solution.py:20
  14.3 0.3 collective-permute-start.7
  14.7 1.8 %collective-permute-start.11 = (f32[448,128]{1,0:T(8,128)S(1)}, f32[448,128]{1,0:T(8,128)S(1)}, u32[]{:S(2)}, u32[]{:S(2)}) collective-permute-start(f32[448,128]{1,0:T(8,128)S(1)} %get-tuple-element.44), channel_id=1, source_target_pairs={{0,2},{1,3},{2,0},{3,1},{4,6},{5,7},{6,4},{7,5},{8,10},{9,11},{10,... | collective-permute-start | bytes 688136 | tf_op jit(solution)/shard_map/ppermute | solution.py:20
  16.6 5.7 %collective-permute-done.3.refs_1_ = bf16[16,7296]{1,0:T(8,128)(2,1)S(1)} collective-permute-done((bf16[16,7296]{1,0:T(8,128)(2,1)S(1)}, bf16[16,7296]{1,0:T(8,128)(2,1)S(1)}, u32[]{:S(2)}, u32[]{:S(2)}) %collective-permute-start.3) | collective-permute-done | bytes 233504 | tf_op jit(solution)/shard_map/ppermute | solution.py:35
  22.3 0.6 %collective-permute-start.4 = (bf16[32,4096]{1,0:T(8,128)(2,1)S(1)}, bf16[32,4096]{1,0:T(8,128)(2,1)S(1)}, u32[]{:S(2)}, u32[]{:S(2)}) collective-permute-start(bf16[32,4096]{1,0:T(8,128)(2,1)S(1)} %get-tuple-element.33), channel_id=1, source_target_pairs={{0,2},{1,3},{2,0},{3,1},{4,6},{5,7},{6,4},{7,5},{8,10},{9,11},{10,... | collective-permute-start | bytes 786440 | tf_op jit(solution)/shard_map/ppermute | solution.py:20
  23.0 0.1 collective-permute-start.10
  23.0 0.9 %collective-permute-done.11 = f32[448,128]{1,0:T(8,128)S(1)} collective-permute-done((f32[448,128]{1,0:T(8,128)S(1)}, f32[448,128]{1,0:T(8,128)S(1)}, u32[]{:S(2)}, u32[]{:S(2)}) %collective-permute-start.11) | collective-permute-done | bytes 229408 | tf_op jit(solution)/shard_map/ppermute | solution.py:20
  23.9 0.8 %collective-permute-done.7 = f32[448,128]{1,0:T(8,128)S(1)} collective-permute-done((f32[448,128]{1,0:T(8,128)S(1)}, f32[448,128]{1,0:T(8,128)S(1)}, u32[]{:S(2)}, u32[]{:S(2)}) %collective-permute-start.7) | collective-permute-done | bytes 229408 | tf_op jit(solution)/shard_map/ppermute | solution.py:20
  24.8 1.1 %collective-permute-start.8 = (f32[448,128]{1,0:T(8,128)S(1)}, f32[448,128]{1,0:T(8,128)S(1)}, u32[]{:S(2)}, u32[]{:S(2)}) collective-permute-start(f32[448,128]{1,0:T(8,128)S(1)} %get-tuple-element.39), channel_id=1, source_target_pairs={{0,2},{1,3},{2,0},{3,1},{4,6},{5,7},{6,4},{7,5},{8,10},{9,11},{10,... | collective-permute-start | bytes 688136 | tf_op jit(solution)/shard_map/ppermute | solution.py:20
  26.0 5.5 %collective-permute-done.4.refs_1_ = bf16[32,4096]{1,0:T(8,128)(2,1)S(1)} collective-permute-done((bf16[32,4096]{1,0:T(8,128)(2,1)S(1)}, bf16[32,4096]{1,0:T(8,128)(2,1)S(1)}, u32[]{:S(2)}, u32[]{:S(2)}) %collective-permute-start.4) | collective-permute-done | bytes 262176 | tf_op jit(solution)/shard_map/ppermute | solution.py:20
  31.6 0.3 collective-permute-done.10
  31.9 2.1 %collective-permute-done.8 = f32[448,128]{1,0:T(8,128)S(1)} collective-permute-done((f32[448,128]{1,0:T(8,128)S(1)}, f32[448,128]{1,0:T(8,128)S(1)}, u32[]{:S(2)}, u32[]{:S(2)}) %collective-permute-start.8) | collective-permute-done | bytes 229408 | tf_op jit(solution)/shard_map/ppermute | solution.py:20
  34.1 3.1 %collective-permute-done.12 = f32[448,128]{1,0:T(8,128)S(1)} collective-permute-done((f32[448,128]{1,0:T(8,128)S(1)}, f32[448,128]{1,0:T(8,128)S(1)}, u32[]{:S(2)}, u32[]{:S(2)}) %collective-permute-start.12) | collective-permute-done | bytes 229408 | tf_op jit(solution)/shard_map/ppermute | solution.py:20
  37.2 1.9 %shard_map.44 = (f32[1,384,1792]{2,1,0:T(8,128)}, f32[448,128]{1,0:T(8,128)}) custom-call(bf16[32,2304]{1,0:T(8,128)(2,1)S(1)} %get-tuple-element.32.refs_0_, bf16[32,4096]{1,0:T(8,128)(2,1)S(1)} %collective-permute-done.4.refs_1_, bf16[64,2304]{1,0:T(8,128)(2,1)S(1)} %collective-permute-done.5.refs_2_, f32[448,128]{1,0:T(8,128)S(1)} %add_multiply_fusion.refs_3_), custom_call_target="tpu_custom_call" | custom-call | flops 176160768 | bytes 2752512 | tf_op jit(solution)/shard_map/pallas_call | solution.py:39
  (18 shorter events, 0.5 us)
Async XLA Ops:
  0.6 4.1 %collective-permute-start = (bf16[128,7168]{1,0:T(8,128)(2,1)}, bf16[128,7168]{1,0:T(8,128)(2,1)S(1)}, u32[]{:S(2)}, u32[]{:S(2)}) collective-permute-start(bf16[128,7168]{1,0:T(8,128)(2,1)} %tokens_ref.1), channel_id=1, source_target_pairs={{0,1},{1,0},{2,3},{3,2},{4,5},{5,4},{6,7},{7,6},{8,9},{9,8},{10,11... | collective-permute-start | bytes 5505032 | tf_op jit(solution)/shard_map/ppermute | solution.py:20
  0.7 4.0 %collective-permute-start.1 = (s32[8,128]{1,0:T(8,128)}, s32[8,128]{1,0:T(8,128)S(1)}, u32[]{:S(2)}, u32[]{:S(2)}) collective-permute-start(s32[8,128]{1,0:T(8,128)} %bitcast.1), channel_id=1, source_target_pairs={{0,1},{1,0},{2,3},{3,2},{4,5},{5,4},{6,7},{7,6},{8,9},{9,8},{10,11... | collective-permute-start | bytes 12296 | tf_op jit(solution)/shard_map/ppermute | solution.py:20
  1.2 1.5 %copy-start = (bf16[128,7168]{1,0:T(8,128)(2,1)S(1)}, bf16[128,7168]{1,0:T(8,128)(2,1)}, u32[]{:S(2)}) copy-start(bf16[128,7168]{1,0:T(8,128)(2,1)} %tokens_ref.1) | copy-start | bytes 5505028
  2.7 0.7 %copy-start.1 = (s32[128,8]{0,1:T(8,128)S(1)}, s32[128,8]{0,1:T(8,128)}, u32[]{:S(2)}) copy-start(s32[128,8]{0,1:T(8,128)} %param.3) | copy-start | bytes 12292
  5.8 8.5 %collective-permute-start.6 = (f32[464,128]{1,0:T(8,128)S(1)}, f32[464,128]{1,0:T(8,128)S(1)}, u32[]{:S(2)}, u32[]{:S(2)}) collective-permute-start(f32[464,128]{1,0:T(8,128)S(1)} %get-tuple-element.38), channel_id=1, source_target_pairs={{0,2},{1,3},{2,0},{3,1},{4,6},{5,7},{6,4},{7,5},{8,10},{9,11},{10,... | collective-permute-start | bytes 712712 | tf_op jit(solution)/shard_map/ppermute | solution.py:20
  7.3 9.2 %collective-permute-start.2 = (bf16[16,7296]{1,0:T(8,128)(2,1)S(1)}, bf16[16,7296]{1,0:T(8,128)(2,1)S(1)}, u32[]{:S(2)}, u32[]{:S(2)}) collective-permute-start(bf16[16,7296]{1,0:T(8,128)(2,1)S(1)} %get-tuple-element.30), channel_id=1, source_target_pairs={{1,5},{3,7},{5,1},{7,3},{9,13},{11,15},{13,9},{15,11},{17,21},{19,... | collective-permute-start | bytes 700424 | tf_op jit(solution)/shard_map/ppermute | solution.py:35
  8.0 14.3 %collective-permute-start.3 = (bf16[16,7296]{1,0:T(8,128)(2,1)S(1)}, bf16[16,7296]{1,0:T(8,128)(2,1)S(1)}, u32[]{:S(2)}, u32[]{:S(2)}) collective-permute-start(bf16[16,7296]{1,0:T(8,128)(2,1)S(1)} %get-tuple-element.31), channel_id=1, source_target_pairs={{0,8},{1,13},{2,10},{3,15},{4,12},{5,9},{6,14},{7,11},{8,0},{9,5},... | collective-permute-start | bytes 700424 | tf_op jit(solution)/shard_map/ppermute | solution.py:35
  8.4 14.5 %collective-permute-start.9 = (f32[448,128]{1,0:T(8,128)S(1)}, f32[448,128]{1,0:T(8,128)S(1)}, u32[]{:S(2)}, u32[]{:S(2)}) collective-permute-start(f32[448,128]{1,0:T(8,128)S(1)} %get-tuple-element.41), channel_id=1, source_target_pairs={{0,2},{1,3},{2,0},{3,1},{4,6},{5,7},{6,4},{7,5},{8,10},{9,11},{10,... | collective-permute-start | bytes 688136 | tf_op jit(solution)/shard_map/ppermute | solution.py:20
  14.3 10.4 %collective-permute-start.7 = (f32[448,128]{1,0:T(8,128)S(1)}, f32[448,128]{1,0:T(8,128)S(1)}, u32[]{:S(2)}, u32[]{:S(2)}) collective-permute-start(f32[448,128]{1,0:T(8,128)S(1)} %slice_add_fusion), channel_id=1, source_target_pairs={{0,4},{4,0},{8,12},{12,8},{1,5},{5,1},{9,13},{13,9},{2,6},{6,2},{1... | collective-permute-start | bytes 688136 | tf_op jit(solution)/shard_map/ppermute | solution.py:20
  14.7 9.3 %collective-permute-start.11 = (f32[448,128]{1,0:T(8,128)S(1)}, f32[448,128]{1,0:T(8,128)S(1)}, u32[]{:S(2)}, u32[]{:S(2)}) collective-permute-start(f32[448,128]{1,0:T(8,128)S(1)} %get-tuple-element.44), channel_id=1, source_target_pairs={{0,2},{1,3},{2,0},{3,1},{4,6},{5,7},{6,4},{7,5},{8,10},{9,11},{10,... | collective-permute-start | bytes 688136 | tf_op jit(solution)/shard_map/ppermute | solution.py:20
  22.3 9.2 %collective-permute-start.4 = (bf16[32,4096]{1,0:T(8,128)(2,1)S(1)}, bf16[32,4096]{1,0:T(8,128)(2,1)S(1)}, u32[]{:S(2)}, u32[]{:S(2)}) collective-permute-start(bf16[32,4096]{1,0:T(8,128)(2,1)S(1)} %get-tuple-element.33), channel_id=1, source_target_pairs={{0,2},{1,3},{2,0},{3,1},{4,6},{5,7},{6,4},{7,5},{8,10},{9,11},{10,... | collective-permute-start | bytes 786440 | tf_op jit(solution)/shard_map/ppermute | solution.py:20
  23.0 9.0 %collective-permute-start.10 = (f32[448,128]{1,0:T(8,128)S(1)}, f32[448,128]{1,0:T(8,128)S(1)}, u32[]{:S(2)}, u32[]{:S(2)}) collective-permute-start(f32[448,128]{1,0:T(8,128)S(1)} %add.28), channel_id=1, source_target_pairs={{0,4},{4,0},{8,12},{12,8},{1,5},{5,1},{9,13},{13,9},{2,6},{6,2},{1... | collective-permute-start | bytes 688136 | tf_op jit(solution)/shard_map/ppermute | solution.py:20
  24.8 12.4 %collective-permute-start.12 = (f32[448,128]{1,0:T(8,128)S(1)}, f32[448,128]{1,0:T(8,128)S(1)}, u32[]{:S(2)}, u32[]{:S(2)}) collective-permute-start(f32[448,128]{1,0:T(8,128)S(1)} %add_add_fusion), channel_id=1, source_target_pairs={{0,8},{4,12},{8,0},{12,4},{1,9},{5,13},{9,1},{13,5},{2,10},{6,14},... | collective-permute-start | bytes 688136 | tf_op jit(solution)/shard_map/ppermute | solution.py:20
  24.8 9.2 %collective-permute-start.8 = (f32[448,128]{1,0:T(8,128)S(1)}, f32[448,128]{1,0:T(8,128)S(1)}, u32[]{:S(2)}, u32[]{:S(2)}) collective-permute-start(f32[448,128]{1,0:T(8,128)S(1)} %get-tuple-element.39), channel_id=1, source_target_pairs={{0,2},{1,3},{2,0},{3,1},{4,6},{5,7},{6,4},{7,5},{8,10},{9,11},{10,... | collective-permute-start | bytes 688136 | tf_op jit(solution)/shard_map/ppermute | solution.py:20
  31.5 5.6 %collective-permute-start.5 = (bf16[64,2304]{1,0:T(8,128)(2,1)S(1)}, bf16[64,2304]{1,0:T(8,128)(2,1)S(1)}, u32[]{:S(2)}, u32[]{:S(2)}) collective-permute-start(bf16[64,2304]{1,0:T(8,128)(2,1)S(1)} %pad_maximum_fusion), channel_id=1, source_target_pairs={{0,1},{1,0},{2,3},{3,2},{4,5},{5,4},{6,7},{7,6},{8,9},{9,8},{10,11... | collective-permute-start | bytes 884744 | tf_op jit(solution)/shard_map/ppermute | solution.py:20
